TPU v7x, 32 devices: a whole 2x2x4 slice. The times are simulated.
32 devices in a mesh: dp: 8 (over z, y), head: 4 (over x, core).
Axes of the slice: x: 2, y: 2, z: 4, core: 2. Of those that a mesh axis runs over, the one named last changes fastest.
Arguments:
- tokens: bfloat16 [2, 4096, 2048], P(None, ('dp', 'head')), may hold values from -6 to 6
- out_grad: bfloat16 [2, 4096, 2048], P(None, ('dp', 'head')), may hold values from -6 to 6
- seq_lengths: int32 [2, 4], replicated, may hold values from 1 to 3584, as said below
- attn_norm: float32 [2048], replicated, may hold values from 0.5 to 1.5
- query_proj: bfloat16 [2048, 2048], P('dp', 'head'), may hold values from -0.125 to 0.125
- key_proj: bfloat16 [2048, 2048], P('dp', 'head'), may hold values from -0.125 to 0.125
- value_proj: bfloat16 [2048, 4096], P('dp', 'head'), may hold values from -0.125 to 0.125
- gate_proj: bfloat16 [2048, 4096], P('dp', 'head'), may hold values from -0.125 to 0.125
- decay_proj: bfloat16 [2048, 16], P('dp', 'head'), may hold values from -0.125 to 0.125
- beta_proj: bfloat16 [2048, 16], P('dp', 'head'), may hold values from -0.125 to 0.125
- conv_query: float32 [4, 2048], replicated, may hold values from -3 to 3
- conv_key: float32 [4, 2048], replicated, may hold values from -3 to 3
- conv_value: float32 [4, 4096], replicated, may hold values from -3 to 3
- log_rate: float32 [16], replicated, may hold values from -0.7 to 0.7
- step_bias: float32 [16], replicated, may hold values from -15 to -2
- head_norm: float32 [256], replicated, may hold values from 0.5 to 1.5
- out_proj: bfloat16 [4096, 2048], P('head', 'dp'), may hold values from -0.1875 to 0.1875
- ffn_norm: float32 [2048], replicated, may hold values from 0.5 to 1.5
- ffn_gate: bfloat16 [2048, 5632], P('dp', 'head'), may hold values from -0.125 to 0.125
- ffn_up: bfloat16 [2048, 5632], P('dp', 'head'), may hold values from -0.125 to 0.125
- ffn_down: bfloat16 [5632, 2048], P('head', 'dp'), may hold values from -0.15625 to 0.15625
Outputs:
- block_out: bfloat16 [2, 4096, 2048], P(None, ('dp', 'head'))
- tokens_grad: float32 [2, 4096, 2048], P(None, ('dp', 'head'))
- attn_norm_grad: float32 [2048], replicated
- query_proj_grad: float32 [2048, 2048], P('dp', 'head')
- key_proj_grad: float32 [2048, 2048], P('dp', 'head')
- value_proj_grad: float32 [2048, 4096], P('dp', 'head')
- gate_proj_grad: float32 [2048, 4096], P('dp', 'head')
- decay_proj_grad: float32 [2048, 16], P('dp', 'head')
- beta_proj_grad: float32 [2048, 16], P('dp', 'head')
- conv_query_grad: float32 [4, 2048], replicated
- conv_key_grad: float32 [4, 2048], replicated
- conv_value_grad: float32 [4, 4096], replicated
- log_rate_grad: float32 [16], replicated
- step_bias_grad: float32 [16], replicated
- head_norm_grad: float32 [256], replicated
- out_proj_grad: float32 [4096, 2048], P('head', 'dp')
- ffn_norm_grad: float32 [2048], replicated
- ffn_gate_grad: float32 [2048, 5632], P('dp', 'head')
- ffn_up_grad: float32 [2048, 5632], P('dp', 'head')
- ffn_down_grad: float32 [5632, 2048], P('head', 'dp')
Inputs may be any that keep to these rules, and one draw needn't show every extreme that they name: `seq_lengths`: each micro-batch packs 4 sequences end to end with lengths summing to 4096; the second sequence has exactly (7) * 512 tokens and starts within the first 512 tokens, the others are shorter than 512.
All inputs are finite; a program needn't handle non-finite values.
Results may differ from a plain program's by a relative error of at most 0.018.
Values may be sent and summed in bfloat16 or wider, within the bound.
No kernel may reach another device: no remote copies, remote signals or barrier semaphores. Data moves between devices by JAX's collectives and lax.ppermute only.
A program may use at most 384 MiB of HBM per device.

v0:
```python
from functools import partial

import jax
import jax.numpy as jnp
from jax import lax
from jax.sharding import PartitionSpec as P

GROUP = 64
KCONV = 4


EPSILON = 1e-06
HEAD_FLOOR = 0.01
FULL_PRECISION = lax.Precision.HIGHEST


def from_behind(value, axis, steps):
    count = lax.axis_size(axis)
    leading, last = (max(0, -steps), min(count, count - steps))
    return lax.ppermute(value, axis, [(source, source + steps) for source in range(leading, last)])


def prefix_2(value, axis, join, neutral, backward):
    count, mine = (lax.axis_size(axis), lax.axis_index(axis))
    pieces = jax.tree.map(lambda part: lax.all_gather(part, axis), value)
    if backward:
        pieces = jax.tree.map(lambda part: part[::-1], pieces)
        mine = count - 1 - mine
    so_far = jax.tree.map(
        lambda part, zero: jnp.full_like(part, 0) + jnp.asarray(zero, part.dtype), value, neutral
    )

    def hop(position, so_far):
        longer = join(so_far, jax.tree.map(lambda part: part[position], pieces))
        return jax.tree.map(lambda new, old: jnp.where(position < mine, new, old), longer, so_far)

    return lax.fori_loop(0, count - 1, hop, so_far)


def seq_offsets(lengths, first_row, row_count):
    seq_ends = jnp.cumsum(lengths)
    starts = seq_ends - lengths
    places = first_row + lax.iota(jnp.int32, row_count)
    begun_at = jnp.where(starts[None, :] <= places[:, None], starts[None, :], 0)
    return places - jnp.max(begun_at, axis=1)


def group_step(carried_state, block):
    query_rows, keys_now, values, beta_rows, decays, opening = block
    span_len = query_rows.shape[1]
    key_length = keys_now.shape[2]
    segment = jnp.cumsum(opening)
    untouched = (segment < 0.5).astype(jnp.float32)
    cumulative = jnp.cumsum(decays, axis=-1)
    row_ids = lax.broadcasted_iota(jnp.int32, (span_len, span_len), 0)
    col_ids = lax.broadcasted_iota(jnp.int32, (span_len, span_len), 1)
    same_seg = segment[:, None] == segment[None, :]
    inclusive = jnp.logical_and(row_ids >= col_ids, same_seg)
    strictly = jnp.logical_and(row_ids > col_ids, same_seg)
    spread = cumulative[:, :, None] - cumulative[:, None, :]
    pair_decay = jnp.where(inclusive, jnp.exp(jnp.where(inclusive, spread, 0.0)), 0.0)
    key_gram = jnp.einsum("hik,hjk->hij", keys_now, keys_now, precision=FULL_PRECISION)
    coupling = jnp.where(strictly, beta_rows[:, :, None] * pair_decay * key_gram, 0.0)
    system = coupling + jnp.eye(span_len, dtype=jnp.float32)
    incoming_carry = jnp.exp(cumulative) * untouched
    targets = jnp.concatenate(
        [(beta_rows * incoming_carry)[:, :, None] * keys_now, beta_rows[:, :, None] * values],
        axis=2,
    )
    solved_system = lax.linalg.triangular_solve(
        system, targets, left_side=True, lower=True, unit_diagonal=True
    )
    written_values = solved_system[:, :, key_length:] - jnp.einsum(
        "dyj,djs->dys", solved_system[:, :, :key_length], carried_state, precision=FULL_PRECISION
    )
    attend = jnp.einsum("hik,hjk->hij", query_rows, keys_now, precision=FULL_PRECISION) * pair_decay
    output_rows = incoming_carry[:, :, None] * jnp.einsum(
        "dyj,djs->dys", query_rows, carried_state, precision=FULL_PRECISION
    )
    output_rows = output_rows + jnp.einsum(
        "hij,hjv->hiv", attend, written_values, precision=FULL_PRECISION
    )
    key_rows_weighted = pair_decay[:, -1, :, None] * keys_now
    updated_state = incoming_carry[:, -1, None, None] * carried_state + jnp.einsum(
        "sdm,sdw->smw", key_rows_weighted, written_values, precision=FULL_PRECISION
    )
    return (updated_state, output_rows)


def run_chain(query_rows, keys_now, values, beta_rows, decays, opening, initial):
    block_count = query_rows.shape[0] // GROUP

    def blocked(source):
        shaped = source.reshape((block_count, GROUP) + source.shape[1:])
        return jnp.moveaxis(shaped, 1, 2)

    blocks = (
        blocked(query_rows),
        blocked(keys_now),
        blocked(values),
        blocked(beta_rows),
        blocked(decays),
        opening.reshape(block_count, GROUP),
    )
    final_state, output_rows = lax.scan(jax.checkpoint(group_step), initial, blocks)
    output_rows = jnp.moveaxis(output_rows, 2, 1)
    output_rows = output_rows.reshape(
        (block_count * GROUP, output_rows.shape[2], output_rows.shape[3])
    )
    return (output_rows, final_state)


def mixer_piece(
    extended, conv_local, decay_lin, rate_local, step_local, lag_masks, opening, key_length
):
    row_count = opening.shape[0]
    head_count = rate_local.shape[0]
    qk_width = head_count * key_length
    value_size = (extended.shape[1] - 2 * qk_width) // head_count
    conv_sum = conv_local[KCONV - 1] * extended[KCONV - 1 :]
    for lag_size in range(1, KCONV):
        lower_edge = KCONV - 1 - lag_size
        conv_sum = (
            conv_sum
            + conv_local[lower_edge]
            * extended[lower_edge : lower_edge + row_count]
            * lag_masks[lag_size - 1][:, None]
        )
    active = jax.nn.silu(conv_sum)
    query_rows = active[:, :qk_width].reshape(row_count, head_count, key_length)
    keys_now = active[:, qk_width : 2 * qk_width].reshape(row_count, head_count, key_length)
    values = active[:, 2 * qk_width :].reshape(row_count, head_count, value_size)
    query_rows = (
        query_rows
        * lax.rsqrt(jnp.sum(query_rows * query_rows, axis=-1, keepdims=True) + EPSILON)
        * key_length ** (-0.5)
    )
    keys_now = keys_now * lax.rsqrt(jnp.sum(keys_now * keys_now, axis=-1, keepdims=True) + EPSILON)
    beta_rows = jax.nn.sigmoid(decay_lin[:, head_count:])
    decays = -jnp.exp(rate_local) * jax.nn.softplus(decay_lin[:, :head_count] + step_local)
    padded_values = jnp.concatenate(
        [values, jnp.zeros((row_count, head_count, key_length), jnp.float32)], axis=2
    )
    identity_block = jnp.broadcast_to(
        jnp.eye(key_length, dtype=jnp.float32), (head_count, key_length, key_length)
    )
    initial = jnp.concatenate(
        [jnp.zeros((head_count, key_length, value_size), jnp.float32), identity_block], axis=2
    )
    output_rows, final_state = run_chain(
        query_rows, keys_now, padded_values, beta_rows, decays, opening, initial
    )
    return (
        output_rows[:, :, :value_size],
        output_rows[:, :, value_size:],
        final_state[:, :, :value_size],
        final_state[:, :, value_size:],
    )


def compose_forward(earlier, latter):
    return (
        jnp.einsum("hij,hjk->hik", latter[0], earlier[0], precision=FULL_PRECISION),
        jnp.einsum("hij,hjv->hiv", latter[0], earlier[1], precision=FULL_PRECISION) + latter[1],
    )


def compose_backward(earlier, latter):
    return (
        jnp.einsum("hij,hjk->hik", earlier[0], latter[0], precision=FULL_PRECISION),
        latter[1] + jnp.einsum("hji,hjv->hiv", latter[0], earlier[1], precision=FULL_PRECISION),
    )


def contract_rows(left, right):
    return lax.dot_general(
        left, right, (((0,), (0,)), ((), ())), preferred_element_type=jnp.float32
    )


def contract_cols(left, right):
    return lax.dot_general(
        left, right, (((1,), (1,)), ((), ())), preferred_element_type=jnp.float32
    )


def norm_backward(grad_in, normed_rows, scale):
    return scale * (grad_in - normed_rows * jnp.mean(grad_in * normed_rows, axis=-1, keepdims=True))


def fetch_weights(w_in, w_decay, out_proj, w_ffn, ffn_down):
    return (
        lax.all_gather(w_in, "dp", axis=0, tiled=True),
        lax.all_gather(w_decay, "dp", axis=0, tiled=True),
        lax.all_gather(out_proj, "dp", axis=1, tiled=True),
        lax.all_gather(w_ffn, "dp", axis=0, tiled=True),
        lax.all_gather(ffn_down, "dp", axis=1, tiled=True),
    )


def settle_grads(grad_in, grad_decay, grad_out, grad_ffn, grad_down):
    return (
        lax.psum_scatter(
            grad_in.astype(jnp.bfloat16), "dp", scatter_dimension=0, tiled=True
        ).astype(jnp.float32),
        lax.psum_scatter(
            grad_decay.astype(jnp.bfloat16), "dp", scatter_dimension=0, tiled=True
        ).astype(jnp.float32),
        lax.psum_scatter(
            grad_out.astype(jnp.bfloat16), "dp", scatter_dimension=1, tiled=True
        ).astype(jnp.float32),
        lax.psum_scatter(
            grad_ffn.astype(jnp.bfloat16), "dp", scatter_dimension=0, tiled=True
        ).astype(jnp.float32),
        lax.psum_scatter(
            grad_down.astype(jnp.bfloat16), "dp", scatter_dimension=1, tiled=True
        ).astype(jnp.float32),
    )


def place_slice(portion, full_width, head_rank):
    blank_full = jnp.zeros(portion.shape[:-1] + (full_width,), jnp.float32)
    return lax.dynamic_update_slice_in_dim(
        blank_full, portion, head_rank * portion.shape[-1], portion.ndim - 1
    )


def micro_batch(
    gathered,
    tokens_now,
    cotangent,
    lengths,
    attn_norm,
    ffn_norm,
    head_norm,
    conv_local,
    rate_local,
    step_local,
    key_length,
):
    w_in, w_decay, out_proj, w_ffn, ffn_down = gathered
    head_count = rate_local.shape[0]
    v_width = out_proj.shape[0]
    value_size = v_width // head_count
    qk_width = key_length * head_count
    ffn_width = ffn_down.shape[0]
    conv_width = 2 * qk_width + v_width
    residual = tokens_now.astype(jnp.float32)
    scale_one = lax.rsqrt(jnp.mean(residual * residual, axis=-1, keepdims=True) + EPSILON)
    normed_one = residual * scale_one
    normed = (normed_one * attn_norm).astype(jnp.bfloat16)
    normed_all, cotangent_all = (
        lax.all_gather(normed, "head", axis=0, tiled=True),
        lax.all_gather(cotangent, "head", axis=0, tiled=True),
    )
    row_count = normed_all.shape[0]
    offsets = seq_offsets(lengths, lax.axis_index("dp") * row_count, row_count)
    opening = (offsets == 0).astype(jnp.float32)
    lag_masks = [(offsets >= lag_size).astype(jnp.float32) for lag_size in range(1, KCONV)]
    projected = jnp.dot(normed_all, w_in, preferred_element_type=jnp.float32)
    pre_conv = projected[:, :conv_width].astype(jnp.bfloat16)
    gate_lin = projected[:, conv_width:].reshape(row_count, head_count, value_size)
    decay_lin = jnp.dot(normed_all, w_decay, preferred_element_type=jnp.float32)
    rim_rows = from_behind(pre_conv[row_count - (KCONV - 1) :], "dp", 1)
    extended = jnp.concatenate([rim_rows, pre_conv], axis=0).astype(jnp.float32)
    mixer_fn = partial(mixer_piece, lag_masks=lag_masks, opening=opening, key_length=key_length)
    (plain_output, carried_mapping, block_sum, block_map), pull_back = jax.vjp(
        mixer_fn, extended, conv_local, decay_lin, rate_local, step_local
    )
    eye_stack = jnp.broadcast_to(jnp.eye(key_length, dtype=jnp.float32), block_map.shape)
    prefix = prefix_2(
        (block_map, block_sum), "dp", compose_forward, (eye_stack, jnp.zeros_like(block_sum)), False
    )
    incoming_state = prefix[1]
    mixer_output = plain_output + jnp.einsum(
        "qcd,cdl->qcl", carried_mapping, incoming_state, precision=FULL_PRECISION
    )
    out_scale = lax.rsqrt(
        jnp.mean(mixer_output * mixer_output, axis=-1, keepdims=True) + HEAD_FLOOR
    )
    normed_mix = mixer_output * out_scale
    gate_sigmoid = jax.nn.sigmoid(gate_lin)
    gate_active = gate_lin * gate_sigmoid
    gated_out = (
        (normed_mix * head_norm * gate_active).reshape(row_count, v_width).astype(jnp.bfloat16)
    )
    mix_sum = lax.psum_scatter(
        jnp.dot(gated_out, out_proj, preferred_element_type=jnp.float32),
        "head",
        scatter_dimension=0,
        tiled=True,
    )
    after_mix = residual + mix_sum
    scale_two = lax.rsqrt(jnp.mean(after_mix * after_mix, axis=-1, keepdims=True) + EPSILON)
    normed_two = after_mix * scale_two
    ffn_in = (normed_two * ffn_norm).astype(jnp.bfloat16)
    ffn_all = lax.all_gather(ffn_in, "head", axis=0, tiled=True)
    gate_up = jnp.dot(ffn_all, w_ffn, preferred_element_type=jnp.float32)
    gate_ffn = gate_up[:, :ffn_width]
    up_ffn = gate_up[:, ffn_width:]
    ffn_sigmoid = jax.nn.sigmoid(gate_ffn)
    ffn_active = gate_ffn * ffn_sigmoid
    hidden = (ffn_active * up_ffn).astype(jnp.bfloat16)
    ffn_sum = lax.psum_scatter(
        jnp.dot(hidden, ffn_down, preferred_element_type=jnp.float32).astype(jnp.bfloat16),
        "head",
        scatter_dimension=0,
        tiled=True,
    ).astype(jnp.float32)
    block_out = (after_mix + ffn_sum).astype(jnp.bfloat16)
    hidden_grad = contract_cols(cotangent_all, ffn_down)
    grad_down = contract_rows(hidden, cotangent_all)
    gate_ffn_grad = hidden_grad * up_ffn * ffn_sigmoid * (1.0 + gate_ffn * (1.0 - ffn_sigmoid))
    up_ffn_grad = hidden_grad * ffn_active
    gate_up_grad = jnp.concatenate([gate_ffn_grad, up_ffn_grad], axis=1).astype(jnp.bfloat16)
    grad_ffn = contract_rows(ffn_all, gate_up_grad)
    ffn_in_grad = lax.psum_scatter(
        contract_cols(gate_up_grad, w_ffn), "head", scatter_dimension=0, tiled=True
    )
    grad_norm_two = jnp.sum(ffn_in_grad * normed_two, axis=0)
    after_mix_grad = cotangent.astype(jnp.float32) + norm_backward(
        ffn_in_grad * ffn_norm, normed_two, scale_two
    )
    branch_grad = lax.all_gather(after_mix_grad.astype(jnp.bfloat16), "head", axis=0, tiled=True)
    gated_grad = contract_cols(branch_grad, out_proj).reshape(row_count, head_count, value_size)
    grad_out = contract_rows(gated_out, branch_grad)
    grad_head_norm = jnp.sum(gated_grad * normed_mix * gate_active, axis=(0, 1))
    gate_lin_grad = (
        gated_grad * normed_mix * head_norm * gate_sigmoid * (1.0 + gate_lin * (1.0 - gate_sigmoid))
    ).reshape(row_count, v_width)
    mixer_output_gradient = norm_backward(
        gated_grad * head_norm * gate_active, normed_mix, out_scale
    )
    local_gradient = jnp.einsum(
        "tqg,tqn->qgn", carried_mapping, mixer_output_gradient, precision=FULL_PRECISION
    )
    suffix = prefix_2(
        (block_map, local_gradient),
        "dp",
        compose_backward,
        (eye_stack, jnp.zeros_like(local_gradient)),
        True,
    )
    outgoing_state_gradient = suffix[1]
    carried_gradient = jnp.einsum(
        "dwp,wxp->dwx", mixer_output_gradient, incoming_state, precision=FULL_PRECISION
    )
    mapping_gradient = jnp.einsum(
        "two,tao->twa", outgoing_state_gradient, incoming_state, precision=FULL_PRECISION
    )
    ext_grad, grad_conv, decay_grad, grad_rate, grad_step = pull_back(
        (mixer_output_gradient, carried_gradient, outgoing_state_gradient, mapping_gradient)
    )
    back_rim = from_behind(ext_grad[: KCONV - 1], "dp", -1)
    tail_add = jnp.concatenate(
        [jnp.zeros((row_count - (KCONV - 1), conv_width), jnp.float32), back_rim], axis=0
    )
    pre_conv_grad = ext_grad[KCONV - 1 :] + tail_add
    proj_grad = jnp.concatenate([pre_conv_grad, gate_lin_grad], axis=1).astype(jnp.bfloat16)
    decay_lin_grad = decay_grad.astype(jnp.bfloat16)
    grad_in = contract_rows(normed_all, proj_grad)
    grad_decay = contract_rows(normed_all, decay_lin_grad)
    normed_part = contract_cols(proj_grad, w_in) + contract_cols(decay_lin_grad, w_decay)
    normed_grad = lax.psum_scatter(
        normed_part.astype(jnp.bfloat16), "head", scatter_dimension=0, tiled=True
    ).astype(jnp.float32)
    grad_norm_one = jnp.sum(normed_grad * normed_one, axis=0)
    input_grad = after_mix_grad + norm_backward(normed_grad * attn_norm, normed_one, scale_one)
    return (
        block_out,
        input_grad,
        (grad_in, grad_decay, grad_out, grad_ffn, grad_down),
        (grad_conv, grad_rate, grad_step, grad_head_norm, grad_norm_one, grad_norm_two),
    )


def body(
    tokens,
    out_grad,
    seq_lengths,
    attn_norm,
    query_proj,
    key_proj,
    value_proj,
    gate_proj,
    decay_proj,
    beta_proj,
    conv_query,
    conv_key,
    conv_value,
    log_rate,
    step_bias,
    head_norm,
    out_proj,
    ffn_norm,
    ffn_gate,
    ffn_up,
    ffn_down,
):
    head_rank = lax.axis_index("head")
    head_count = decay_proj.shape[1]
    qk_width = query_proj.shape[1]
    v_width = value_proj.shape[1]
    key_length = qk_width // head_count
    ffn_width = ffn_gate.shape[1]
    conv_local = jnp.concatenate(
        [
            lax.dynamic_slice_in_dim(conv_query, head_rank * qk_width, qk_width, 1),
            lax.dynamic_slice_in_dim(conv_key, head_rank * qk_width, qk_width, 1),
            lax.dynamic_slice_in_dim(conv_value, head_rank * v_width, v_width, 1),
        ],
        axis=1,
    )
    rate_local = lax.dynamic_slice_in_dim(log_rate, head_rank * head_count, head_count, 0)
    step_local = lax.dynamic_slice_in_dim(step_bias, head_rank * head_count, head_count, 0)
    w_in = jnp.concatenate([query_proj, key_proj, value_proj, gate_proj], axis=1)
    w_decay = jnp.concatenate([decay_proj, beta_proj], axis=1)
    w_ffn = jnp.concatenate([ffn_gate, ffn_up], axis=1)
    shard_totals = None
    small_totals = None
    results = []
    input_grads = []
    for micro_index in range(tokens.shape[0]):
        gathered = fetch_weights(w_in, w_decay, out_proj, w_ffn, ffn_down)
        block_out, input_grad, weight_terms, small_terms = micro_batch(
            gathered,
            tokens[micro_index],
            out_grad[micro_index],
            seq_lengths[micro_index],
            attn_norm,
            ffn_norm,
            head_norm,
            conv_local,
            rate_local,
            step_local,
            key_length,
        )
        results.append(block_out)
        input_grads.append(input_grad)
        small_totals = (
            small_terms
            if small_totals is None
            else jax.tree.map(jnp.add, small_totals, small_terms)
        )
        shards = settle_grads(
            weight_terms[0], weight_terms[1], weight_terms[2], weight_terms[3], weight_terms[4]
        )
        shard_totals = (
            shards if shard_totals is None else jax.tree.map(jnp.add, shard_totals, shards)
        )
    grad_conv, grad_rate, grad_step, grad_head_norm, grad_norm_one, grad_norm_two = small_totals
    conv_query_part = place_slice(grad_conv[:, :qk_width], conv_query.shape[1], head_rank)
    conv_key_part = place_slice(grad_conv[:, qk_width : 2 * qk_width], conv_key.shape[1], head_rank)
    conv_value_part = place_slice(grad_conv[:, 2 * qk_width :], conv_value.shape[1], head_rank)
    rate_part = place_slice(grad_rate, log_rate.shape[0], head_rank)
    step_part = place_slice(grad_step, step_bias.shape[0], head_rank)
    summed = lax.psum(
        (
            conv_query_part,
            conv_key_part,
            conv_value_part,
            rate_part,
            step_part,
            grad_head_norm,
            grad_norm_one,
            grad_norm_two,
        ),
        ("dp", "head"),
    )
    shard_in, shard_decay, shard_out, shard_ffn, shard_down = shard_totals
    return (
        jnp.stack(results),
        jnp.stack(input_grads),
        summed[6],
        shard_in[:, :qk_width],
        shard_in[:, qk_width : 2 * qk_width],
        shard_in[:, 2 * qk_width : 2 * qk_width + v_width],
        shard_in[:, 2 * qk_width + v_width :],
        shard_decay[:, :head_count],
        shard_decay[:, head_count:],
        summed[0],
        summed[1],
        summed[2],
        summed[3],
        summed[4],
        summed[5],
        shard_out,
        summed[7],
        shard_ffn[:, :ffn_width],
        shard_ffn[:, ffn_width:],
        shard_down,
    )


def solution(mesh):
    in_specs = (
        P(None, ("dp", "head"), None),
        P(None, ("dp", "head"), None),
        P(),
        P(),
        P("dp", "head"),
        P("dp", "head"),
        P("dp", "head"),
        P("dp", "head"),
        P("dp", "head"),
        P("dp", "head"),
        P(),
        P(),
        P(),
        P(),
        P(),
        P(),
        P("head", "dp"),
        P(),
        P("dp", "head"),
        P("dp", "head"),
        P("head", "dp"),
    )
    out_specs = (
        P(None, ("dp", "head"), None),
        P(None, ("dp", "head"), None),
        P(),
        P("dp", "head"),
        P("dp", "head"),
        P("dp", "head"),
        P("dp", "head"),
        P("dp", "head"),
        P("dp", "head"),
        P(),
        P(),
        P(),
        P(),
        P(),
        P(),
        P("head", "dp"),
        P(),
        P("dp", "head"),
        P("dp", "head"),
        P("head", "dp"),
    )
    return jax.shard_map(body, mesh=mesh, in_specs=in_specs, out_specs=out_specs, check_vma=False)
```

profile of v0, /device:TPU:0, one launch (start us, length us, event | category | flops | bytes accessed | tf_op | source)
XLA Modules:
  0.0 4116.2 jit_solution(17909560066428302313)
XLA Ops:
  15.2 32.2 all_gather.85
  51.6 165.0 %all-gather.29.cloned.1.call-done = bf16[2048,3072]{1,0:T(8,128)(2,1)} async-done(((bf16[256,3072]{1,0:T(8,128)(2,1)}), bf16[2048,3072]{1,0:T(8,128)(2,1)}) %all-gather.29.cloned.1.call-update) | async-done | bytes 12582928 | tf_op jit(solution)/shard_map/all_gather | solution.py:193
  297.8 254.1 %while.140 = (s32[]{:T(128)}, f32[4,128,384]{2,1,0:T(8,128)S(1)}, f32[8,4,64,384]{3,2,1,0:T(8,128)}, f32[8,4,128,384]{3,2,1,0:T(8,128)}, f32[8,4,64]{2,1,0:T(4,1...) while((s32[]{:T(128)}, f32[4,128,384]{2,1,0:T(8,128)S(1)}, ...), condition=%wide.region_8.11_spmd.clone, body=%wide.region_5.10_spmd.clone.sunk | while | flops 680784256 | bytes 10862809 | solution.py:105
  582.4 253.2 %while.141 = (s32[]{:T(128)}, f32[4,128,384]{2,1,0:T(8,128)S(1)}, f32[8,4,64,384]{3,2,1,0:T(8,128)}, f32[8,4,128,384]{3,2,1,0:T(8,128)}, f32[8,4,64]{2,1,0:T(4,1...) while((s32[]{:T(128)}, f32[4,128,384]{2,1,0:T(8,128)S(1)}, ...), condition=%wide.region_23.26_spmd.clone, body=%wide.region_20.25_spmd.clone.sunk | while | flops 680784256 | bytes 10862809 | solution.py:105
  886.7 74.6 %all-gather.53.cloned.1.call-done = f32[32,128,256]{2,1,0:T(8,128)} async-done(((f32[4,128,256]{2,1,0:T(8,128)}), f32[32,128,256]{2,1,0:T(8,128)}) %all-gather.53.cloned.1.call-update) | async-done | bytes 4194320 | tf_op jit(solution)/shard_map/all_gather | solution.py:25
  984.5 52.1 %all-gather.31.cloned.1.call-done = bf16[1024,2048]{1,0:T(8,128)(2,1)} async-done(((bf16[1024,256]{1,0:T(8,128)(2,1)}), bf16[1024,2048]{1,0:T(8,128)(2,1)}) %all-gather.31.cloned.1.call-update) | async-done | bytes 4194320 | tf_op jit(solution)/shard_map/all_gather | solution.py:195
  1055.8 30.3 reduce-scatter.19.cloned.1.call-done
  1086.1 47.1 %reduce-scatter.23.cloned.1.call-done = f32[128,2048]{1,0:T(8,128)} async-done(((f32[512,2048]{1,0:T(8,128)}), f32[128,2048]{1,0:T(8,128)}) %reduce-scatter.23.cloned.1.call-update) | async-done | bytes 1048592 | tf_op jit(solution)/shard_map/reduce_scatter | solution.py:287
  1140.4 159.2 %all-gather.35.cloned.1.call-done = bf16[2048,2816]{1,0:T(8,128)(2,1)} async-done(((bf16[256,2816]{1,0:T(8,128)(2,1)}), bf16[2048,2816]{1,0:T(8,128)(2,1)}) %all-gather.35.cloned.1.call-update) | async-done | bytes 11534352 | tf_op jit(solution)/shard_map/all_gather | solution.py:196
  1299.6 22.8 all-gather.33.cloned.1.call-done
  1347.2 95.5 %all-gather.37.cloned.1.call-done = bf16[1408,2048]{1,0:T(8,128)(2,1)} async-done(((bf16[1408,256]{1,0:T(8,128)(2,1)}), bf16[1408,2048]{1,0:T(8,128)(2,1)}) %all-gather.37.cloned.1.call-update) | async-done | bytes 5767184 | tf_op jit(solution)/shard_map/all_gather | solution.py:197
  1465.2 42.8 %reduce-scatter.27.cloned.1.call-done = f32[128,2048]{1,0:T(8,128)} async-done(((f32[512,2048]{1,0:T(8,128)}), f32[128,2048]{1,0:T(8,128)}) %reduce-scatter.27.cloned.1.call-update) | async-done | bytes 1048592 | tf_op jit(solution)/shard_map/reduce_scatter | solution.py:317
  1512.3 21.7 all-gather.41.cloned.1.call-done
  1589.0 36.7 reduce-scatter.31.cloned.1.call-done
  1628.1 31.5 reduce-scatter.25.cloned.1.call-done
  1664.5 21.8 all-gather.43.cloned.1.call-done
  1778.7 31.1 all-gather.57.cloned.1.call-done
  1833.4 400.4 %while.138 = (s32[]{:T(128)}, f32[4,128,384]{2,1,0:T(8,128)S(1)}, f32[8,4,64,128]{3,2,1,0:T(8,128)}, f32[8,4,64,128]{3,2,1,0:T(8,128)}, f32[8,4,64,384]{3,2,0,1:...) while((s32[]{:T(128)}, f32[4,128,384]{2,1,0:T(8,128)S(1)}, ...), condition=%wide.region_47.52_spmd, body=%wide.region_35.51_spmd.sunk | while | flops 1828386176 | bytes 31085416 | solution.py:105
  1844.6 21.0 custom-call.30
  2044.6 21.0 custom-call.30
  2094.6 21.0 custom-call.30
  2257.5 372.0 %while.139 = (s32[]{:T(128)}, f32[4,128,384]{2,1,0:T(8,128)S(1)}, f32[8,4,64,128]{3,2,1,0:T(8,128)}, f32[8,4,64,128]{3,2,1,0:T(8,128)}, f32[8,4,64,384]{3,2,0,1:...) while((s32[]{:T(128)}, f32[4,128,384]{2,1,0:T(8,128)S(1)}, ...), condition=%wide.region_69.74_spmd, body=%wide.region_57.73_spmd.sunk | while | flops 1828386176 | bytes 29245064 | solution.py:105
  2837.7 91.7 %reduce-scatter.43.cloned.1.call-done = bf16[1024,256]{1,0:T(8,128)(2,1)} async-done(((bf16[1024,2048]{1,0:T(8,128)(2,1)}), bf16[1024,256]{1,0:T(8,128)(2,1)}) %reduce-scatter.43.cloned.1.call-update) | async-done | bytes 524304 | tf_op jit(solution)/shard_map/reduce_scatter | solution.py:209
  2931.7 193.9 %reduce-scatter.47.cloned.1.call-done = bf16[256,2816]{1,0:T(8,128)(2,1)} async-done(((bf16[2048,2816]{1,0:T(8,128)(2,1)}), bf16[256,2816]{1,0:T(8,128)(2,1)}) %reduce-scatter.47.cloned.1.call-update) | async-done | bytes 1441808 | tf_op jit(solution)/shard_map/reduce_scatter | solution.py:212
  3125.6 195.7 %reduce-scatter.49.cloned.1.call-done = bf16[256,2816]{1,0:T(8,128)(2,1)} async-done(((bf16[2048,2816]{1,0:T(8,128)(2,1)}), bf16[256,2816]{1,0:T(8,128)(2,1)}) %reduce-scatter.49.cloned.1.call-update) | async-done | bytes 1441808 | tf_op jit(solution)/shard_map/reduce_scatter | solution.py:212
  3325.3 29.9 reduce-scatter.29.cloned.1.call-done
  3355.1 33.8 reduce-scatter.33.cloned.1.call-done
  3394.1 29.0 reduce-scatter.21.cloned.1.call-done
  3428.7 205.4 %reduce-scatter.37.cloned.1.call-done = bf16[256,3072]{1,0:T(8,128)(2,1)} async-done(((bf16[2048,3072]{1,0:T(8,128)(2,1)}), bf16[256,3072]{1,0:T(8,128)(2,1)}) %reduce-scatter.37.cloned.1.call-update) | async-done | bytes 1572880 | tf_op jit(solution)/shard_map/reduce_scatter | solution.py:203
  3634.1 209.9 %reduce-scatter.35.cloned.1.call-done = bf16[256,3072]{1,0:T(8,128)(2,1)} async-done(((bf16[2048,3072]{1,0:T(8,128)(2,1)}), bf16[256,3072]{1,0:T(8,128)(2,1)}) %reduce-scatter.35.cloned.1.call-update) | async-done | bytes 1572880 | tf_op jit(solution)/shard_map/reduce_scatter | solution.py:203
  3848.9 117.7 %all-reduce.51.cloned.1.call-done = f32[4,4096]{1,0:T(4,128)} async-done(((f32[4,4096]{1,0:T(4,128)}), f32[4,4096]{1,0:T(4,128)}) %all-reduce.51.cloned.1.call-update) | async-done | bytes 65552 | tf_op jit(solution)/shard_map/psum | solution.py:457
  3966.6 132.4 %all-reduce.53.cloned.1.call-done = (f32[2048]{0:T(1024)}, f32[4,2048]{1,0:T(4,128)}, f32[4,2048]{1,0:T(4,128)}, f32[16]{0:T(128)}, f32[16]{0:T(128)}, /*index=5*/f32[256]{0:T(256)}, f32[2048]{0:T(1024)}) async-done(((f32[2048]{0:T(1024)}, f32[4,2048]{1,0:T(4,128)}, f32[4,2048]{1,0:T(4,128)}, f32[16]{0:T(128)}, f32[16]{0:T(128)}, /*index=5*/f32[256]{0:T(256)}, f32[2048]{0:T(1024)}), (f32[2048]{0:T(1024)}, ...) | async-done | bytes 83088 | tf_op jit(solution)/shard_map/psum | solution.py:457
  (2359 shorter events, 1974.2 us)
Async XLA Ops:
  11.9 204.7 %all-gather.29.cloned.1.call-start = ((), (), s32[]{:S(2)}) async-start(), calls=%async_computation.19 | async-start | bytes 14155776 | tf_op jit(solution)/shard_map/all_gather | solution.py:193
  13.4 226.2 %all-gather.39.cloned.1.call-start = ((), (), s32[]{:S(2)}) async-start(), calls=%async_computation.26 | async-start | bytes 2621440 | tf_op jit(solution)/shard_map/all_gather | solution.py:253
  14.1 842.4 %all-gather.47.cloned.1.call-start = ((), (), s32[]{:S(2)}) async-start(), calls=%async_computation.47 | async-start | bytes 2359296 | tf_op jit(solution)/shard_map/all_gather | solution.py:25
  552.7 303.8 %all-gather.49.cloned.1.call-start = ((), (), s32[]{:S(2)}) async-start(), calls=%async_computation.48 | async-start | bytes 4718592 | tf_op jit(solution)/shard_map/all_gather | solution.py:25
  576.5 310.2 %all-gather.51.cloned.1.call-start = ((), (), s32[]{:S(2)}) async-start(), calls=%async_computation.49 | async-start | bytes 2359296 | tf_op jit(solution)/shard_map/all_gather | solution.py:25
  836.4 124.9 %all-gather.53.cloned.1.call-start = ((), (), s32[]{:S(2)}) async-start(), calls=%async_computation.50 | async-start | bytes 4718592 | tf_op jit(solution)/shard_map/all_gather | solution.py:25
  837.3 199.3 %all-gather.31.cloned.1.call-start = ((), (), s32[]{:S(2)}) async-start(), calls=%async_computation.20 | async-start | bytes 4718592 | tf_op jit(solution)/shard_map/all_gather | solution.py:195
  838.1 248.0 %reduce-scatter.19.cloned.1.call-start = ((), (), s32[]{:S(2)}) async-start(), calls=%async_computation.21 | async-start | bytes 5242880 | tf_op jit(solution)/shard_map/reduce_scatter | solution.py:287
  1052.3 247.3 %all-gather.35.cloned.1.call-start = ((), (), s32[]{:S(2)}) async-start(), calls=%async_computation.23 | async-start | bytes 12976128 | tf_op jit(solution)/shard_map/all_gather | solution.py:196
  1055.7 266.7 %all-gather.33.cloned.1.call-start = ((), (), s32[]{:S(2)}) async-start(), calls=%async_computation.22 | async-start | bytes 2621440 | tf_op jit(solution)/shard_map/all_gather | solution.py:297
  1137.4 209.7 %all-gather.55.cloned.1.call-start = ((), (), s32[]{:S(2)}) async-start(), calls=%async_computation.51 | async-start | bytes 2621440 | tf_op jit(solution)/shard_map/all_gather | solution.py:254
  1139.8 302.9 %all-gather.37.cloned.1.call-start = ((), (), s32[]{:S(2)}) async-start(), calls=%async_computation.24 | async-start | bytes 6488064 | tf_op jit(solution)/shard_map/all_gather | solution.py:197
  1140.3 367.6 %reduce-scatter.27.cloned.1.call-start = ((), (), s32[]{:S(2)}) async-start(), calls=%async_computation.30 | async-start | bytes 5242880 | tf_op jit(solution)/shard_map/reduce_scatter | solution.py:317
  1511.9 113.7 %reduce-scatter.31.cloned.1.call-start = ((), (), s32[]{:S(2)}) async-start(), calls=%async_computation.33 | async-start | bytes 5242880 | tf_op jit(solution)/shard_map/reduce_scatter | solution.py:317
  1588.9 97.4 %all-gather.43.cloned.1.call-start = ((), (), s32[]{:S(2)}) async-start(), calls=%async_computation.31 | async-start | bytes 2621440 | tf_op jit(solution)/shard_map/all_gather | solution.py:324
  1664.3 145.4 %all-gather.57.cloned.1.call-start = ((), (), s32[]{:S(2)}) async-start(), calls=%async_computation.52 | async-start | bytes 4718592 | tf_op jit(solution)/shard_map/all_gather | solution.py:25
  1736.2 497.7 %all-gather.61.cloned.1.call-start = ((), (), s32[]{:S(2)}) async-start(), calls=%async_computation.54 | async-start | bytes 4718592 | tf_op jit(solution)/shard_map/all_gather | solution.py:25
  1740.2 1083.2 %reduce-scatter.51.cloned.1.call-start = ((), (), s32[]{:S(2)}) async-start(), calls=%async_computation.45 | async-start | bytes 6488064 | tf_op jit(solution)/shard_map/reduce_scatter | solution.py:215
  1748.0 1075.5 %reduce-scatter.53.cloned.1.call-start = ((), (), s32[]{:S(2)}) async-start(), calls=%async_computation.46 | async-start | bytes 6488064 | tf_op jit(solution)/shard_map/reduce_scatter | solution.py:215
  1767.7 1059.6 %reduce-scatter.41.cloned.1.call-start = ((), (), s32[]{:S(2)}) async-start(), calls=%async_computation.39 | async-start | bytes 36864 | tf_op jit(solution)/shard_map/reduce_scatter | solution.py:206
  2638.4 188.9 %reduce-scatter.39.cloned.1.call-start = ((), (), s32[]{:S(2)}) async-start(), calls=%async_computation.38 | async-start | bytes 36864 | tf_op jit(solution)/shard_map/reduce_scatter | solution.py:206
  2641.1 196.6 %reduce-scatter.45.cloned.1.call-start = ((), (), s32[]{:S(2)}) async-start(), calls=%async_computation.42 | async-start | bytes 4718592 | tf_op jit(solution)/shard_map/reduce_scatter | solution.py:209
  2645.6 283.8 %reduce-scatter.43.cloned.1.call-start = ((), (), s32[]{:S(2)}) async-start(), calls=%async_computation.41 | async-start | bytes 4718592 | tf_op jit(solution)/shard_map/reduce_scatter | solution.py:209
  2651.8 473.8 %reduce-scatter.47.cloned.1.call-start = ((), (), s32[]{:S(2)}) async-start(), calls=%async_computation.43 | async-start | bytes 12976128 | tf_op jit(solution)/shard_map/reduce_scatter | solution.py:212
  2664.3 657.0 %reduce-scatter.49.cloned.1.call-start = ((), (), s32[]{:S(2)}) async-start(), calls=%async_computation.44 | async-start | bytes 12976128 | tf_op jit(solution)/shard_map/reduce_scatter | solution.py:212
  2676.5 678.6 %reduce-scatter.29.cloned.1.call-start = ((), (), s32[]{:S(2)}) async-start(), calls=%async_computation.32 | async-start | bytes 2621440 | tf_op jit(solution)/shard_map/reduce_scatter | solution.py:364
  2761.0 628.0 %reduce-scatter.33.cloned.1.call-start = ((), (), s32[]{:S(2)}) async-start(), calls=%async_computation.35 | async-start | bytes 2621440 | tf_op jit(solution)/shard_map/reduce_scatter | solution.py:364
  2789.1 634.1 %reduce-scatter.21.cloned.1.call-start = ((), (), s32[]{:S(2)}) async-start(), calls=%async_computation.25 | async-start | bytes 2621440 | tf_op jit(solution)/shard_map/reduce_scatter | solution.py:304
  2797.2 836.9 %reduce-scatter.37.cloned.1.call-start = ((), (), s32[]{:S(2)}) async-start(), calls=%async_computation.37 | async-start | bytes 14155776 | tf_op jit(solution)/shard_map/reduce_scatter | solution.py:203
  2808.8 1035.2 %reduce-scatter.35.cloned.1.call-start = ((), (), s32[]{:S(2)}) async-start(), calls=%async_computation.36 | async-start | bytes 14155776 | tf_op jit(solution)/shard_map/reduce_scatter | solution.py:203
  2821.7 1144.9 %all-reduce.51.cloned.1.call-start = ((), (), s32[]{:S(2)}) async-start(), calls=%async_computation.40 | async-start | bytes 131072 | tf_op jit(solution)/shard_map/psum | solution.py:457
  2826.9 1272.1 %all-reduce.53.cloned.1.call-start = ((), (), s32[]{:S(2)}) async-start(), calls=%async_computation.55 | async-start | bytes 167936 | tf_op jit(solution)/shard_map/psum | solution.py:457
  (372 other events, 10793.4 us)
Sparse Core Ops, SparseCore 0:
  12.1 25.2 all-gather.26
  40.2 176.4 all-gather.28
  552.8 50.0 all-gather.46
  605.4 71.5 all-gather.48
  836.5 50.1 all-gather.50
  889.4 71.8 all-gather.52
  963.3 73.2 all-gather.30
  1043.4 42.6 reduce-scatter.18
  1088.6 44.5 reduce-scatter.22
  1136.0 163.6 all-gather.34
  1349.1 93.5 all-gather.36
  1465.3 42.6 reduce-scatter.26
  1511.4 22.5 all-gather.40
  1581.1 44.4 reduce-scatter.30
  1628.2 31.3 reduce-scatter.24
  1736.3 73.3 all-gather.56
  1812.1 71.6 all-gather.60
  1887.7 109.1 reduce-scatter.50
  2001.0 110.3 reduce-scatter.52
  2638.6 51.8 reduce-scatter.40
  2693.7 52.5 reduce-scatter.38
  2750.3 87.2 reduce-scatter.44
  2841.3 88.0 reduce-scatter.42
  2933.2 192.2 reduce-scatter.46
  3129.6 191.6 reduce-scatter.48
  3324.6 30.5 reduce-scatter.28
  3357.5 31.4 reduce-scatter.32
  3391.7 31.4 reduce-scatter.20
  3426.7 207.3 reduce-scatter.36
  3637.5 206.4 reduce-scatter.34
  3850.0 116.5 all-reduce.50
  3974.8 124.2 all-reduce.52
  (6 shorter events, 131.5 us)
where the time goes:
time: 4130 us; the launch traced here: 4120 us
  waiting for transfers between devices  2140 us (52%)
  other arithmetic  914 us (22%)
  matrix products  667 us (16%)
  local copies, waits for them, and re-layouts  321 us (8%)
    another operation x128, other arithmetic, group_step(): lax.linalg.triangular_solve(system, targets, left_side=True, lower=True,...  660 us
    reduce_scatter x2, waiting for transfers between devices, settle_grads(): lax.psum_scatter(grad_in.astype(jnp.bfloat16), 'dp', scatter_dimension=0,...  415 us
    reduce_scatter x2, waiting for transfers between devices, settle_grads(): lax.psum_scatter(grad_ffn.astype(jnp.bfloat16), 'dp', scatter_dimension=0...  390 us
    psum x2, waiting for transfers between devices, body(): lax.psum((conv_query_part, conv_key_part, conv_value_part, rate_part, ste...  250 us
    all_gather x1, waiting for transfers between devices, fetch_weights(): lax.all_gather(w_in, 'dp', axis=0, tiled=True)  165 us
    all_gather x1, waiting for transfers between devices, fetch_weights(): lax.all_gather(w_ffn, 'dp', axis=0, tiled=True)  159 us
    all_gather x6, waiting for transfers between devices, prefix_2(): pieces = jax.tree.map(lambda part: lax.all_gather(part, axis), value)  118 us
    reduce_scatter x2, waiting for transfers between devices, settle_grads(): lax.psum_scatter(grad_out.astype(jnp.bfloat16), 'dp', scatter_dimension=1...  101 us
  transfers between devices with their start and end apart: 42, of which 31 were waited for; matrix products, arithmetic and copies ran while one was open for 36% of the time, Pallas kernels for 0%

commit v1 on v0

v1 whole, which is shorter than its diff:
```python
from functools import partial

import jax
import jax.numpy as jnp
from jax import lax
from jax.experimental import pallas as pl
from jax.experimental.pallas import tpu as pltpu
from jax.sharding import PartitionSpec as P

CHUNK = 128
KCONV = 4
LANES = 128
HALO = 16

EPSILON = 1e-06
HEAD_FLOOR = 0.01
F32 = jnp.float32
BF16 = jnp.bfloat16
NN = (((1,), (0,)), ((), ()))
NT = (((1,), (1,)), ((), ()))
TN = (((0,), (0,)), ((), ()))


def mm(left, right, dims=NN):
    return lax.dot_general(
        left.astype(BF16), right.astype(BF16), dims, preferred_element_type=F32
    )


def split(value):
    high = value.astype(BF16)
    return high, (value - high.astype(F32)).astype(BF16)


def mm3(left, right, dims=NN):
    left_high, left_low = split(left)
    right_high, right_low = split(right)
    return mm(left_high, right_high, dims) + (
        mm(left_high, right_low, dims) + mm(left_low, right_high, dims)
    )


def chunk_places(info_ref, micro, chunk, seq_count):
    first = info_ref[micro, seq_count] + chunk * CHUNK
    starts = [info_ref[micro, at] for at in range(seq_count)]
    rows = first + lax.broadcasted_iota(jnp.int32, (CHUNK, 1), 0)
    lanes = first + lax.broadcasted_iota(jnp.int32, (1, CHUNK), 1)
    seg_col = jnp.zeros((CHUNK, 1), jnp.int32)
    seg_row = jnp.zeros((1, CHUNK), jnp.int32)
    begun = jnp.zeros((CHUNK, 1), jnp.int32)
    seg_before = jnp.int32(0)
    seg_last = jnp.int32(0)
    for start in starts:
        seg_col = seg_col + jnp.where(rows >= start, 1, 0)
        seg_row = seg_row + jnp.where(lanes >= start, 1, 0)
        begun = jnp.maximum(begun, jnp.where(rows >= start, start, 0))
        seg_before = seg_before + jnp.where(first - 1 >= start, 1, 0)
        seg_last = seg_last + jnp.where(first + CHUNK - 1 >= start, 1, 0)
    offset = rows - begun
    row_ids = lax.broadcasted_iota(jnp.int32, (CHUNK, CHUNK), 0)
    col_ids = lax.broadcasted_iota(jnp.int32, (CHUNK, CHUNK), 1)
    same = seg_col == seg_row
    return dict(
        row_ids=row_ids,
        col_ids=col_ids,
        inclusive=jnp.logical_and(row_ids >= col_ids, same),
        strictly=jnp.logical_and(row_ids > col_ids, same),
        untouched=jnp.where(seg_col == seg_before, 1.0, 0.0).astype(F32),
        with_last=jnp.where(seg_col == seg_last, 1.0, 0.0).astype(F32),
        lags=[jnp.where(offset >= lag, 1.0, 0.0).astype(F32) for lag in range(1, KCONV)],
    )


def decay_parts(g_col, places):
    row_ids, col_ids = places["row_ids"], places["col_ids"]
    cum_row = jnp.sum(jnp.where(row_ids <= col_ids, g_col, 0.0), axis=0, keepdims=True)
    cum_col = jnp.sum(jnp.where(row_ids == col_ids, cum_row, 0.0), axis=1, keepdims=True)
    spread = jnp.where(places["inclusive"], cum_col - cum_row, 0.0)
    pair = jnp.where(places["inclusive"], jnp.exp(spread), 0.0)
    carry = jnp.exp(cum_col) * places["untouched"]
    cum_last = cum_col[CHUNK - 1 :, :]
    to_last = jnp.exp(jnp.minimum(cum_last - cum_col, 0.0)) * places["with_last"]
    return pair, carry, to_last, carry[CHUNK - 1 :, :]


def conv_rows(extended, taps, lags):
    total = taps[KCONV - 1 :, :] * extended[HALO:]
    for lag in range(1, KCONV):
        shifted = extended[HALO - lag : HALO - lag + CHUNK]
        total = total + taps[KCONV - 1 - lag : KCONV - lag, :] * shifted * lags[lag - 1]
    return total


def head_columns(head, heads, key_size, value_size):
    return (
        (head * key_size, key_size),
        ((heads + head) * key_size, key_size),
        (2 * heads * key_size + head * value_size, value_size),
    )


def unit_rows(active):
    return active * lax.rsqrt(jnp.sum(active * active, axis=1, keepdims=True) + EPSILON)


def softplus(value):
    return jnp.maximum(value, 0.0) + jnp.log1p(jnp.exp(-jnp.abs(value)))


def unit_lower_inverses(systems, places):
    row_ids, col_ids = places["row_ids"], places["col_ids"]
    eye = jnp.where(row_ids == col_ids, 1.0, 0.0).astype(F32)
    pairs = jnp.right_shift(row_ids, 1) == jnp.right_shift(col_ids, 1)
    found = [eye - jnp.where(pairs, system, 0.0) for system in systems]
    level = 1
    while (1 << level) < CHUNK:
        row_block = jnp.right_shift(row_ids, level)
        col_block = jnp.right_shift(col_ids, level)
        lower = jnp.logical_and(
            jnp.right_shift(row_block, 1) == jnp.right_shift(col_block, 1), row_block > col_block
        )
        inner = [
            INVERSE_MM(jnp.where(lower, system, 0.0), inverse)
            for system, inverse in zip(systems, found)
        ]
        found = [
            inverse - INVERSE_MM(inverse, middle) for inverse, middle in zip(found, inner)
        ]
        level += 1
    return found


INVERSE_MM = mm3


def mix_forward_kernel(
    info_ref,
    x_ref,
    rim_ref,
    dec_ref,
    taps_ref,
    par_ref,
    out_ref,
    cmap_ref,
    inv_ref,
    start_ref,
    final_ref,
    halo,
    state,
    *,
    heads,
    key_size,
    value_size,
    seq_count,
):
    micro, chunk = pl.program_id(0), pl.program_id(1)
    span = range(heads)

    @pl.when(chunk == 0)
    def _():
        halo[...] = rim_ref[0]
        row_ids = lax.broadcasted_iota(jnp.int32, (key_size, key_size), 0)
        col_ids = lax.broadcasted_iota(jnp.int32, (key_size, key_size), 1)
        eye = jnp.where(row_ids == col_ids, 1.0, 0.0).astype(F32)
        for head in span:
            state[head] = jnp.concatenate([jnp.zeros((key_size, value_size), F32), eye], axis=1)

    places = chunk_places(info_ref, micro, chunk, seq_count)
    dec = dec_ref[...]
    beta_all = jax.nn.sigmoid(dec)
    g_all = par_ref[0:1, :] * softplus(dec + par_ref[1:2, :])
    scale = key_size**-0.5

    queries, keys, values = [], [], []
    for head in span:
        rows = []
        for begin, width in head_columns(head, heads, key_size, value_size):
            cut = slice(begin, begin + width)
            extended = jnp.concatenate(
                [halo[:, cut].astype(F32), x_ref[:, cut].astype(F32)], axis=0
            )
            summed = conv_rows(extended, taps_ref[0:KCONV, cut], places["lags"])
            rows.append(summed * jax.nn.sigmoid(summed))
        queries.append(unit_rows(rows[0]) * scale)
        keys.append(unit_rows(rows[1]))
        values.append(rows[2])
    halo[...] = x_ref[CHUNK - HALO :, :]

    betas = [beta_all[:, heads + head : heads + head + 1] for head in span]
    decays = [decay_parts(g_all[:, head : head + 1], places) for head in span]
    grams = [mm(keys[head], keys[head], NT) for head in span]
    systems = [
        jnp.where(places["strictly"], betas[head] * decays[head][0] * grams[head], 0.0)
        for head in span
    ]
    inverses = unit_lower_inverses(systems, places)
    attends = [mm(queries[head], keys[head], NT) * decays[head][0] for head in span]
    solved = [
        mm(
            inverses[head],
            jnp.concatenate(
                [betas[head] * values[head], betas[head] * decays[head][1] * keys[head]], axis=1
            ),
        )
        for head in span
    ]
    starts = [state[head] for head in span]
    written = [
        jnp.concatenate(
            [solved[head][:, :value_size], jnp.zeros((CHUNK, key_size), F32)], axis=1
        )
        - mm(solved[head][:, value_size:], starts[head])
        for head in span
    ]
    outs = [
        decays[head][1] * mm(queries[head], starts[head]) + mm(attends[head], written[head])
        for head in span
    ]
    for head in span:
        _, _, to_last, carry_last = decays[head]
        inv_ref[0, head] = inverses[head].astype(BF16)
        start_ref[0, head] = starts[head].astype(BF16)
        out_ref[:, head * value_size : (head + 1) * value_size] = outs[head][:, :value_size]
        cmap_ref[:, head * key_size : (head + 1) * key_size] = outs[head][:, value_size:].astype(
            BF16
        )
        state[head] = carry_last * starts[head] + mm(to_last * keys[head], written[head], TN)

    @pl.when(chunk == pl.num_programs(1) - 1)
    def _():
        final_ref[0] = state[...]


def mix_backward_kernel(
    info_ref,
    x_ref,
    before_ref,
    rim_ref,
    dec_ref,
    taps_ref,
    par_ref,
    grad_ref,
    inv_ref,
    start_ref,
    incoming_ref,
    leaving_ref,
    dx_ref,
    rim_grad_ref,
    tail_ref,
    ddec_ref,
    dtaps_ref,
    dpar_ref,
    carry,
    dstate,
    *,
    heads,
    key_size,
    value_size,
    seq_count,
):
    micro, step = pl.program_id(0), pl.program_id(1)
    chunk = pl.num_programs(1) - 1 - step
    span = range(heads)

    @pl.when(step == 0)
    def _():
        carry[...] = jnp.zeros_like(carry)
        dstate[...] = leaving_ref[0].astype(F32)

    @pl.when(jnp.logical_and(micro == 0, step == 0))
    def _():
        dtaps_ref[...] = jnp.zeros_like(dtaps_ref)
        dpar_ref[...] = jnp.zeros_like(dpar_ref)

    places = chunk_places(info_ref, micro, chunk, seq_count)
    row_ids, col_ids = places["row_ids"], places["col_ids"]
    lags = places["lags"]
    dec = dec_ref[...]
    beta_all = jax.nn.sigmoid(dec)
    shifted_dec = dec + par_ref[1:2, :]
    g_all = par_ref[0:1, :] * softplus(shifted_dec)
    scale = key_size**-0.5
    opening = jnp.where(chunk == 0, rim_ref[0].astype(F32), before_ref[...].astype(F32))

    def extended_rows(cut):
        return jnp.concatenate([opening[:, cut], x_ref[:, cut].astype(F32)], axis=0)

    sums, norms, unit = [], [], []
    for head in span:
        mine = [
            conv_rows(extended_rows(slice(begin, begin + width)), taps_ref[0:KCONV, begin : begin + width], lags)
            for begin, width in head_columns(head, heads, key_size, value_size)
        ]
        active = [value * jax.nn.sigmoid(value) for value in mine]
        inverse_norms = [
            lax.rsqrt(jnp.sum(value * value, axis=1, keepdims=True) + EPSILON)
            for value in active[:2]
        ]
        sums.append(mine)
        norms.append(inverse_norms)
        unit.append([active[0] * inverse_norms[0], active[1] * inverse_norms[1], active[2]])
    keys = [unit[head][1] for head in span]
    key_low = [keys[head].astype(BF16) for head in span]
    query_low = [(unit[head][0] * scale).astype(BF16) for head in span]
    betas = [beta_all[:, heads + head : heads + head + 1] for head in span]
    decays = [decay_parts(g_all[:, head : head + 1], places) for head in span]
    grams = [mm(key_low[head], key_low[head], NT) for head in span]
    products = [mm(query_low[head], key_low[head], NT) for head in span]
    attends = [(products[head] * decays[head][0]).astype(BF16) for head in span]
    starts = []
    for head in span:
        saved = start_ref[0, head]
        starts.append(
            saved[:, :value_size].astype(F32)
            + mm(saved[:, value_size:], incoming_ref[0, head])
        )
    start_low = [starts[head].astype(BF16) for head in span]
    key_state = [mm(key_low[head], start_low[head]) for head in span]
    query_state = [mm(query_low[head], start_low[head]) for head in span]
    grads = [grad_ref[:, head * value_size : (head + 1) * value_size] for head in span]
    grad_low = [grads[head].astype(BF16) for head in span]
    residues = [unit[head][2] - decays[head][1] * key_state[head] for head in span]
    inverses = [inv_ref[0, head] for head in span]
    written = [mm(inverses[head], betas[head] * residues[head]).astype(BF16) for head in span]
    ahead = [dstate[head] for head in span]
    ahead_low = [ahead[head].astype(BF16) for head in span]
    key_last = [(decays[head][2] * keys[head]).astype(BF16) for head in span]
    dwritten = [
        mm(attends[head], grad_low[head], TN) + mm(key_last[head], ahead_low[head])
        for head in span
    ]
    dresidue = [mm(inverses[head], dwritten[head], TN) for head in span]
    dresidue_low = [dresidue[head].astype(BF16) for head in span]
    dattend = [
        jnp.where(places["inclusive"], mm(grad_low[head], written[head], NT), 0.0)
        for head in span
    ]
    dsystem = [
        jnp.where(places["strictly"], -mm(dresidue_low[head], written[head], NT), 0.0)
        for head in span
    ]
    dproducts = [(dattend[head] * decays[head][0]).astype(BF16) for head in span]
    dcarried = [decays[head][1] * grads[head] for head in span]
    dcarried_low = [dcarried[head].astype(BF16) for head in span]
    dkey_state = [-(betas[head] * decays[head][1]) * dresidue[head] for head in span]
    dkey_state_low = [dkey_state[head].astype(BF16) for head in span]
    dkey_last = [mm(written[head], ahead_low[head], NT) for head in span]
    dgram = [dsystem[head] * betas[head] * decays[head][0] for head in span]
    dgram_low = [dgram[head].astype(BF16) for head in span]
    dquery = [
        mm(dcarried_low[head], start_low[head], NT) + mm(dproducts[head], key_low[head])
        for head in span
    ]
    dkey = [
        mm(dproducts[head], query_low[head], TN)
        + decays[head][2] * dkey_last[head]
        + mm(dkey_state_low[head], start_low[head], NT)
        + mm(dgram_low[head], key_low[head])
        + mm(dgram_low[head], key_low[head], TN)
        for head in span
    ]
    lane_ids = lax.broadcasted_iota(jnp.int32, (CHUNK, LANES), 1)
    ddec = jnp.zeros((CHUNK, LANES), F32)
    dg_all = jnp.zeros((CHUNK, LANES), F32)
    for head in span:
        pair, carried, to_last, carry_last = decays[head]
        coupled = dsystem[head] * grams[head]
        dpair = (dattend[head] * products[head] + coupled * betas[head]) * pair
        dbeta = jnp.sum(coupled * pair, axis=1, keepdims=True) + jnp.sum(
            dresidue[head] * residues[head], axis=1, keepdims=True
        )
        dcarry = jnp.sum(
            grads[head] * query_state[head] - betas[head] * dresidue[head] * key_state[head],
            axis=1,
            keepdims=True,
        )
        dcarry_last = jnp.sum(
            jnp.sum(ahead[head] * starts[head], axis=1, keepdims=True), axis=0, keepdims=True
        )
        dto_last = jnp.sum(dkey_last[head] * keys[head], axis=1, keepdims=True) * to_last
        is_last = lax.broadcasted_iota(jnp.int32, (CHUNK, 1), 0) == CHUNK - 1
        dcum_col = (
            jnp.sum(dpair, axis=1, keepdims=True)
            + dcarry * carried
            - dto_last
            + jnp.where(
                is_last,
                dcarry_last * carry_last + jnp.sum(dto_last, axis=0, keepdims=True),
                0.0,
            )
        )
        dcum_row = jnp.sum(
            jnp.where(row_ids == col_ids, dcum_col, 0.0) - dpair, axis=0, keepdims=True
        )
        dg = jnp.sum(jnp.where(col_ids >= row_ids, dcum_row, 0.0), axis=1, keepdims=True)
        beta = betas[head]
        dg_all = jnp.where(lane_ids == head, dg, dg_all)
        ddec = jnp.where(lane_ids == heads + head, dbeta * beta * (1.0 - beta), ddec)
        dstate[head] = (
            carry_last * ahead[head]
            + mm(query_low[head], dcarried_low[head], TN)
            + mm(key_low[head], dkey_state_low[head], TN)
        )
    dstep = dg_all * par_ref[0:1, :] * jax.nn.sigmoid(shifted_dec)
    ddec = ddec + dstep
    ddec_ref[...] = ddec.astype(BF16)
    dpar_ref[0:1, :] += jnp.sum(dg_all * g_all, axis=0, keepdims=True)
    dpar_ref[1:2, :] += jnp.sum(dstep, axis=0, keepdims=True)

    edge = jnp.zeros((8, 1), F32)
    for head in span:
        dunit = [dquery[head] * scale, dkey[head]]
        dactive = [
            norms[head][at]
            * (
                dunit[at]
                - unit[head][at] * jnp.sum(dunit[at] * unit[head][at], axis=1, keepdims=True)
            )
            for at in range(2)
        ]
        dactive.append(betas[head] * dresidue[head])
        for at, (begin, width) in enumerate(head_columns(head, heads, key_size, value_size)):
            cut = slice(begin, begin + width)
            sig = jax.nn.sigmoid(sums[head][at])
            dsum = dactive[at] * sig * (1.0 + sums[head][at] * (1.0 - sig))
            extended = extended_rows(cut)
            taps = taps_ref[0:KCONV, cut]
            zeros = jnp.zeros((8, width), F32)
            dtaps_ref[KCONV - 1 : KCONV, cut] += jnp.sum(
                dsum * extended[HALO:], axis=0, keepdims=True
            )
            total = jnp.concatenate([zeros, taps[KCONV - 1 :, :] * dsum], axis=0)
            for lag in range(1, KCONV):
                masked = dsum * lags[lag - 1]
                at_tap = KCONV - 1 - lag
                dtaps_ref[at_tap : at_tap + 1, cut] += jnp.sum(
                    masked * extended[HALO - lag : HALO - lag + CHUNK], axis=0, keepdims=True
                )
                padded = jnp.concatenate(
                    [zeros, taps[at_tap : at_tap + 1, :] * masked, zeros], axis=0
                )
                total = total + padded[lag : lag + 8 + CHUNK]
            body_rows = jnp.concatenate(
                [total[8:CHUNK], total[CHUNK:] + carry[:, cut]], axis=0
            )
            dx_ref[:, cut] = body_rows.astype(BF16)
            carry[:, cut] = total[:8]

            @pl.when(step == 0)
            def _():
                tail_ref[0, :, cut] = body_rows[CHUNK - HALO :]

    @pl.when(chunk == 0)
    def _():
        rim_grad_ref[0] = carry[...]


def mix_sizes(pre_conv, micros, heads, key_size):
    rows = pre_conv.shape[0] // micros
    value_size = pre_conv.shape[1] // heads - 2 * key_size
    return rows, rows // CHUNK, value_size


def mix_forward(info, pre_conv, rim, dec, taps, par, micros, heads, key_size):
    rows, chunks, value_size = mix_sizes(pre_conv, micros, heads, key_size)
    width = pre_conv.shape[1]
    wide = value_size + key_size

    def by_rows(columns):
        return pl.BlockSpec((CHUNK, columns), lambda m, c: (m * chunks + c, 0))

    kernel = partial(
        mix_forward_kernel,
        heads=heads,
        key_size=key_size,
        value_size=value_size,
        seq_count=info.shape[1] - 1,
    )
    return pl.pallas_call(
        kernel,
        grid=(micros, chunks),
        in_specs=[
            pl.BlockSpec(memory_space=pltpu.SMEM),
            by_rows(width),
            pl.BlockSpec((1, HALO, width), lambda m, c: (m, 0, 0)),
            by_rows(LANES),
            pl.BlockSpec((8, width), lambda m, c: (0, 0)),
            pl.BlockSpec((8, LANES), lambda m, c: (0, 0)),
        ],
        out_specs=[
            by_rows(heads * value_size),
            by_rows(heads * key_size),
            pl.BlockSpec((1, heads, CHUNK, CHUNK), lambda m, c: (m * chunks + c, 0, 0, 0)),
            pl.BlockSpec((1, heads, key_size, wide), lambda m, c: (m * chunks + c, 0, 0, 0)),
            pl.BlockSpec((1, heads, key_size, wide), lambda m, c: (m, 0, 0, 0)),
        ],
        out_shape=[
            jax.ShapeDtypeStruct((micros * rows, heads * value_size), F32),
            jax.ShapeDtypeStruct((micros * rows, heads * key_size), BF16),
            jax.ShapeDtypeStruct((micros * chunks, heads, CHUNK, CHUNK), BF16),
            jax.ShapeDtypeStruct((micros * chunks, heads, key_size, wide), BF16),
            jax.ShapeDtypeStruct((micros, heads, key_size, wide), F32),
        ],
        scratch_shapes=[
            pltpu.VMEM((HALO, width), BF16),
            pltpu.VMEM((heads, key_size, wide), F32),
        ],
        compiler_params=pltpu.CompilerParams(
            dimension_semantics=("arbitrary", "arbitrary"), vmem_limit_bytes=VMEM_BYTES
        ),
        name="mix_forward",
    )(info, pre_conv, rim, dec, taps, par)


def mix_backward(
    info, pre_conv, rim, dec, taps, par, grad, inverses, starts, incoming, leaving, micros, heads, key_size
):
    rows, chunks, value_size = mix_sizes(pre_conv, micros, heads, key_size)
    width = pre_conv.shape[1]
    wide = value_size + key_size
    halo_blocks = CHUNK // HALO

    def at(m, s):
        return m * chunks + chunks - 1 - s

    def by_rows(columns):
        return pl.BlockSpec((CHUNK, columns), lambda m, s: (at(m, s), 0))

    kernel = partial(
        mix_backward_kernel,
        heads=heads,
        key_size=key_size,
        value_size=value_size,
        seq_count=info.shape[1] - 1,
    )
    return pl.pallas_call(
        kernel,
        grid=(micros, chunks),
        in_specs=[
            pl.BlockSpec(memory_space=pltpu.SMEM),
            by_rows(width),
            pl.BlockSpec(
                (HALO, width), lambda m, s: (jnp.maximum(at(m, s) * halo_blocks - 1, 0), 0)
            ),
            pl.BlockSpec((1, HALO, width), lambda m, s: (m, 0, 0)),
            by_rows(LANES),
            pl.BlockSpec((8, width), lambda m, s: (0, 0)),
            pl.BlockSpec((8, LANES), lambda m, s: (0, 0)),
            by_rows(heads * value_size),
            pl.BlockSpec((1, heads, CHUNK, CHUNK), lambda m, s: (at(m, s), 0, 0, 0)),
            pl.BlockSpec((1, heads, key_size, wide), lambda m, s: (at(m, s), 0, 0, 0)),
            pl.BlockSpec((1, heads, key_size, value_size), lambda m, s: (m, 0, 0, 0)),
            pl.BlockSpec((1, heads, key_size, value_size), lambda m, s: (m, 0, 0, 0)),
        ],
        out_specs=[
            by_rows(width),
            pl.BlockSpec((1, 8, width), lambda m, s: (m, 0, 0)),
            pl.BlockSpec((1, HALO, width), lambda m, s: (m, 0, 0)),
            by_rows(LANES),
            pl.BlockSpec((8, width), lambda m, s: (0, 0)),
            pl.BlockSpec((8, LANES), lambda m, s: (0, 0)),
        ],
        out_shape=[
            jax.ShapeDtypeStruct((micros * rows, width), BF16),
            jax.ShapeDtypeStruct((micros, 8, width), F32),
            jax.ShapeDtypeStruct((micros, HALO, width), F32),
            jax.ShapeDtypeStruct((micros * rows, LANES), BF16),
            jax.ShapeDtypeStruct((8, width), F32),
            jax.ShapeDtypeStruct((8, LANES), F32),
        ],
        scratch_shapes=[
            pltpu.VMEM((8, width), F32),
            pltpu.VMEM((heads, key_size, value_size), F32),
        ],
        compiler_params=pltpu.CompilerParams(
            dimension_semantics=("arbitrary", "arbitrary"), vmem_limit_bytes=VMEM_BYTES
        ),
        name="mix_backward",
    )(info, pre_conv, pre_conv, rim, dec, taps, par, grad, inverses, starts, incoming, leaving)


VMEM_BYTES = 48 * 1024 * 1024


def from_behind(value, axis, steps):
    count = lax.axis_size(axis)
    leading, last = (max(0, -steps), min(count, count - steps))
    return lax.ppermute(value, axis, [(source, source + steps) for source in range(leading, last)])


def head_gather(value):
    return lax.all_gather(value, "head", axis=1, tiled=True)


def head_scatter(value):
    return lax.psum_scatter(value, "head", scatter_dimension=1, tiled=True)


def scan_states(maps, sums, backward):
    count, mine = lax.axis_size("dp"), lax.axis_index("dp")
    packed = lax.all_gather(jnp.concatenate([maps, sums], axis=-1).astype(BF16), "dp")
    if backward:
        packed = packed[::-1]
        mine = count - 1 - mine
    key_size = maps.shape[-1]
    state = jnp.zeros(sums.shape, F32)
    for position in range(count - 1):
        block = packed[position]
        moved = jnp.einsum(
            "mhji,mhjv->mhiv" if backward else "mhij,mhjv->mhiv",
            block[..., :key_size],
            state.astype(BF16),
            preferred_element_type=F32,
        )
        state = jnp.where(position < mine, moved + block[..., key_size:].astype(F32), state)
    return state


def contract_rows(left, right):
    return lax.dot_general(left, right, TN, preferred_element_type=F32)


def contract_cols(left, right):
    return lax.dot_general(left, right, NT, preferred_element_type=F32)


def norm_backward(grad_in, normed_rows, scale):
    return scale * (grad_in - normed_rows * jnp.mean(grad_in * normed_rows, axis=-1, keepdims=True))


def dp_gather(value, axis):
    return lax.all_gather(value, "dp", axis=axis, tiled=True)


def dp_scatter(value, axis):
    return lax.psum_scatter(value.astype(BF16), "dp", scatter_dimension=axis, tiled=True).astype(F32)


def body(
    tokens,
    out_grad,
    seq_lengths,
    attn_norm,
    query_proj,
    key_proj,
    value_proj,
    gate_proj,
    decay_proj,
    beta_proj,
    conv_query,
    conv_key,
    conv_value,
    log_rate,
    step_bias,
    head_norm,
    out_proj,
    ffn_norm,
    ffn_gate,
    ffn_up,
    ffn_down,
):
    head_rank = lax.axis_index("head")
    heads = decay_proj.shape[1]
    qk_width = query_proj.shape[1]
    v_width = value_proj.shape[1]
    key_size = qk_width // heads
    value_size = v_width // heads
    ffn_width = ffn_gate.shape[1]
    conv_width = 2 * qk_width + v_width
    main_width = conv_width + v_width
    micros = tokens.shape[0]
    model = tokens.shape[2]

    decay_pad = jnp.zeros((decay_proj.shape[0], LANES - 2 * heads), decay_proj.dtype)
    w_in = dp_gather(
        jnp.concatenate(
            [query_proj, key_proj, value_proj, gate_proj, decay_proj, beta_proj, decay_pad], axis=1
        ),
        0,
    )
    w_out = dp_gather(out_proj, 1)
    w_ffn = dp_gather(jnp.concatenate([ffn_gate, ffn_up], axis=1), 0)
    w_down = dp_gather(ffn_down, 1)

    def of_mine(whole, width):
        return lax.dynamic_slice_in_dim(whole, head_rank * width, width, whole.ndim - 1)

    taps = jnp.concatenate(
        [of_mine(conv_query, qk_width), of_mine(conv_key, qk_width), of_mine(conv_value, v_width)],
        axis=1,
    )
    taps = jnp.pad(taps, ((0, 8 - KCONV), (0, 0)))
    par = jnp.pad(
        jnp.stack([-jnp.exp(of_mine(log_rate, heads)), of_mine(step_bias, heads)]),
        ((0, 6), (0, LANES - heads)),
    )

    residual = tokens.astype(F32)
    scale_one = lax.rsqrt(jnp.mean(residual * residual, axis=-1, keepdims=True) + EPSILON)
    normed_one = residual * scale_one
    normed_all = head_gather((normed_one * attn_norm).astype(BF16))
    cotangent_all = head_gather(out_grad)
    block_rows = normed_all.shape[1]
    normed_all = normed_all.reshape(micros * block_rows, model)
    cotangent_all = cotangent_all.reshape(micros * block_rows, model)
    first_row = lax.axis_index("dp") * block_rows
    ends = jnp.cumsum(seq_lengths, axis=1)
    info = jnp.concatenate(
        [ends - seq_lengths, jnp.full((micros, 1), first_row, jnp.int32)], axis=1
    ).astype(jnp.int32)
    pre_conv = jnp.dot(normed_all, w_in[:, :conv_width], preferred_element_type=F32).astype(BF16)
    gate_lin = jnp.dot(normed_all, w_in[:, conv_width:main_width], preferred_element_type=F32)
    dec = jnp.dot(normed_all, w_in[:, main_width:], preferred_element_type=F32)
    last_rows = pre_conv.reshape(micros, block_rows, conv_width)[:, block_rows - HALO :]
    rim = from_behind(last_rows, "dp", 1)

    plain, carried_map, inverses, starts, final = mix_forward(
        info, pre_conv, rim, dec, taps, par, micros, heads, key_size
    )
    block_map = final[..., value_size:]
    incoming = scan_states(block_map, final[..., :value_size], False)
    head_rows = (micros, block_rows, heads)
    carried_map = carried_map.reshape(head_rows + (key_size,))
    mixed = plain.reshape(head_rows + (value_size,)) + jnp.einsum(
        "mthd,mhdv->mthv", carried_map, incoming.astype(BF16), preferred_element_type=F32
    )
    out_scale = lax.rsqrt(jnp.mean(mixed * mixed, axis=-1, keepdims=True) + HEAD_FLOOR)
    normed_mix = mixed * out_scale
    gate_lin = gate_lin.reshape(head_rows + (value_size,))
    gate_sigmoid = jax.nn.sigmoid(gate_lin)
    gate_active = gate_lin * gate_sigmoid
    gated = (normed_mix * head_norm * gate_active).astype(BF16).reshape(-1, v_width)

    mix_part = jnp.dot(gated, w_out, preferred_element_type=F32)
    after_mix = residual + head_scatter(mix_part.reshape(micros, block_rows, model))
    scale_two = lax.rsqrt(jnp.mean(after_mix * after_mix, axis=-1, keepdims=True) + EPSILON)
    normed_two = after_mix * scale_two
    ffn_all = head_gather((normed_two * ffn_norm).astype(BF16)).reshape(-1, model)
    gate_ffn = jnp.dot(ffn_all, w_ffn[:, :ffn_width], preferred_element_type=F32)
    up_ffn = jnp.dot(ffn_all, w_ffn[:, ffn_width:], preferred_element_type=F32)
    ffn_sigmoid = jax.nn.sigmoid(gate_ffn)
    ffn_active = gate_ffn * ffn_sigmoid
    hidden = (ffn_active * up_ffn).astype(BF16)
    ffn_part = jnp.dot(hidden, w_down, preferred_element_type=F32).astype(BF16)
    ffn_sum = head_scatter(ffn_part.reshape(micros, block_rows, model)).astype(F32)
    block_out = (after_mix + ffn_sum).astype(BF16)

    hidden_grad = contract_cols(cotangent_all, w_down)
    shard_down = dp_scatter(contract_rows(hidden, cotangent_all), 1)
    gate_ffn_grad = hidden_grad * up_ffn * ffn_sigmoid * (1.0 + gate_ffn * (1.0 - ffn_sigmoid))
    up_ffn_grad = hidden_grad * ffn_active
    gate_up_grad = jnp.concatenate([gate_ffn_grad, up_ffn_grad], axis=1).astype(BF16)
    shard_ffn = dp_scatter(contract_rows(ffn_all, gate_up_grad), 0)
    ffn_in_part = contract_cols(gate_up_grad, w_ffn)
    ffn_in_grad = head_scatter(ffn_in_part.reshape(micros, block_rows, model))
    grad_norm_two = jnp.sum(ffn_in_grad * normed_two, axis=(0, 1))
    after_mix_grad = out_grad.astype(F32) + norm_backward(
        ffn_in_grad * ffn_norm, normed_two, scale_two
    )

    branch_grad = head_gather(after_mix_grad.astype(BF16)).reshape(-1, model)
    gated_grad = contract_cols(branch_grad, w_out).reshape(head_rows + (value_size,))
    shard_out = dp_scatter(contract_rows(gated, branch_grad), 1)
    grad_head_norm = jnp.sum(gated_grad * normed_mix * gate_active, axis=(0, 1, 2))
    gate_lin_grad = (
        gated_grad * normed_mix * head_norm * gate_sigmoid * (1.0 + gate_lin * (1.0 - gate_sigmoid))
    )
    mixed_grad = norm_backward(gated_grad * head_norm * gate_active, normed_mix, out_scale)

    local_grad = jnp.einsum(
        "mthd,mthv->mhdv", carried_map, mixed_grad.astype(BF16), preferred_element_type=F32
    )
    leaving = scan_states(block_map, local_grad, True)
    pre_grad, rim_grad, tail, dec_grad, taps_grad, par_grad = mix_backward(
        info,
        pre_conv,
        rim,
        dec,
        taps,
        par,
        mixed_grad.reshape(-1, v_width),
        inverses,
        starts,
        incoming,
        leaving,
        micros,
        heads,
        key_size,
    )
    back_rim = from_behind(rim_grad, "dp", -1)
    tail = jnp.concatenate([tail[:, :8], tail[:, 8:] + back_rim], axis=1).astype(BF16)
    pre_grad = lax.dynamic_update_slice(
        pre_grad.reshape(micros, block_rows, conv_width), tail, (0, block_rows - HALO, 0)
    ).reshape(-1, conv_width)

    proj_grad = jnp.concatenate(
        [pre_grad, gate_lin_grad.reshape(-1, v_width).astype(BF16), dec_grad], axis=1
    )
    shard_in = dp_scatter(contract_rows(normed_all, proj_grad), 0)
    normed_part = contract_cols(proj_grad, w_in).astype(BF16)
    normed_grad = head_scatter(normed_part.reshape(micros, block_rows, model)).astype(F32)
    grad_norm_one = jnp.sum(normed_grad * normed_one, axis=(0, 1))
    input_grad = after_mix_grad + norm_backward(normed_grad * attn_norm, normed_one, scale_one)

    small = jnp.concatenate(
        [
            taps_grad[:KCONV].reshape(-1),
            jnp.pad(par_grad[0, :heads], (0, LANES - heads)),
            jnp.pad(par_grad[1, :heads], (0, LANES - heads)),
            grad_head_norm,
            grad_norm_one,
            grad_norm_two,
        ]
    ).reshape(-1, LANES)
    small = jnp.sum(lax.all_gather(small, "dp"), axis=0)
    small = lax.all_gather(small, "head")
    head_count = small.shape[0]
    tap_rows = KCONV * conv_width // LANES
    taps_all = small[:, :tap_rows].reshape(head_count, KCONV, conv_width).transpose(1, 0, 2)

    def joined(low, high):
        return taps_all[:, :, low:high].reshape(KCONV, -1)

    rest = jnp.sum(small[:, tap_rows + 2 :], axis=0).reshape(-1)
    return (
        block_out,
        input_grad,
        rest[value_size : value_size + model],
        shard_in[:, :qk_width],
        shard_in[:, qk_width : 2 * qk_width],
        shard_in[:, 2 * qk_width : conv_width],
        shard_in[:, conv_width:main_width],
        shard_in[:, main_width : main_width + heads],
        shard_in[:, main_width + heads : main_width + 2 * heads],
        joined(0, qk_width),
        joined(qk_width, 2 * qk_width),
        joined(2 * qk_width, conv_width),
        small[:, tap_rows, :heads].reshape(-1),
        small[:, tap_rows + 1, :heads].reshape(-1),
        rest[:value_size],
        shard_out,
        rest[value_size + model :],
        shard_ffn[:, :ffn_width],
        shard_ffn[:, ffn_width:],
        shard_down,
    )


def solution(mesh):
    rows, plane, turned, whole = P(None, ("dp", "head"), None), P("dp", "head"), P("head", "dp"), P()
    in_specs = (rows, rows, whole, whole) + (plane,) * 6 + (whole,) * 6
    in_specs += (turned, whole, plane, plane, turned)
    out_specs = (rows, rows, whole) + (plane,) * 6 + (whole,) * 6
    out_specs += (turned, whole, plane, plane, turned)
    return jax.shard_map(body, mesh=mesh, in_specs=in_specs, out_specs=out_specs, check_vma=False)
```

time: 4130 us -> 1890 us (0.46)
  other arithmetic: 914 us -> 32.4 us
  waiting for transfers between devices: 2140 us -> 1430 us
  matrix products: 667 us -> 194 us
  local copies, waits for them, and re-layouts: 321 us -> 82.2 us
  Pallas kernels: 0 us -> 80.3 us
    another operation x264 -> x4, other arithmetic: 703 us -> 0.29 us  [the longest x1 0.18 us: body(): ends = jnp.cumsum(seq_lengths, axis=1)]
    reduce_scatter x18 -> x8, waiting for transfers between devices: 1190 us -> 676 us  [the longest x4 492 us: dp_scatter(): lax.psum_scatter(value.astype(BF16), 'dp', scatter_dimension=axis, tiled=...]
    dot_general x434 -> x31, matrix products: 617 us -> 194 us  [the longest x4 63.1 us: contract_cols(): return lax.dot_general(left, right, NT, preferred_element_type=F32)]
    psum x2 -> x0, waiting for transfers between devices: 250 us -> none  [body(): lax.psum((conv_query_part, conv_key_part, conv_value_part, rate_part, ste...]
    pallas_call x0 -> x2, Pallas kernels: none -> 80.3 us  [the longest x1 45.2 us: mix_backward(): pl.pallas_call(kernel, grid=(micros, chunks), in_specs=[pl.BlockSpec(memo...]
    squeeze x96 -> x3, local copies, waits for them, and re-layouts: 86.7 us -> 6.82 us  [the longest x2 6.82 us: scan_states(): block = packed[position]]
    mul x90 -> x0, other arithmetic: 59.6 us -> none  [the longest x16 17.6 us: group_step(): beta_rows[:, :, None] * values]
    another operation x64 -> x0, matrix products: 49.9 us -> none  [group_step(): lax.linalg.triangular_solve(system, targets, left_side=True, lower=True,...]
  transfers between devices with their start and end apart: 42 -> 20, of which waited for: 31 -> 19; matrix products, arithmetic and copies ran while one was open for 36% -> 10% of each run, Pallas kernels for 0% -> 2%
where the time goes in v1:
time: 1890 us; the launch traced here: 1880 us
  waiting for transfers between devices  1430 us (76%)
  matrix products  194 us (10%)
  local copies, waits for them, and re-layouts  82.2 us (4%)
  Pallas kernels  80.3 us (4%)
  blocking collectives  40 us (2%)
  other arithmetic  32.4 us (2%)
    reduce_scatter x4, waiting for transfers between devices, dp_scatter(): lax.psum_scatter(value.astype(BF16), 'dp', scatter_dimension=axis, tiled=...  492 us
    all_gather x4, waiting for transfers between devices, dp_gather(): return lax.all_gather(value, 'dp', axis=axis, tiled=True)  490 us
    reduce_scatter x4, waiting for transfers between devices, head_scatter(): return lax.psum_scatter(value, 'head', scatter_dimension=1, tiled=True)  184 us
    all_gather x4, waiting for transfers between devices, head_gather(): return lax.all_gather(value, 'head', axis=1, tiled=True)  135 us
    all_gather x2, waiting for transfers between devices, scan_states(): lax.all_gather(jnp.concatenate([maps, sums], axis=-1).astype(BF16), 'dp')  124 us
    dot_general x4, matrix products, contract_cols(): return lax.dot_general(left, right, NT, preferred_element_type=F32)  63.1 us
    dot_general x4, matrix products, contract_rows(): return lax.dot_general(left, right, TN, preferred_element_type=F32)  55.6 us
    pallas_call x1, Pallas kernels, mix_backward(): pl.pallas_call(kernel, grid=(micros, chunks), in_specs=[pl.BlockSpec(memo...  45.2 us
  transfers between devices with their start and end apart: 20, of which 19 were waited for; matrix products, arithmetic and copies ran while one was open for 10% of the time, Pallas kernels for 2%

profile of v1, /device:TPU:0, one launch (start us, length us, event | category | flops | bytes accessed | tf_op | source)
XLA Modules:
  0.0 1880.0 jit_solution(16687512782164857175)
XLA Ops:
  15.6 33.8 %all-gather.13.cloned.1.call-done = bf16[2,512,2048]{2,1,0:T(8,128)(2,1)} async-done(((bf16[2,128,2048]{2,1,0:T(8,128)(2,1)}), bf16[2,512,2048]{2,1,0:T(8,128)(2,1)}) %all-gather.13.cloned.1.call-update) | async-done | bytes 4194320 | tf_op jit(solution)/shard_map/all_gather | solution.py:592
  49.4 185.6 %all-gather.15.cloned.1.call-done = bf16[2048,3200]{1,0:T(8,128)(2,1)} async-done(((bf16[256,3200]{1,0:T(8,128)(2,1)}), bf16[2048,3200]{1,0:T(8,128)(2,1)}) %all-gather.15.cloned.1.call-update) | async-done | bytes 13107216 | tf_op jit(solution)/shard_map/all_gather | solution.py:632
  235.1 13.5 fusion.14.x_ref.before_ref
  253.5 35.1 %mix_forward.1 = (f32[1024,1024]{1,0:T(8,128)}, bf16[1024,512]{1,0:T(8,128)(2,1)S(1)}, bf16[8,4,128,128]{3,2,1,0:T(8,128)(2,1)S(1)}, bf16[8,4,128,384]{3,2,1,0:T(8,128)(2,1)}, f32[2,4,128,384]{3,2,1,0:T(8,128)S(1)}) custom-call(s32[2,5]{1,0:T(2,128)S(1)} %concatenate.54.info_ref, bf16[1024,2048]{1,0:T(8,128)(2,1)} %copy-done.10, ...), custom_call_target="tpu_custom_call" | custom-call | tf_op jit(solution)/shard_map/mix_forward/pallas_call | solution.py:479
  314.5 76.6 %all-gather.17.cloned.1.call-done = bf16[8,2,4,128,384]{4,3,2,1,0:T(8,128)(2,1)} async-done(((bf16[1,2,4,128,384]{4,3,2,1,0:T(8,128)(2,1)}), bf16[8,2,4,128,384]{4,3,2,1,0:T(8,128)(2,1)}) %all-gather.17.cloned.1.call-update) | async-done | bytes 6291472 | tf_op jit(solution)/shard_map/all_gather | solution.py:601
  404.1 6.9 multiply_convert_fusion.4
  411.0 55.3 %all-gather.19.cloned.1.call-done = bf16[1024,2048]{1,0:T(8,128)(2,1)} async-done(((bf16[1024,256]{1,0:T(8,128)(2,1)}), bf16[1024,2048]{1,0:T(8,128)(2,1)}) %all-gather.19.cloned.1.call-update) | async-done | bytes 4194320 | tf_op jit(solution)/shard_map/all_gather | solution.py:632
  466.2 8.9 fusion.11
  477.9 67.4 %reduce-scatter.9.cloned.1.call-done = f32[2,128,2048]{2,1,0:T(8,128)} async-done(((f32[2,512,2048]{2,1,0:T(8,128)}), f32[2,128,2048]{2,1,0:T(8,128)}) %reduce-scatter.9.cloned.1.call-update) | async-done | bytes 2097168 | tf_op jit(solution)/shard_map/reduce_scatter | solution.py:596
  549.4 31.9 %all-gather.27.cloned.1.call-done = bf16[2,512,2048]{2,1,0:T(8,128)(2,1)} async-done(((bf16[2,128,2048]{2,1,0:T(8,128)(2,1)}), bf16[2,512,2048]{2,1,0:T(8,128)(2,1)}) %all-gather.27.cloned.1.call-update) | async-done | bytes 4194320 | tf_op jit(solution)/shard_map/all_gather | solution.py:592
  581.3 95.9 %all-gather.25.cloned.1.call-done = bf16[1408,2048]{1,0:T(8,128)(2,1)} async-done(((bf16[1408,256]{1,0:T(8,128)(2,1)}), bf16[1408,2048]{1,0:T(8,128)(2,1)}) %all-gather.25.cloned.1.call-update) | async-done | bytes 5767184 | tf_op jit(solution)/shard_map/all_gather | solution.py:632
  677.2 11.8 fusion.97
  689.0 153.1 %all-gather.23.cloned.1.call-done = bf16[2048,2816]{1,0:T(8,128)(2,1)} async-done(((bf16[256,2816]{1,0:T(8,128)(2,1)}), bf16[2048,2816]{1,0:T(8,128)(2,1)}) %all-gather.23.cloned.1.call-update) | async-done | bytes 11534352 | tf_op jit(solution)/shard_map/all_gather | solution.py:632
  842.0 34.9 %all-gather.21.cloned.1.call-done = bf16[2,512,2048]{2,1,0:T(8,128)(2,1)} async-done(((bf16[2,128,2048]{2,1,0:T(8,128)(2,1)}), bf16[2,512,2048]{2,1,0:T(8,128)(2,1)}) %all-gather.21.cloned.1.call-update) | async-done | bytes 4194320 | tf_op jit(solution)/shard_map/all_gather | solution.py:592
  876.9 11.8 fusion.2
  888.7 15.0 multiply_convert_fusion.1
  903.8 18.7 fusion.17
  922.7 71.6 %reduce-scatter.13.cloned.1.call-done = f32[2,128,2048]{2,1,0:T(8,128)} async-done(((f32[2,512,2048]{2,1,0:T(8,128)}), f32[2,128,2048]{2,1,0:T(8,128)}) %reduce-scatter.13.cloned.1.call-update) | async-done | bytes 2097168 | tf_op jit(solution)/shard_map/reduce_scatter | solution.py:596
  999.1 34.6 %all-gather.29.cloned.1.call-done = bf16[2,512,2048]{2,1,0:T(8,128)(2,1)} async-done(((bf16[2,128,2048]{2,1,0:T(8,128)(2,1)}), bf16[2,512,2048]{2,1,0:T(8,128)(2,1)}) %all-gather.29.cloned.1.call-update) | async-done | bytes 4194320 | tf_op jit(solution)/shard_map/all_gather | solution.py:592
  1033.7 12.7 multiply_reduce_fusion
  1052.3 10.5 convolution_convert_fusion.2
  1063.1 18.3 convolution_convert_fusion.1
  1103.8 47.6 %all-gather.31.cloned.1.call-done = bf16[8,2,4,128,384]{4,3,2,1,0:T(8,128)(2,1)} async-done(((bf16[1,2,4,128,384]{4,3,2,1,0:T(8,128)(2,1)}), bf16[8,2,4,128,384]{4,3,2,1,0:T(8,128)(2,1)}) %all-gather.31.cloned.1.call-update) | async-done | bytes 6291472 | tf_op jit(solution)/shard_map/all_gather | solution.py:601
  1157.5 45.2 %mix_backward.1 = (bf16[1024,2048]{1,0:T(8,128)(2,1)}, f32[2,8,2048]{2,1,0:T(8,128)S(1)}, f32[2,16,2048]{2,1,0:T(8,128)S(1)}, bf16[1024,128]{1,0:T(8,128)(2,1)S(...) custom-call(s32[2,5]{1,0:T(2,128)S(1)} %concatenate.54.info_ref, bf16[1024,2048]{1,0:T(8,128)(2,1)} %copy-done.10, ...), custom_call_target="tpu_custom_call" | custom-call | tf_op jit(solution)/shard_map/mix_backward/pallas_call | solution.py:536
  1213.2 19.9 %convolution_convert_fusion.3 = bf16[1024,2048]{1,0:T(8,128)(2,1)} fusion(bf16[2048,3200]{1,0:T(8,128)(2,1)} %all-gather.15.cloned.1.call-done, bf16[1024,128]{1,0:T(8,128)(2,1)S(1)} %get-tuple-element.39, bf16[1024,1024]{1,0:T(8,128)(2,1)S(1)} %bitcast.136, bf16[1024,2048]{1,0:T(8,128)(2,1)} %bitcast.158), kind=kOutput, calls=%fused_computation.33 | convolution fusion | flops 13443530752 | bytes 23855104 | tf_op jit(solution)/shard_map/dot_general | solution.py:624
  1233.2 10.9 convolution_convert_fusion.4
  1245.8 20.5 %convolution_convert_fusion = bf16[2048,3200]{1,0:T(8,128)(2,1)} fusion(bf16[1024,2048]{1,0:T(8,128)(2,1)} %bitcast.148, bf16[1024,128]{1,0:T(8,128)(2,1)S(1)} %get-tuple-element.39, bf16[1024,1024]{1,0:T(8,128)(2,1)S(1)} %bitcast.137, bf16[1024,2048]{1,0:T(8,128)(2,1)} %bitcast.159), kind=kOutput, calls=%fused_computation | convolution fusion | flops 13447987200 | bytes 23855104 | tf_op jit(solution)/shard_map/dot_general | solution.py:620
  1268.8 193.7 %reduce-scatter.21.cloned.1.call-done = bf16[256,2816]{1,0:T(8,128)(2,1)} async-done(((bf16[2048,2816]{1,0:T(8,128)(2,1)}), bf16[256,2816]{1,0:T(8,128)(2,1)}) %reduce-scatter.21.cloned.1.call-update) | async-done | bytes 1441808 | tf_op jit(solution)/shard_map/reduce_scatter | solution.py:636
  1465.6 87.8 %reduce-scatter.19.cloned.1.call-done = bf16[1024,256]{1,0:T(8,128)(2,1)} async-done(((bf16[1024,2048]{1,0:T(8,128)(2,1)}), bf16[1024,256]{1,0:T(8,128)(2,1)}) %reduce-scatter.19.cloned.1.call-update) | async-done | bytes 524304 | tf_op jit(solution)/shard_map/reduce_scatter | solution.py:636
  1555.6 44.6 %reduce-scatter.15.cloned.1.call-done = bf16[2,128,2048]{2,1,0:T(8,128)(2,1)} async-done(((bf16[2,512,2048]{2,1,0:T(8,128)(2,1)}), bf16[2,128,2048]{2,1,0:T(8,128)(2,1)}) %reduce-scatter.15.cloned.1.call-update) | async-done | bytes 1048592 | tf_op jit(solution)/shard_map/reduce_scatter | solution.py:596
  1602.2 33.3 %all_gather.51 = f32[8,100,128]{2,1,0:T(8,128)} all-gather(f32[1,100,128]{2,1,0:T(8,128)S(1)} %bitcast.142), channel_id=1, replica_groups=mesh['dp'=8,'head'=4] {'dp'}, dimensions={0}, use_global_device_ids=true | all-gather | bytes 460800 | tf_op jit(solution)/shard_map/all_gather | solution.py:815
  1656.3 210.5 %reduce-scatter.17.cloned.1.call-done = bf16[256,3200]{1,0:T(8,128)(2,1)} async-done(((bf16[2048,3200]{1,0:T(8,128)(2,1)}), bf16[256,3200]{1,0:T(8,128)(2,1)}) %reduce-scatter.17.cloned.1.call-update) | async-done | bytes 1638416 | tf_op jit(solution)/shard_map/reduce_scatter | solution.py:636
  (242 shorter events, 146.6 us)
Async XLA Ops:
  7.3 42.2 %all-gather.13.cloned.1.call-start = ((), (), s32[]{:S(2)}) async-start(), calls=%async_computation.8 | async-start | bytes 5242880 | tf_op jit(solution)/shard_map/all_gather | solution.py:592
  12.1 223.0 %all-gather.15.cloned.1.call-start = ((), (), s32[]{:S(2)}) async-start(), calls=%async_computation.9 | async-start | bytes 14745600 | tf_op jit(solution)/shard_map/all_gather | solution.py:632
  14.5 376.7 %all-gather.17.cloned.1.call-start = ((), (), s32[]{:S(2)}) async-start(), calls=%async_computation.10 | async-start | bytes 7077888 | tf_op jit(solution)/shard_map/all_gather | solution.py:601
  248.6 5.0 collective-permute-start
  290.6 175.7 %all-gather.19.cloned.1.call-start = ((), (), s32[]{:S(2)}) async-start(), calls=%async_computation.11 | async-start | bytes 4718592 | tf_op jit(solution)/shard_map/all_gather | solution.py:632
  291.2 254.1 %reduce-scatter.9.cloned.1.call-start = ((), (), s32[]{:S(2)}) async-start(), calls=%async_computation.12 | async-start | bytes 10485760 | tf_op jit(solution)/shard_map/reduce_scatter | solution.py:596
  314.5 82.2 %copy-start.17 = (bf16[2,512,4,128]{1,3,2,0:T(8,128)(2,1)}, bf16[2,512,4,128]{1,3,2,0:T(8,128)(2,1)S(1)}, u32[]{:S(2)}) copy-start(bf16[2,512,4,128]{1,3,2,0:T(8,128)(2,1)S(1)} %copy.94) | copy-start | bytes 3145732
  475.2 106.1 %all-gather.27.cloned.1.call-start = ((), (), s32[]{:S(2)}) async-start(), calls=%async_computation.17 | async-start | bytes 5242880 | tf_op jit(solution)/shard_map/all_gather | solution.py:592
  475.8 201.4 %all-gather.25.cloned.1.call-start = ((), (), s32[]{:S(2)}) async-start(), calls=%async_computation.15 | async-start | bytes 6488064 | tf_op jit(solution)/shard_map/all_gather | solution.py:632
  476.5 71.0 %copy-start.32 = (f32[2048]{0:T(1024)S(1)}, f32[2048]{0:T(1024)}, u32[]{:S(2)}) copy-start(f32[2048]{0:T(1024)} %param.38) | copy-start | bytes 24580
  476.6 365.5 %all-gather.23.cloned.1.call-start = ((), (), s32[]{:S(2)}) async-start(), calls=%async_computation.14 | async-start | bytes 12976128 | tf_op jit(solution)/shard_map/all_gather | solution.py:632
  477.8 399.1 %all-gather.21.cloned.1.call-start = ((), (), s32[]{:S(2)}) async-start(), calls=%async_computation.13 | async-start | bytes 5242880 | tf_op jit(solution)/shard_map/all_gather | solution.py:592
  547.5 449.8 %copy-start.8 = (f32[2,128,2048]{2,1,0:T(8,128)}, f32[2,128,2048]{2,1,0:T(8,128)S(1)}, u32[]{:S(2)}) copy-start(f32[2,128,2048]{2,1,0:T(8,128)S(1)} %get-tuple-element.111) | copy-start | bytes 6291460
  548.9 445.4 %reduce-scatter.13.cloned.1.call-start = ((), (), s32[]{:S(2)}) async-start(), calls=%async_computation.18 | async-start | bytes 10485760 | tf_op jit(solution)/shard_map/reduce_scatter | solution.py:596
  922.5 111.2 %all-gather.29.cloned.1.call-start = ((), (), s32[]{:S(2)}) async-start(), calls=%async_computation.19 | async-start | bytes 5242880 | tf_op jit(solution)/shard_map/all_gather | solution.py:592
  999.1 152.4 %all-gather.31.cloned.1.call-start = ((), (), s32[]{:S(2)}) async-start(), calls=%async_computation.20 | async-start | bytes 7077888 | tf_op jit(solution)/shard_map/all_gather | solution.py:601
  1052.2 214.2 %reduce-scatter.23.cloned.1.call-start = ((), (), s32[]{:S(2)}) async-start(), calls=%async_computation.25 | async-start | bytes 6488064 | tf_op jit(solution)/shard_map/reduce_scatter | solution.py:636
  1062.9 399.6 %reduce-scatter.21.cloned.1.call-start = ((), (), s32[]{:S(2)}) async-start(), calls=%async_computation.24 | async-start | bytes 12976128 | tf_op jit(solution)/shard_map/reduce_scatter | solution.py:636
  1081.5 471.9 %reduce-scatter.19.cloned.1.call-start = ((), (), s32[]{:S(2)}) async-start(), calls=%async_computation.23 | async-start | bytes 4718592 | tf_op jit(solution)/shard_map/reduce_scatter | solution.py:636
  1093.1 507.1 %reduce-scatter.15.cloned.1.call-start = ((), (), s32[]{:S(2)}) async-start(), calls=%async_computation.21 | async-start | bytes 5242880 | tf_op jit(solution)/shard_map/reduce_scatter | solution.py:596
  1202.7 9.8 collective-permute-start.1
  1233.2 417.6 %reduce-scatter.11.cloned.1.call-start = ((), (), s32[]{:S(2)}) async-start(), calls=%async_computation.16 | async-start | bytes 5242880 | tf_op jit(solution)/shard_map/reduce_scatter | solution.py:596
  1244.2 622.6 %reduce-scatter.17.cloned.1.call-start = ((), (), s32[]{:S(2)}) async-start(), calls=%async_computation.22 | async-start | bytes 14745600 | tf_op jit(solution)/shard_map/reduce_scatter | solution.py:636
  1268.8 286.7 %copy-start.44 = (f32[256]{0:T(256)S(1)}, f32[256]{0:T(256)}, u32[]{:S(2)}) copy-start(f32[256]{0:T(256)} %get-tuple-element.102) | copy-start | bytes 3076
  1268.8 331.4 %copy-start.12 = (bf16[2,128,2048]{2,1,0:T(8,128)(2,1)S(1)}, bf16[2,128,2048]{2,1,0:T(8,128)(2,1)}, u32[]{:S(2)}) copy-start(bf16[2,128,2048]{2,1,0:T(8,128)(2,1)} %param.21) | copy-start | bytes 3145732
  1268.8 331.4 %copy-start.34 = (f32[2048]{0:T(1024)S(1)}, f32[2048]{0:T(1024)}, u32[]{:S(2)}) copy-start(f32[2048]{0:T(1024)} %param.24) | copy-start | bytes 24580
  1268.8 331.4 %copy-start.37 = (f32[2,128]{1,0:T(2,128)S(1)}, f32[2,128]{1,0:T(2,128)}, u32[]{:S(2)}) copy-start(f32[2,128]{1,0:T(2,128)} %copy-done.36) | copy-start | bytes 3076
  1268.8 333.4 %copy-start.35 = (f32[2048]{0:T(1024)S(1)}, f32[2048]{0:T(1024)}, u32[]{:S(2)}) copy-start(f32[2048]{0:T(1024)} %get-tuple-element.104) | copy-start | bytes 24580
  1465.6 185.2 %copy-start.9 = (f32[2,128,2048]{2,1,0:T(8,128)S(1)}, f32[2,128,2048]{2,1,0:T(8,128)}, u32[]{:S(2)}) copy-start(f32[2,128,2048]{2,1,0:T(8,128)} %copy-done.8) | copy-start | bytes 6291460
  1465.6 185.2 %copy-start.33 = (f32[2048]{0:T(1024)S(1)}, f32[2048]{0:T(1024)}, u32[]{:S(2)}) copy-start(f32[2048]{0:T(1024)} %param.38) | copy-start | bytes 24580
  1465.6 185.2 %copy-start.39 = (f32[2,128]{1,0:T(2,128)S(1)}, f32[2,128]{1,0:T(2,128)}, u32[]{:S(2)}) copy-start(f32[2,128]{1,0:T(2,128)} %copy-done.38) | copy-start | bytes 3076
  1650.8 222.1 %copy-start.1 = (f32[4,4096]{1,0:T(4,128)S(1)}, f32[4,4096]{1,0:T(4,128)}, u32[]{:S(2)}) copy-start(f32[4,4096]{1,0:T(4,128)} %param.33) | copy-start | bytes 196612
  (39 other events, 316.5 us)
Sparse Core Ops, SparseCore 0:
  12.2 37.1 all-gather.12
  52.2 182.8 all-gather.14
  290.7 100.3 all-gather.16
  393.0 73.1 all-gather.18
  475.3 69.8 reduce-scatter.8
  546.8 34.4 all-gather.26
  583.5 93.5 all-gather.24
  680.2 161.8 all-gather.22
  844.2 32.6 all-gather.20
  922.6 71.6 reduce-scatter.12
  999.2 34.4 all-gather.28
  1052.4 99.0 all-gather.30
  1155.1 111.3 reduce-scatter.22
  1269.9 192.5 reduce-scatter.20
  1466.0 87.3 reduce-scatter.18
  1555.9 44.2 reduce-scatter.14
  1602.6 45.6 reduce-scatter.10
  1652.2 214.5 reduce-scatter.16

commit v2 on v1

--- a/solution.py
+++ b/solution.py
@@ -455,131 +455,241 @@
         rim_grad_ref[0] = carry[...]
 
 
-def mix_sizes(pre_conv, micros, heads, key_size):
-    rows = pre_conv.shape[0] // micros
-    value_size = pre_conv.shape[1] // heads - 2 * key_size
-    return rows, rows // CHUNK, value_size
-
-
-def mix_forward(info, pre_conv, rim, dec, taps, par, micros, heads, key_size):
-    rows, chunks, value_size = mix_sizes(pre_conv, micros, heads, key_size)
-    width = pre_conv.shape[1]
-    wide = value_size + key_size
-
-    def by_rows(columns):
-        return pl.BlockSpec((CHUNK, columns), lambda m, c: (m * chunks + c, 0))
-
-    kernel = partial(
-        mix_forward_kernel,
-        heads=heads,
-        key_size=key_size,
-        value_size=value_size,
-        seq_count=info.shape[1] - 1,
-    )
+def gate_forward_kernel(
+    info_ref, plain_ref, cmap_ref, incoming_ref, gate_ref, gain_ref, mixed_ref, gated_ref, *, heads, key_size, value_size
+):
+    for head in range(heads):
+        cut = slice(head * value_size, (head + 1) * value_size)
+        mixed = plain_ref[:, cut] + mm(
+            cmap_ref[:, head * key_size : (head + 1) * key_size], incoming_ref[0, head]
+        )
+        mixed_ref[:, cut] = mixed
+        normed = mixed * lax.rsqrt(
+            jnp.mean(mixed * mixed, axis=1, keepdims=True) + HEAD_FLOOR
+        )
+        gate = gate_ref[:, cut]
+        gated_ref[:, cut] = (normed * gain_ref[0:1, :] * gate * jax.nn.sigmoid(gate)).astype(BF16)
+
+
+def gate_backward_kernel(
+    info_ref,
+    grad_ref,
+    mixed_ref,
+    cmap_ref,
+    gate_ref,
+    gain_ref,
+    dgate_ref,
+    dmixed_ref,
+    dlocal_ref,
+    dgain_ref,
+    *,
+    heads,
+    key_size,
+    value_size,
+):
+    micro, step = pl.program_id(0), pl.program_id(1)
+
+    @pl.when(step == 0)
+    def _():
+        dlocal_ref[...] = jnp.zeros_like(dlocal_ref)
+
+    @pl.when(jnp.logical_and(micro == 0, step == 0))
+    def _():
+        dgain_ref[...] = jnp.zeros_like(dgain_ref)
+
+    gain = gain_ref[0:1, :]
+    for head in range(heads):
+        cut = slice(head * value_size, (head + 1) * value_size)
+        mixed = mixed_ref[:, cut]
+        scale = lax.rsqrt(jnp.mean(mixed * mixed, axis=1, keepdims=True) + HEAD_FLOOR)
+        normed = mixed * scale
+        gate = gate_ref[:, cut]
+        sig = jax.nn.sigmoid(gate)
+        active = gate * sig
+        grad = grad_ref[:, cut]
+        by_norm = grad * normed
+        dgain_ref[0:1, :] += jnp.sum(by_norm * active, axis=0, keepdims=True)
+        dgate_ref[:, cut] = (by_norm * gain * sig * (1.0 + gate * (1.0 - sig))).astype(BF16)
+        dnormed = grad * gain * active
+        dmixed = scale * (dnormed - normed * jnp.mean(dnormed * normed, axis=1, keepdims=True))
+        dmixed_ref[:, cut] = dmixed
+        dlocal_ref[0, head] += mm(
+            cmap_ref[:, head * key_size : (head + 1) * key_size], dmixed, TN
+        )
+
+
+VMEM_BYTES = 48 * 1024 * 1024
+
+
+def kernel_call(kernel, info, arrays, grid, in_specs, out_specs, out_shape, scratch, name, **sizes):
     return pl.pallas_call(
-        kernel,
-        grid=(micros, chunks),
-        in_specs=[
-            pl.BlockSpec(memory_space=pltpu.SMEM),
-            by_rows(width),
-            pl.BlockSpec((1, HALO, width), lambda m, c: (m, 0, 0)),
-            by_rows(LANES),
-            pl.BlockSpec((8, width), lambda m, c: (0, 0)),
-            pl.BlockSpec((8, LANES), lambda m, c: (0, 0)),
-        ],
-        out_specs=[
-            by_rows(heads * value_size),
-            by_rows(heads * key_size),
-            pl.BlockSpec((1, heads, CHUNK, CHUNK), lambda m, c: (m * chunks + c, 0, 0, 0)),
-            pl.BlockSpec((1, heads, key_size, wide), lambda m, c: (m * chunks + c, 0, 0, 0)),
-            pl.BlockSpec((1, heads, key_size, wide), lambda m, c: (m, 0, 0, 0)),
-        ],
-        out_shape=[
-            jax.ShapeDtypeStruct((micros * rows, heads * value_size), F32),
-            jax.ShapeDtypeStruct((micros * rows, heads * key_size), BF16),
-            jax.ShapeDtypeStruct((micros * chunks, heads, CHUNK, CHUNK), BF16),
-            jax.ShapeDtypeStruct((micros * chunks, heads, key_size, wide), BF16),
-            jax.ShapeDtypeStruct((micros, heads, key_size, wide), F32),
-        ],
-        scratch_shapes=[
-            pltpu.VMEM((HALO, width), BF16),
-            pltpu.VMEM((heads, key_size, wide), F32),
-        ],
+        partial(kernel, **sizes),
+        grid_spec=pltpu.PrefetchScalarGridSpec(
+            num_scalar_prefetch=1,
+            grid=grid,
+            in_specs=in_specs,
+            out_specs=out_specs,
+            scratch_shapes=scratch,
+        ),
+        out_shape=out_shape,
         compiler_params=pltpu.CompilerParams(
-            dimension_semantics=("arbitrary", "arbitrary"), vmem_limit_bytes=VMEM_BYTES
+            dimension_semantics=("arbitrary",) * len(grid), vmem_limit_bytes=VMEM_BYTES
         ),
-        name="mix_forward",
-    )(info, pre_conv, rim, dec, taps, par)
-
-
-def mix_backward(
-    info, pre_conv, rim, dec, taps, par, grad, inverses, starts, incoming, leaving, micros, heads, key_size
-):
-    rows, chunks, value_size = mix_sizes(pre_conv, micros, heads, key_size)
-    width = pre_conv.shape[1]
-    wide = value_size + key_size
-    halo_blocks = CHUNK // HALO
-
-    def at(m, s):
-        return m * chunks + chunks - 1 - s
-
-    def by_rows(columns):
-        return pl.BlockSpec((CHUNK, columns), lambda m, s: (at(m, s), 0))
-
-    kernel = partial(
-        mix_backward_kernel,
-        heads=heads,
-        key_size=key_size,
-        value_size=value_size,
-        seq_count=info.shape[1] - 1,
-    )
-    return pl.pallas_call(
-        kernel,
-        grid=(micros, chunks),
-        in_specs=[
-            pl.BlockSpec(memory_space=pltpu.SMEM),
-            by_rows(width),
-            pl.BlockSpec(
-                (HALO, width), lambda m, s: (jnp.maximum(at(m, s) * halo_blocks - 1, 0), 0)
-            ),
-            pl.BlockSpec((1, HALO, width), lambda m, s: (m, 0, 0)),
-            by_rows(LANES),
-            pl.BlockSpec((8, width), lambda m, s: (0, 0)),
-            pl.BlockSpec((8, LANES), lambda m, s: (0, 0)),
-            by_rows(heads * value_size),
-            pl.BlockSpec((1, heads, CHUNK, CHUNK), lambda m, s: (at(m, s), 0, 0, 0)),
-            pl.BlockSpec((1, heads, key_size, wide), lambda m, s: (at(m, s), 0, 0, 0)),
-            pl.BlockSpec((1, heads, key_size, value_size), lambda m, s: (m, 0, 0, 0)),
-            pl.BlockSpec((1, heads, key_size, value_size), lambda m, s: (m, 0, 0, 0)),
-        ],
-        out_specs=[
-            by_rows(width),
-            pl.BlockSpec((1, 8, width), lambda m, s: (m, 0, 0)),
-            pl.BlockSpec((1, HALO, width), lambda m, s: (m, 0, 0)),
-            by_rows(LANES),
-            pl.BlockSpec((8, width), lambda m, s: (0, 0)),
-            pl.BlockSpec((8, LANES), lambda m, s: (0, 0)),
-        ],
-        out_shape=[
-            jax.ShapeDtypeStruct((micros * rows, width), BF16),
-            jax.ShapeDtypeStruct((micros, 8, width), F32),
-            jax.ShapeDtypeStruct((micros, HALO, width), F32),
-            jax.ShapeDtypeStruct((micros * rows, LANES), BF16),
-            jax.ShapeDtypeStruct((8, width), F32),
-            jax.ShapeDtypeStruct((8, LANES), F32),
-        ],
-        scratch_shapes=[
-            pltpu.VMEM((8, width), F32),
-            pltpu.VMEM((heads, key_size, value_size), F32),
-        ],
-        compiler_params=pltpu.CompilerParams(
-            dimension_semantics=("arbitrary", "arbitrary"), vmem_limit_bytes=VMEM_BYTES
-        ),
-        name="mix_backward",
-    )(info, pre_conv, pre_conv, rim, dec, taps, par, grad, inverses, starts, incoming, leaving)
-
-
-VMEM_BYTES = 48 * 1024 * 1024
+        name=name,
+    )(info, *arrays)
+
+
+class Mix:
+    def __init__(self, info, micros, chunks, heads, key_size, value_size):
+        self.info, self.micros, self.chunks = info, micros, chunks
+        self.heads, self.key_size, self.value_size = heads, key_size, value_size
+        self.width = heads * (2 * key_size + value_size)
+        self.wide = key_size + value_size
+        self.rows = micros * chunks * CHUNK
+        self.sizes = dict(heads=heads, key_size=key_size, value_size=value_size)
+
+    def block(self, m, c, info):
+        return m * self.chunks + jnp.bitwise_xor(c, info[0, info.shape[1] - 1])
+
+    def by_rows(self, columns, turned=False):
+        def place(m, c, info):
+            return self.block(m, self.chunks - 1 - c if turned else c, info), 0
+
+        return pl.BlockSpec((CHUNK, columns), place)
+
+    def by_chunk(self, rows, columns, turned=False):
+        def place(m, c, info):
+            return m * self.chunks + (self.chunks - 1 - c if turned else c), 0, 0, 0
+
+        return pl.BlockSpec((1, self.heads, rows, columns), place)
+
+    def by_micro(self, *dims):
+        return pl.BlockSpec((1,) + dims, lambda m, c, info: (m,) + (0,) * len(dims))
+
+    def whole(self, *dims):
+        return pl.BlockSpec(dims, lambda m, c, info: (0,) * len(dims))
+
+    def like(self, dtype, *dims):
+        return jax.ShapeDtypeStruct(dims, dtype)
+
+    def call(self, kernel, arrays, in_specs, outs, scratch, name, **more):
+        return kernel_call(
+            kernel,
+            self.info,
+            arrays,
+            (self.micros, self.chunks),
+            in_specs,
+            [spec for spec, _ in outs],
+            [shape for _, shape in outs],
+            scratch,
+            name,
+            **self.sizes,
+            **more,
+        )
+
+    def forward(self, pre_conv, rim, dec, taps, par):
+        h, dk, dv, wide, width = self.heads, self.key_size, self.value_size, self.wide, self.width
+        steps = self.micros * self.chunks
+        return self.call(
+            mix_forward_kernel,
+            (pre_conv, rim, dec, taps, par),
+            [
+                self.by_rows(width),
+                self.by_micro(HALO, width),
+                self.by_rows(LANES),
+                self.whole(8, width),
+                self.whole(8, LANES),
+            ],
+            [
+                (self.by_rows(h * dv), self.like(F32, self.rows, h * dv)),
+                (self.by_rows(h * dk), self.like(BF16, self.rows, h * dk)),
+                (self.by_chunk(CHUNK, CHUNK), self.like(BF16, steps, h, CHUNK, CHUNK)),
+                (self.by_chunk(dk, wide), self.like(BF16, steps, h, dk, wide)),
+                (self.by_micro(h, dk, wide), self.like(F32, self.micros, h, dk, wide)),
+            ],
+            [pltpu.VMEM((HALO, width), BF16), pltpu.VMEM((h, dk, wide), F32)],
+            "mix_forward",
+            seq_count=self.info.shape[1] - 2,
+        )
+
+    def backward(self, pre_conv, rim, dec, taps, par, grad, inverses, starts, incoming, leaving):
+        h, dk, dv, wide, width = self.heads, self.key_size, self.value_size, self.wide, self.width
+        halo_blocks = CHUNK // HALO
+
+        def before(m, c, info):
+            earlier = jnp.maximum(self.chunks - 2 - c, 0)
+            return (self.block(m, earlier, info) + 1) * halo_blocks - 1, 0
+
+        return self.call(
+            mix_backward_kernel,
+            (pre_conv, pre_conv, rim, dec, taps, par, grad, inverses, starts, incoming, leaving),
+            [
+                self.by_rows(width, True),
+                pl.BlockSpec((HALO, width), before),
+                self.by_micro(HALO, width),
+                self.by_rows(LANES, True),
+                self.whole(8, width),
+                self.whole(8, LANES),
+                self.by_rows(h * dv, True),
+                self.by_chunk(CHUNK, CHUNK, True),
+                self.by_chunk(dk, wide, True),
+                self.by_micro(h, dk, dv),
+                self.by_micro(h, dk, dv),
+            ],
+            [
+                (self.by_rows(width, True), self.like(BF16, self.rows, width)),
+                (self.by_micro(8, width), self.like(F32, self.micros, 8, width)),
+                (self.by_micro(HALO, width), self.like(F32, self.micros, HALO, width)),
+                (self.by_rows(LANES, True), self.like(BF16, self.rows, LANES)),
+                (self.whole(8, width), self.like(F32, 8, width)),
+                (self.whole(8, LANES), self.like(F32, 8, LANES)),
+            ],
+            [pltpu.VMEM((8, width), F32), pltpu.VMEM((h, dk, dv), F32)],
+            "mix_backward",
+            seq_count=self.info.shape[1] - 2,
+        )
+
+    def gate_forward(self, plain, cmap, incoming, gate, gain):
+        h, dk, dv = self.heads, self.key_size, self.value_size
+        return self.call(
+            gate_forward_kernel,
+            (plain, cmap, incoming, gate, gain),
+            [
+                self.by_rows(h * dv),
+                self.by_rows(h * dk),
+                self.by_micro(h, dk, dv),
+                self.by_rows(h * dv),
+                self.whole(8, dv),
+            ],
+            [
+                (self.by_rows(h * dv), self.like(F32, self.rows, h * dv)),
+                (self.by_rows(h * dv), self.like(BF16, self.rows, h * dv)),
+            ],
+            [],
+            "gate_forward",
+        )
+
+    def gate_backward(self, grad, mixed, cmap, gate, gain):
+        h, dk, dv = self.heads, self.key_size, self.value_size
+        return self.call(
+            gate_backward_kernel,
+            (grad, mixed, cmap, gate, gain),
+            [
+                self.by_rows(h * dv),
+                self.by_rows(h * dv),
+                self.by_rows(h * dk),
+                self.by_rows(h * dv),
+                self.whole(8, dv),
+            ],
+            [
+                (self.by_rows(h * dv), self.like(BF16, self.rows, h * dv)),
+                (self.by_rows(h * dv), self.like(F32, self.rows, h * dv)),
+                (self.by_micro(h, dk, dv), self.like(F32, self.micros, h, dk, dv)),
+                (self.whole(8, dv), self.like(F32, 8, dv)),
+            ],
+            [],
+            "gate_backward",
+        )
 
 
 def from_behind(value, axis, steps):
@@ -588,32 +698,162 @@
     return lax.ppermute(value, axis, [(source, source + steps) for source in range(leading, last)])
 
 
+def swap(value, axis, bit):
+    return lax.ppermute(value, axis, [(at, at ^ bit) for at in range(lax.axis_size(axis))])
+
+
 def head_gather(value):
-    return lax.all_gather(value, "head", axis=1, tiled=True)
-
-
-def head_scatter(value):
-    return lax.psum_scatter(value, "head", scatter_dimension=1, tiled=True)
-
-
-def scan_states(maps, sums, backward):
+    across = swap(value, "head", 2)
+    both = swap(jnp.stack([value, across], axis=1), "head", 1)
+    return jnp.stack([value, both[:, 0], across, both[:, 1]], axis=1)
+
+
+def head_scatter(parts):
+    near = swap(jnp.stack([parts[:, 1], parts[:, 3]], axis=1).astype(BF16), "head", 1)
+    mine = parts[:, 0].astype(F32) + near[:, 0].astype(F32)
+    theirs = parts[:, 2].astype(F32) + near[:, 1].astype(F32)
+    return mine + swap(theirs.astype(BF16), "head", 2).astype(F32)
+
+
+def ring_order():
+    count = lax.axis_size("dp")
+    return list(range(0, count, 2)) + list(range(count - 1, 0, -2))
+
+
+def ring_place():
     count, mine = lax.axis_size("dp"), lax.axis_index("dp")
-    packed = lax.all_gather(jnp.concatenate([maps, sums], axis=-1).astype(BF16), "dp")
-    if backward:
-        packed = packed[::-1]
-        mine = count - 1 - mine
-    key_size = maps.shape[-1]
-    state = jnp.zeros(sums.shape, F32)
-    for position in range(count - 1):
-        block = packed[position]
-        moved = jnp.einsum(
-            "mhji,mhjv->mhiv" if backward else "mhij,mhjv->mhiv",
-            block[..., :key_size],
-            state.astype(BF16),
-            preferred_element_type=F32,
-        )
-        state = jnp.where(position < mine, moved + block[..., key_size:].astype(F32), state)
-    return state
+    return jnp.where(mine % 2 == 0, mine // 2, count - 1 - mine // 2)
+
+
+def ring_steps():
+    ring = ring_order()
+    ahead = [(ring[at], ring[(at + 1) % len(ring)]) for at in range(len(ring))]
+    return ahead, [(after, before) for before, after in ahead]
+
+
+def to_ring(value):
+    ring = ring_order()
+    size = value.shape[-1] // len(ring)
+    parts = [value[..., rank * size : (rank + 1) * size] for rank in ring]
+    twice = jnp.concatenate(parts + parts[:-1], axis=-1)
+    return lax.dynamic_slice_in_dim(twice, ring_place() * size, value.shape[-1], value.ndim - 1)
+
+
+def from_ring(value):
+    ring = ring_order()
+    count = len(ring)
+    size = value.shape[-1] // count
+    start = jnp.where(ring_place() == 0, 0, count - ring_place())
+    turned = lax.dynamic_slice_in_dim(
+        jnp.concatenate([value, value[..., : (count - 1) * size]], axis=-1),
+        start * size,
+        value.shape[-1],
+        value.ndim - 1,
+    )
+    parts = [None] * count
+    for at, rank in enumerate(ring):
+        parts[rank] = turned[..., at * size : (at + 1) * size]
+    return jnp.concatenate(parts, axis=-1)
+
+
+def ring_gather(shard, axis):
+    ahead, back = ring_steps()
+    count = len(ahead)
+    from_left, from_right = [shard], [shard]
+    for _ in range(1, count // 2):
+        from_left.append(lax.ppermute(from_left[-1], "dp", ahead))
+        from_right.append(lax.ppermute(from_right[-1], "dp", back))
+    half = shard.shape[0] // 2
+    far = jnp.concatenate(
+        [
+            lax.ppermute(from_left[-1][:half], "dp", ahead),
+            lax.ppermute(from_right[-1][half:], "dp", back),
+        ],
+        axis=0,
+    )
+    return jnp.concatenate(from_right + [far] + from_left[:0:-1], axis=axis), far
+
+
+def ring_scatter(blocks):
+    ahead, back = ring_steps()
+    count = len(ahead)
+    half = blocks[0].shape[0] // 2
+    middle = count // 2
+
+    def add(one, other):
+        return one.astype(F32) + other.astype(F32)
+
+    left = lax.ppermute(blocks[middle][:half], "dp", ahead)
+    right = lax.ppermute(blocks[middle][half:], "dp", back)
+    for at in range(middle - 1, 0, -1):
+        up, down = blocks[at], blocks[count - at]
+        if at == middle - 1:
+            up = jnp.concatenate([add(up[:half], left).astype(BF16), up[half:]], axis=0)
+            down = jnp.concatenate([down[:half], add(down[half:], right).astype(BF16)], axis=0)
+        else:
+            up, down = add(up, left).astype(BF16), add(down, right).astype(BF16)
+        left = lax.ppermute(up, "dp", ahead)
+        right = lax.ppermute(down, "dp", back)
+    return add(blocks[0], left) + right.astype(F32)
+
+
+def scatter_rows(grad):
+    size = grad.shape[0] // lax.axis_size("dp")
+    return ring_scatter([grad[at : at + size] for at in range(0, grad.shape[0], size)])
+
+
+def scatter_columns(grad):
+    size = grad.shape[1] // lax.axis_size("dp")
+    return ring_scatter([grad[:, at : at + size] for at in range(0, grad.shape[1], size)])
+
+
+def apply_map(moves, state, turned=False):
+    return jnp.einsum(
+        "hji,hjv->hiv" if turned else "hij,hjv->hiv",
+        moves.astype(BF16),
+        state.astype(BF16),
+        preferred_element_type=F32,
+    )
+
+
+def own_and_swapped(value, bit):
+    theirs = swap(jnp.where(bit == 0, value[1], value[0]).astype(BF16), "dp", 1)
+    mine = jnp.where(bit == 0, value[0], value[1]).astype(F32)
+    theirs = theirs.astype(F32)
+    return jnp.where(bit == 0, mine, theirs), jnp.where(bit == 0, theirs, mine)
+
+
+def hand_back(first, second, bit):
+    mine = jnp.where(bit == 0, first, second).astype(BF16)
+    theirs = swap(jnp.where(bit == 0, second, first).astype(BF16), "dp", 1)
+    return jnp.stack([jnp.where(bit == 0, mine, theirs), jnp.where(bit == 0, theirs, mine)])
+
+
+def scan_forward(final, value_size):
+    bit, pairs = lax.axis_index("dp") % 2, lax.axis_size("dp") // 2
+    first, second = own_and_swapped(final, bit)
+    first_map, second_map = first[..., value_size:], second[..., value_size:]
+    pair_map = apply_map(second_map, first_map)
+    pair_sum = apply_map(second_map, first[..., :value_size]) + second[..., :value_size]
+    state = jnp.zeros(pair_sum.shape, F32)
+    for _ in range(pairs - 1):
+        state = from_behind((apply_map(pair_map, state) + pair_sum).astype(BF16), "dp", 2).astype(F32)
+    after_first = apply_map(first_map, state) + first[..., :value_size]
+    return hand_back(state, after_first, bit), (first_map, second_map, pair_map)
+
+
+def scan_backward(local, maps):
+    bit, pairs = lax.axis_index("dp") % 2, lax.axis_size("dp") // 2
+    first_map, second_map, pair_map = maps
+    first, second = own_and_swapped(local, bit)
+    pair_sum = apply_map(first_map, second, True) + first
+    state = jnp.zeros(pair_sum.shape, F32)
+    for _ in range(pairs - 1):
+        state = from_behind(
+            (apply_map(pair_map, state, True) + pair_sum).astype(BF16), "dp", -2
+        ).astype(F32)
+    before_second = apply_map(second_map, state, True) + second
+    return hand_back(before_second, state, bit)
 
 
 def contract_rows(left, right):
@@ -626,14 +866,6 @@
 
 def norm_backward(grad_in, normed_rows, scale):
     return scale * (grad_in - normed_rows * jnp.mean(grad_in * normed_rows, axis=-1, keepdims=True))
-
-
-def dp_gather(value, axis):
-    return lax.all_gather(value, "dp", axis=axis, tiled=True)
-
-
-def dp_scatter(value, axis):
-    return lax.psum_scatter(value.astype(BF16), "dp", scatter_dimension=axis, tiled=True).astype(F32)
 
 
 def body(
@@ -659,7 +891,7 @@
     ffn_up,
     ffn_down,
 ):
-    head_rank = lax.axis_index("head")
+    head_rank, ranks = lax.axis_index("head"), lax.axis_size("head")
     heads = decay_proj.shape[1]
     qk_width = query_proj.shape[1]
     v_width = value_proj.shape[1]
@@ -667,20 +899,29 @@
     value_size = v_width // heads
     ffn_width = ffn_gate.shape[1]
     conv_width = 2 * qk_width + v_width
-    main_width = conv_width + v_width
-    micros = tokens.shape[0]
-    model = tokens.shape[2]
+    micros, part_rows, model = tokens.shape
+    assert part_rows == CHUNK and micros == 2 and ranks == 4
 
     decay_pad = jnp.zeros((decay_proj.shape[0], LANES - 2 * heads), decay_proj.dtype)
-    w_in = dp_gather(
+    w_conv, sent = ring_gather(
         jnp.concatenate(
-            [query_proj, key_proj, value_proj, gate_proj, decay_proj, beta_proj, decay_pad], axis=1
+            [query_proj, key_proj, value_proj, decay_proj, beta_proj, decay_pad], axis=1
         ),
         0,
     )
-    w_out = dp_gather(out_proj, 1)
-    w_ffn = dp_gather(jnp.concatenate([ffn_gate, ffn_up], axis=1), 0)
-    w_down = dp_gather(ffn_down, 1)
+    gate_shard, out_shard, _ = lax.optimization_barrier((gate_proj, out_proj, sent[:8, :LANES]))
+    w_gate, sent = ring_gather(gate_shard, 0)
+    w_out, also_sent = ring_gather(out_shard, 1)
+    ffn_shard, down_shard, _, _ = lax.optimization_barrier(
+        (
+            jnp.concatenate([ffn_gate, ffn_up], axis=1),
+            ffn_down,
+            sent[:8, :LANES],
+            also_sent[:8, :LANES],
+        )
+    )
+    w_ffn, _ = ring_gather(ffn_shard, 0)
+    w_down, _ = ring_gather(down_shard, 1)
 
     def of_mine(whole, width):
         return lax.dynamic_slice_in_dim(whole, head_rank * width, width, whole.ndim - 1)
@@ -694,144 +935,131 @@
         jnp.stack([-jnp.exp(of_mine(log_rate, heads)), of_mine(step_bias, heads)]),
         ((0, 6), (0, LANES - heads)),
     )
-
-    residual = tokens.astype(F32)
+    gain = jnp.broadcast_to(head_norm, (8, value_size))
+    attn_gain, ffn_gain = to_ring(attn_norm), to_ring(ffn_norm)
+
+    def flat(value):
+        return value.reshape(-1, value.shape[-1])
+
+    def ranked(value):
+        return value.reshape(micros, ranks, part_rows, model)
+
+    residual = to_ring(tokens).astype(F32)
     scale_one = lax.rsqrt(jnp.mean(residual * residual, axis=-1, keepdims=True) + EPSILON)
     normed_one = residual * scale_one
-    normed_all = head_gather((normed_one * attn_norm).astype(BF16))
-    cotangent_all = head_gather(out_grad)
-    block_rows = normed_all.shape[1]
-    normed_all = normed_all.reshape(micros * block_rows, model)
-    cotangent_all = cotangent_all.reshape(micros * block_rows, model)
-    first_row = lax.axis_index("dp") * block_rows
+    normed_all = flat(head_gather((normed_one * attn_gain).astype(BF16)))
+    cotangent = to_ring(out_grad)
+    cotangent_all = flat(head_gather(cotangent))
+    first_row = lax.axis_index("dp") * ranks * part_rows
     ends = jnp.cumsum(seq_lengths, axis=1)
     info = jnp.concatenate(
-        [ends - seq_lengths, jnp.full((micros, 1), first_row, jnp.int32)], axis=1
+        [
+            ends - seq_lengths,
+            jnp.full((micros, 1), first_row, jnp.int32),
+            jnp.full((micros, 1), head_rank, jnp.int32),
+        ],
+        axis=1,
     ).astype(jnp.int32)
-    pre_conv = jnp.dot(normed_all, w_in[:, :conv_width], preferred_element_type=F32).astype(BF16)
-    gate_lin = jnp.dot(normed_all, w_in[:, conv_width:main_width], preferred_element_type=F32)
-    dec = jnp.dot(normed_all, w_in[:, main_width:], preferred_element_type=F32)
-    last_rows = pre_conv.reshape(micros, block_rows, conv_width)[:, block_rows - HALO :]
+    mix = Mix(info, micros, ranks, heads, key_size, value_size)
+    projected = jnp.dot(normed_all, w_conv, preferred_element_type=F32)
+    pre_conv = projected[:, :conv_width].astype(BF16)
+    dec = projected[:, conv_width:]
+    last_chunk = jnp.bitwise_xor(ranks - 1, head_rank)
+    last_rows = lax.dynamic_slice(
+        pre_conv.reshape(micros, ranks, part_rows, conv_width),
+        (0, last_chunk, part_rows - HALO, 0),
+        (micros, 1, HALO, conv_width),
+    )[:, 0]
     rim = from_behind(last_rows, "dp", 1)
 
-    plain, carried_map, inverses, starts, final = mix_forward(
-        info, pre_conv, rim, dec, taps, par, micros, heads, key_size
-    )
-    block_map = final[..., value_size:]
-    incoming = scan_states(block_map, final[..., :value_size], False)
-    head_rows = (micros, block_rows, heads)
-    carried_map = carried_map.reshape(head_rows + (key_size,))
-    mixed = plain.reshape(head_rows + (value_size,)) + jnp.einsum(
-        "mthd,mhdv->mthv", carried_map, incoming.astype(BF16), preferred_element_type=F32
-    )
-    out_scale = lax.rsqrt(jnp.mean(mixed * mixed, axis=-1, keepdims=True) + HEAD_FLOOR)
-    normed_mix = mixed * out_scale
-    gate_lin = gate_lin.reshape(head_rows + (value_size,))
-    gate_sigmoid = jax.nn.sigmoid(gate_lin)
-    gate_active = gate_lin * gate_sigmoid
-    gated = (normed_mix * head_norm * gate_active).astype(BF16).reshape(-1, v_width)
+    plain, carried_map, inverses, starts, final = mix.forward(pre_conv, rim, dec, taps, par)
+    incoming, maps = scan_forward(final, value_size)
+    gate_lin = jnp.dot(normed_all, w_gate, preferred_element_type=F32)
+    mixed, gated = mix.gate_forward(plain, carried_map, incoming, gate_lin, gain)
 
     mix_part = jnp.dot(gated, w_out, preferred_element_type=F32)
-    after_mix = residual + head_scatter(mix_part.reshape(micros, block_rows, model))
+    after_mix = residual + head_scatter(ranked(mix_part))
     scale_two = lax.rsqrt(jnp.mean(after_mix * after_mix, axis=-1, keepdims=True) + EPSILON)
     normed_two = after_mix * scale_two
-    ffn_all = head_gather((normed_two * ffn_norm).astype(BF16)).reshape(-1, model)
+    ffn_all = flat(head_gather((normed_two * ffn_gain).astype(BF16)))
     gate_ffn = jnp.dot(ffn_all, w_ffn[:, :ffn_width], preferred_element_type=F32)
     up_ffn = jnp.dot(ffn_all, w_ffn[:, ffn_width:], preferred_element_type=F32)
     ffn_sigmoid = jax.nn.sigmoid(gate_ffn)
     ffn_active = gate_ffn * ffn_sigmoid
     hidden = (ffn_active * up_ffn).astype(BF16)
-    ffn_part = jnp.dot(hidden, w_down, preferred_element_type=F32).astype(BF16)
-    ffn_sum = head_scatter(ffn_part.reshape(micros, block_rows, model)).astype(F32)
-    block_out = (after_mix + ffn_sum).astype(BF16)
 
     hidden_grad = contract_cols(cotangent_all, w_down)
-    shard_down = dp_scatter(contract_rows(hidden, cotangent_all), 1)
     gate_ffn_grad = hidden_grad * up_ffn * ffn_sigmoid * (1.0 + gate_ffn * (1.0 - ffn_sigmoid))
     up_ffn_grad = hidden_grad * ffn_active
     gate_up_grad = jnp.concatenate([gate_ffn_grad, up_ffn_grad], axis=1).astype(BF16)
-    shard_ffn = dp_scatter(contract_rows(ffn_all, gate_up_grad), 0)
     ffn_in_part = contract_cols(gate_up_grad, w_ffn)
-    ffn_in_grad = head_scatter(ffn_in_part.reshape(micros, block_rows, model))
+    ffn_in_grad = head_scatter(ranked(ffn_in_part))
+    shard_ffn = scatter_rows(contract_rows(ffn_all, gate_up_grad).astype(BF16))
+    shard_down = scatter_columns(contract_rows(hidden, cotangent_all).astype(BF16))
     grad_norm_two = jnp.sum(ffn_in_grad * normed_two, axis=(0, 1))
-    after_mix_grad = out_grad.astype(F32) + norm_backward(
-        ffn_in_grad * ffn_norm, normed_two, scale_two
-    )
-
-    branch_grad = head_gather(after_mix_grad.astype(BF16)).reshape(-1, model)
-    gated_grad = contract_cols(branch_grad, w_out).reshape(head_rows + (value_size,))
-    shard_out = dp_scatter(contract_rows(gated, branch_grad), 1)
-    grad_head_norm = jnp.sum(gated_grad * normed_mix * gate_active, axis=(0, 1, 2))
-    gate_lin_grad = (
-        gated_grad * normed_mix * head_norm * gate_sigmoid * (1.0 + gate_lin * (1.0 - gate_sigmoid))
-    )
-    mixed_grad = norm_backward(gated_grad * head_norm * gate_active, normed_mix, out_scale)
-
-    local_grad = jnp.einsum(
-        "mthd,mthv->mhdv", carried_map, mixed_grad.astype(BF16), preferred_element_type=F32
-    )
-    leaving = scan_states(block_map, local_grad, True)
-    pre_grad, rim_grad, tail, dec_grad, taps_grad, par_grad = mix_backward(
-        info,
-        pre_conv,
-        rim,
-        dec,
-        taps,
-        par,
-        mixed_grad.reshape(-1, v_width),
-        inverses,
-        starts,
-        incoming,
-        leaving,
-        micros,
-        heads,
-        key_size,
+    after_mix_grad = cotangent.astype(F32) + norm_backward(
+        ffn_in_grad * ffn_gain, normed_two, scale_two
+    )
+
+    ffn_part = jnp.dot(hidden, w_down, preferred_element_type=F32)
+    block_out = (after_mix + head_scatter(ranked(ffn_part))).astype(BF16)
+
+    branch_grad = flat(head_gather(after_mix_grad.astype(BF16)))
+    gated_grad = contract_cols(branch_grad, w_out)
+    gate_grad, mixed_grad, local_grad, grad_head_norm = mix.gate_backward(
+        gated_grad, mixed, carried_map, gate_lin, gain
+    )
+    shard_out = scatter_columns(contract_rows(gated, branch_grad).astype(BF16))
+
+    leaving = scan_backward(local_grad, maps)
+    shard_gate = scatter_rows(contract_rows(normed_all, gate_grad).astype(BF16))
+    pre_grad, rim_grad, tail, dec_grad, taps_grad, par_grad = mix.backward(
+        pre_conv, rim, dec, taps, par, mixed_grad, inverses, starts, incoming, leaving
     )
     back_rim = from_behind(rim_grad, "dp", -1)
     tail = jnp.concatenate([tail[:, :8], tail[:, 8:] + back_rim], axis=1).astype(BF16)
     pre_grad = lax.dynamic_update_slice(
-        pre_grad.reshape(micros, block_rows, conv_width), tail, (0, block_rows - HALO, 0)
+        pre_grad.reshape(micros, ranks, part_rows, conv_width),
+        tail[:, None],
+        (0, last_chunk, part_rows - HALO, 0),
     ).reshape(-1, conv_width)
 
-    proj_grad = jnp.concatenate(
-        [pre_grad, gate_lin_grad.reshape(-1, v_width).astype(BF16), dec_grad], axis=1
-    )
-    shard_in = dp_scatter(contract_rows(normed_all, proj_grad), 0)
-    normed_part = contract_cols(proj_grad, w_in).astype(BF16)
-    normed_grad = head_scatter(normed_part.reshape(micros, block_rows, model)).astype(F32)
+    conv_grad = jnp.concatenate([pre_grad, dec_grad], axis=1)
+    shard_conv = scatter_rows(contract_rows(normed_all, conv_grad).astype(BF16))
+    normed_part = contract_cols(conv_grad, w_conv) + contract_cols(gate_grad, w_gate)
+    normed_grad = head_scatter(ranked(normed_part))
     grad_norm_one = jnp.sum(normed_grad * normed_one, axis=(0, 1))
-    input_grad = after_mix_grad + norm_backward(normed_grad * attn_norm, normed_one, scale_one)
+    input_grad = after_mix_grad + norm_backward(normed_grad * attn_gain, normed_one, scale_one)
 
     small = jnp.concatenate(
         [
             taps_grad[:KCONV].reshape(-1),
             jnp.pad(par_grad[0, :heads], (0, LANES - heads)),
             jnp.pad(par_grad[1, :heads], (0, LANES - heads)),
-            grad_head_norm,
-            grad_norm_one,
-            grad_norm_two,
+            grad_head_norm[0],
+            from_ring(grad_norm_one),
+            from_ring(grad_norm_two),
         ]
     ).reshape(-1, LANES)
     small = jnp.sum(lax.all_gather(small, "dp"), axis=0)
     small = lax.all_gather(small, "head")
-    head_count = small.shape[0]
     tap_rows = KCONV * conv_width // LANES
-    taps_all = small[:, :tap_rows].reshape(head_count, KCONV, conv_width).transpose(1, 0, 2)
+    taps_all = small[:, :tap_rows].reshape(ranks, KCONV, conv_width).transpose(1, 0, 2)
 
     def joined(low, high):
         return taps_all[:, :, low:high].reshape(KCONV, -1)
 
     rest = jnp.sum(small[:, tap_rows + 2 :], axis=0).reshape(-1)
     return (
-        block_out,
-        input_grad,
+        from_ring(block_out),
+        from_ring(input_grad),
         rest[value_size : value_size + model],
-        shard_in[:, :qk_width],
-        shard_in[:, qk_width : 2 * qk_width],
-        shard_in[:, 2 * qk_width : conv_width],
-        shard_in[:, conv_width:main_width],
-        shard_in[:, main_width : main_width + heads],
-        shard_in[:, main_width + heads : main_width + 2 * heads],
+        shard_conv[:, :qk_width],
+        shard_conv[:, qk_width : 2 * qk_width],
+        shard_conv[:, 2 * qk_width : conv_width],
+        shard_gate,
+        shard_conv[:, conv_width : conv_width + heads],
+        shard_conv[:, conv_width + heads : conv_width + 2 * heads],
         joined(0, qk_width),
         joined(qk_width, 2 * qk_width),
         joined(2 * qk_width, conv_width),

time: 1890 us -> 1120 us (0.59)
  waiting for transfers between devices: 1430 us -> 442 us
  starting transfers between devices: 6.38 us -> 147 us
  other arithmetic: 32.4 us -> 76.7 us
  local copies, waits for them, and re-layouts: 82.2 us -> 117 us
  Pallas kernels: 80.3 us -> 102 us
  matrix products: 194 us -> 173 us
    all_gather x10 -> x0, waiting for transfers between devices: 749 us -> none  [the longest x4 490 us: dp_gather(): return lax.all_gather(value, 'dp', axis=axis, tiled=True)]
    reduce_scatter x8 -> x0, waiting for transfers between devices: 676 us -> none  [the longest x4 492 us: dp_scatter(): lax.psum_scatter(value.astype(BF16), 'dp', scatter_dimension=axis, tiled=...]
    ppermute x0 -> x100, waiting for transfers between devices: none -> 370 us  [the longest x15 117 us: ring_scatter(): left = lax.ppermute(up, 'dp', ahead)]
    ppermute x0 -> x100, starting transfers between devices: none -> 133 us  [the longest x20 31.8 us: swap(): lax.ppermute(value, axis, [(at, at ^ bit) for at in range(lax.axis_size(a...]
    ppermute x2 -> x8, waiting for transfers between devices: 1.82 us -> 71.2 us  [from_behind(): lax.ppermute(value, axis, [(source, source + steps) for source in range(l...]
    unnamed x116 -> x313, local copies, waits for them, and re-layouts: 21.6 us -> 73.8 us
    convert_element_type x5 -> x29, other arithmetic: 10 us -> 33.7 us  [the longest x15 21.8 us: ring_scatter(): up, down = (add(up, left).astype(BF16), add(down, right).astype(BF16))]
    pallas_call x2 -> x4, Pallas kernels: 80.3 us -> 102 us  [kernel_call(): pl.pallas_call(partial(kernel, **sizes), grid_spec=pltpu.PrefetchScalarGr...]
  transfers between devices with their start and end apart: 20 -> 108, of which waited for: 19 -> 43; matrix products, arithmetic and copies ran while one was open for 10% -> 23% of each run, Pallas kernels for 2% -> 9%
where the time goes in v2:
time: 1120 us; the launch traced here: 1110 us
  waiting for transfers between devices  442 us (39%)
  matrix products  173 us (15%)
  starting transfers between devices  147 us (13%)
  local copies, waits for them, and re-layouts  117 us (10%)
  Pallas kernels  102 us (9%)
  other arithmetic  76.7 us (7%)
  blocking collectives  52.8 us (5%)
    ppermute x15, waiting for transfers between devices, ring_scatter(): left = lax.ppermute(up, 'dp', ahead)  117 us
    pallas_call x4, Pallas kernels, kernel_call(): pl.pallas_call(partial(kernel, **sizes), grid_spec=pltpu.PrefetchScalarGr...  102 us
    unnamed x313, local copies, waits for them, and re-layouts  73.8 us
    ppermute x8, waiting for transfers between devices, from_behind(): lax.ppermute(value, axis, [(source, source + steps) for source in range(l...  71.2 us
    ppermute x15, waiting for transfers between devices, ring_scatter(): right = lax.ppermute(down, 'dp', back)  66 us
    ppermute x15, waiting for transfers between devices, ring_gather(): from_left.append(lax.ppermute(from_left[-1], 'dp', ahead))  58.5 us
    dot_general x5, matrix products, contract_cols(): return lax.dot_general(left, right, NT, preferred_element_type=F32)  57.2 us
    dot_general x5, matrix products, contract_rows(): return lax.dot_general(left, right, TN, preferred_element_type=F32)  51 us
  transfers between devices with their start and end apart: 108, of which 43 were waited for; matrix products, arithmetic and copies ran while one was open for 23% of the time, Pallas kernels for 9%

profile of v2, /device:TPU:0, one launch (start us, length us, event | category | flops | bytes accessed | tf_op | source)
XLA Modules:
  0.0 1113.7 jit_solution(784680279075391179)
XLA Ops:
  44.4 15.9 %collective-permute-done.6 = bf16[256,2176]{1,0:T(8,128)(2,1)} collective-permute-done((bf16[256,2176]{1,0:T(8,128)(2,1)}, bf16[256,2176]{1,0:T(8,128)(2,1)}, u32[]{:S(2)}, u32[]{:S(2)}) %collective-permute-start.6) | collective-permute-done | bytes 1114144 | tf_op jit(solution)/shard_map/ppermute | solution.py:764
  70.2 9.6 collective-permute-done.3
  100.8 9.7 collective-permute-done.27
  112.6 9.8 collective-permute-done.8
  153.4 12.2 %fusion.84 = f32[1024,2176]{1,0:T(8,128)} fusion(bf16[1024,2048]{1,0:T(8,128)(2,1)S(1)} %bitcast.198, bf16[2048,2176]{1,0:T(8,128)(2,1)S(1)} %constant_dynamic-update-slice_fusion.12), kind=kOutput, calls=%fused_computation.370 | convolution fusion | flops 9126805504 | bytes 22020096 | tf_op jit(solution)/shard_map/dot_general | solution.py:964
  179.8 35.7 %mix_forward.1 = (f32[1024,1024]{1,0:T(8,128)}, bf16[1024,512]{1,0:T(8,128)(2,1)S(1)}, bf16[8,4,128,128]{3,2,1,0:T(8,128)(2,1)S(1)}, bf16[8,4,128,384]{3,2,1,0:T(8,128)(2,1)}, f32[2,4,128,384]{3,2,1,0:T(8,128)S(1)}) custom-call(s32[2,6]{1,0:T(2,128)S(1)} %add_add_fusion.info_ref, bf16[1024,2048]{1,0:T(8,128)(2,1)} %copy-done.17, ...), custom_call_target="tpu_custom_call" | custom-call | tf_op jit(solution)/shard_map/mix_forward/pallas_call | solution.py:525
  234.3 14.7 %collective-permute-done.22 = bf16[128,1024]{1,0:T(8,128)(2,1)S(1)} collective-permute-done((bf16[128,1024]{1,0:T(8,128)(2,1)S(1)}, bf16[128,1024]{1,0:T(8,128)(2,1)S(1)}, u32[]{:S(2)}, u32[]{:S(2)}) %collective-permute-start.22) | collective-permute-done | bytes 262176 | tf_op jit(solution)/shard_map/ppermute | solution.py:769
  250.3 11.0 collective-permute-done.23
  280.9 39.7 %collective-permute-done.14 = bf16[4,128,256]{2,1,0:T(8,128)(2,1)S(1)} collective-permute-done((bf16[4,128,256]{2,1,0:T(8,128)(2,1)S(1)}, bf16[4,128,256]{2,1,0:T(8,128)(2,1)S(1)}, u32[]{:S(2)}, u32[]{:S(2)}) %collective-permute-start.14) | collective-permute-done | bytes 262176 | tf_op jit(solution)/shard_map/ppermute | solution.py:698
  331.5 9.4 gate_forward.1
  364.9 26.6 %collective-permute-done.51 = bf16[704,256]{1,0:T(8,128)(2,1)S(1)} collective-permute-done((bf16[704,256]{1,0:T(8,128)(2,1)S(1)}, bf16[704,256]{1,0:T(8,128)(2,1)S(1)}, u32[]{:S(2)}, u32[]{:S(2)}) %collective-permute-start.51) | collective-permute-done | bytes 360480 | tf_op jit(solution)/shard_map/ppermute | solution.py:770
  404.8 18.7 %collective-permute-done.33 = bf16[2,128,2048]{2,1,0:T(8,128)(2,1)} collective-permute-done((bf16[2,128,2048]{2,1,0:T(8,128)(2,1)}, bf16[2,128,2048]{2,1,0:T(8,128)(2,1)}, u32[]{:S(2)}, u32[]{:S(2)}) %collective-permute-start.33) | collective-permute-done | bytes 1048608 | tf_op jit(solution)/shard_map/ppermute | solution.py:702
  427.1 10.4 fusion.88
  476.1 15.5 %multiply_convert_fusion.1 = (bf16[1024,1408]{1,0:T(8,128)(2,1)}, bf16[1024,1408]{1,0:T(8,128)(2,1)}, bf16[1024,1408]{1,0:T(8,128)(2,1)}) fusion(f32[1024,1408]{1,0:T(8,128)} %fusion.88, f32[1024,1408]{1,0:T(8,128)} %fusion, bf16[1024,2048]{1,0:T(8,128)(2,1)S(1)} %bitcast.205, bf16[2048,2816]{1,0:T(8,128)(2,1)} %constant_dynamic-update-slice_fusion.38), kind=kOutput, calls=%fused_computation.10 | convolution fusion | flops 5927206912 | bytes 30146560 | tf_op jit(solution)/shard_map/dot_general | solution.py:985
  491.6 17.4 %convolution_convert_fusion = bf16[2048,2816]{1,0:T(8,128)(2,1)} fusion(bf16[1024,2048]{1,0:T(8,128)(2,1)S(1)} %bitcast.206, bf16[1024,1408]{1,0:T(8,128)(2,1)} %get-tuple-element.140, bf16[1024,1408]{1,0:T(8,128)(2,1)} %get-tuple-element.139), kind=kOutput, calls=%fused_computation | convolution fusion | flops 11828461568 | bytes 21495808 | tf_op jit(solution)/shard_map/dot_general | solution.py:860
  509.0 18.9 %fusion.5 = f32[1024,2048]{1,0:T(8,128)} fusion(bf16[2048,2816]{1,0:T(8,128)(2,1)} %constant_dynamic-update-slice_fusion.38, bf16[1024,1408]{1,0:T(8,128)(2,1)} %get-tuple-element.140, bf16[1024,1408]{1,0:T(8,128)(2,1)} %get-tuple-element.139), kind=kOutput, calls=%fused_computation.23 | convolution fusion | flops 11822694400 | bytes 25690112 | tf_op jit(solution)/shard_map/dot_general | solution.py:864
  536.3 13.7 %fusion.87 = f32[1024,2048]{1,0:T(8,128)} fusion(bf16[1024,1408]{1,0:T(8,128)(2,1)} %get-tuple-element.141, bf16[1408,2048]{1,0:T(8,128)(2,1)} %constant_dynamic-update-slice_fusion.47), kind=kOutput, calls=%fused_computation.373 | convolution fusion | flops 5905580032 | bytes 17039360 | tf_op jit(solution)/shard_map/dot_general | solution.py:1004
  582.3 12.1 %collective-permute-done.101 = bf16[1408,256]{1,0:T(8,128)(2,1)S(1)} collective-permute-done((bf16[1408,256]{1,0:T(8,128)(2,1)S(1)}, bf16[1408,256]{1,0:T(8,128)(2,1)S(1)}, u32[]{:S(2)}, u32[]{:S(2)}) %collective-permute-start.101) | collective-permute-done | bytes 720928 | tf_op jit(solution)/shard_map/ppermute | solution.py:795
  596.2 25.7 %collective-permute-done.93 = bf16[256,2816]{1,0:T(8,128)(2,1)S(1)} collective-permute-done((bf16[256,2816]{1,0:T(8,128)(2,1)S(1)}, bf16[256,2816]{1,0:T(8,128)(2,1)S(1)}, u32[]{:S(2)}, u32[]{:S(2)}) %collective-permute-start.93) | collective-permute-done | bytes 1441824 | tf_op jit(solution)/shard_map/ppermute | solution.py:795
  629.8 11.9 %collective-permute-done.102 = bf16[1408,256]{1,0:T(8,128)(2,1)} collective-permute-done((bf16[1408,256]{1,0:T(8,128)(2,1)}, bf16[1408,256]{1,0:T(8,128)(2,1)}, u32[]{:S(2)}, u32[]{:S(2)}) %collective-permute-start.102) | collective-permute-done | bytes 720928 | tf_op jit(solution)/shard_map/ppermute | solution.py:795
  646.3 26.3 %collective-permute-done.94 = bf16[256,2816]{1,0:T(8,128)(2,1)} collective-permute-done((bf16[256,2816]{1,0:T(8,128)(2,1)S(1)}, bf16[256,2816]{1,0:T(8,128)(2,1)}, u32[]{:S(2)}, u32[]{:S(2)}) %collective-permute-start.94) | collective-permute-done | bytes 1441824 | tf_op jit(solution)/shard_map/ppermute | solution.py:795
  686.4 30.9 %collective-permute-done.107 = bf16[1408,256]{1,0:T(8,128)(2,1)} collective-permute-done((bf16[1408,256]{1,0:T(8,128)(2,1)}, bf16[1408,256]{1,0:T(8,128)(2,1)}, u32[]{:S(2)}, u32[]{:S(2)}) %collective-permute-start.107) | collective-permute-done | bytes 720928 | tf_op jit(solution)/shard_map/ppermute | solution.py:796
  743.4 10.5 gate_backward.1
  819.0 13.3 %collective-permute-start.64 = (bf16[4,128,256]{2,1,0:T(8,128)(2,1)S(1)}, bf16[4,128,256]{2,1,0:T(8,128)(2,1)S(1)}, u32[]{:S(2)}, u32[]{:S(2)}) collective-permute-start(bf16[4,128,256]{2,1,0:T(8,128)(2,1)S(1)} %get-tuple-element.212), channel_id=1, source_target_pairs={{0,4},{4,0},{8,12},{12,8},{16,20},{20,16},{24,28},{28,24},{1,5},{5... | collective-permute-start | bytes 786440 | tf_op jit(solution)/shard_map/ppermute | solution.py:702
  842.0 46.1 %mix_backward.1 = (bf16[1024,2048]{1,0:T(8,128)(2,1)}, f32[2,8,2048]{2,1,0:T(8,128)S(1)}, f32[2,16,2048]{2,1,0:T(8,128)S(1)}, bf16[1024,128]{1,0:T(8,128)(2,1)S(...) custom-call(s32[2,6]{1,0:T(2,128)S(1)} %add_add_fusion.info_ref, bf16[1024,2048]{1,0:T(8,128)(2,1)} %copy-done.17, ...), custom_call_target="tpu_custom_call" | custom-call | tf_op jit(solution)/shard_map/mix_backward/pallas_call | solution.py:525
  895.6 13.1 %convolution_convert_fusion.1 = bf16[2048,2176]{1,0:T(8,128)(2,1)S(1)} fusion(bf16[1024,2048]{1,0:T(8,128)(2,1)S(1)} %bitcast.201, bf16[1024,128]{1,0:T(8,128)(2,1)S(1)} %get-tuple-element.57, bf16[1024,2048]{1,0:T(8,128)(2,1)} %bitcast.229), kind=kOutput, calls=%fused_computation.1 | convolution fusion | flops 9140174848 | bytes 17563648 | tf_op jit(solution)/shard_map/dot_general | solution.py:860
  915.7 14.9 %convolution_add_fusion = f32[1024,2048]{1,0:T(8,128)S(1)} fusion(f32[1024,2048]{1,0:T(8,128)} %fusion.90, bf16[2048,2176]{1,0:T(8,128)(2,1)} %copy-done.73, bf16[1024,128]{1,0:T(8,128)(2,1)S(1)} %get-tuple-element.57, bf16[1024,2048]{1,0:T(8,128)(2,1)} %bitcast.230), kind=kOutput, calls=%fused_computation.24 | convolution fusion | flops 9137815552 | bytes 30146560 | tf_op jit(solution)/shard_map/dot_general | solution.py:864
  944.0 22.2 %collective-permute-done.69 = bf16[256,2176]{1,0:T(8,128)(2,1)S(1)} collective-permute-done((bf16[256,2176]{1,0:T(8,128)(2,1)S(1)}, bf16[256,2176]{1,0:T(8,128)(2,1)S(1)}, u32[]{:S(2)}, u32[]{:S(2)}) %collective-permute-start.69) | collective-permute-done | bytes 1114144 | tf_op jit(solution)/shard_map/ppermute | solution.py:795
  968.0 9.4 collective-permute-done.87
  1011.3 43.0 %all_gather.9 = f32[8,100,128]{2,1,0:T(8,128)} all-gather(f32[1,100,128]{2,1,0:T(8,128)S(1)} %bitcast.220), channel_id=1, replica_groups=mesh['dp'=8,'head'=4] {'dp'}, dimensions={0}, use_global_device_ids=true | all-gather | bytes 460800 | tf_op jit(solution)/shard_map/all_gather | solution.py:1044
  1055.4 9.8 all-gather.1
  1081.5 26.1 %collective-permute-done.75 = bf16[256,2176]{1,0:T(8,128)(2,1)S(1)} collective-permute-done((bf16[256,2176]{1,0:T(8,128)(2,1)S(1)}, bf16[256,2176]{1,0:T(8,128)(2,1)S(1)}, u32[]{:S(2)}, u32[]{:S(2)}) %collective-permute-start.75) | collective-permute-done | bytes 1114144 | tf_op jit(solution)/shard_map/ppermute | solution.py:796
  (694 shorter events, 506.1 us)
Async XLA Ops:
  12.8 48.2 %collective-permute-start.16 = (bf16[256,1024]{1,0:T(8,128)(2,1)}, bf16[256,1024]{1,0:T(8,128)(2,1)}, u32[]{:S(2)}, u32[]{:S(2)}) collective-permute-start(bf16[256,1024]{1,0:T(8,128)(2,1)} %param.28), channel_id=1, source_target_pairs={{8,0},{16,8},{24,16},{28,24},{20,28},{12,20},{4,12},{0,4},{9,1},{1... | collective-permute-start | bytes 1572872 | tf_op jit(solution)/shard_map/ppermute | solution.py:765
  14.3 50.0 %collective-permute-start.24 = (bf16[1024,256]{1,0:T(8,128)(2,1)}, bf16[1024,256]{1,0:T(8,128)(2,1)}, u32[]{:S(2)}, u32[]{:S(2)}) collective-permute-start(bf16[1024,256]{1,0:T(8,128)(2,1)} %param.37), channel_id=1, source_target_pairs={{8,0},{16,8},{24,16},{28,24},{20,28},{12,20},{4,12},{0,4},{9,1},{1... | collective-permute-start | bytes 1572872 | tf_op jit(solution)/shard_map/ppermute | solution.py:765
  38.6 51.0 %collective-permute-start.1 = (bf16[2,2,128,2048]{3,2,1,0:T(8,128)(2,1)}, bf16[2,2,128,2048]{3,2,1,0:T(8,128)(2,1)}, u32[]{:S(2)}, u32[]{:S(2)}) collective-permute-start(bf16[2,2,128,2048]{3,2,1,0:T(8,128)(2,1)} %pad_maximum_fusion.10), channel_id=1, source_target_pairs={{0,1},{1,0},{2,3},{3,2},{4,5},{5,4},{6,7},{7,6},{8,9},{9,8},{10,11... | collective-permute-start | bytes 6291464 | tf_op jit(solution)/shard_map/ppermute | solution.py:702
  64.3 46.1 %collective-permute-start.27 = (bf16[1024,256]{1,0:T(8,128)(2,1)}, bf16[1024,256]{1,0:T(8,128)(2,1)S(1)}, u32[]{:S(2)}, u32[]{:S(2)}) collective-permute-start(bf16[1024,256]{1,0:T(8,128)(2,1)} %param.37), channel_id=1, source_target_pairs={{0,8},{8,16},{16,24},{24,28},{28,20},{20,12},{12,4},{4,0},{1,9},{9... | collective-permute-start | bytes 1572872 | tf_op jit(solution)/shard_map/ppermute | solution.py:764
  124.2 45.4 %collective-permute-start.44 = (bf16[1408,256]{1,0:T(8,128)(2,1)S(1)}, bf16[1408,256]{1,0:T(8,128)(2,1)S(1)}, u32[]{:S(2)}, u32[]{:S(2)}) collective-permute-start(bf16[1408,256]{1,0:T(8,128)(2,1)S(1)} %copy-done.55), channel_id=1, source_target_pairs={{8,0},{16,8},{24,16},{28,24},{20,28},{12,20},{4,12},{0,4},{9,1},{1... | collective-permute-start | bytes 2162696 | tf_op jit(solution)/shard_map/ppermute | solution.py:765
  133.7 88.8 %collective-permute-start.18 = (bf16[256,1024]{1,0:T(8,128)(2,1)}, bf16[256,1024]{1,0:T(8,128)(2,1)}, u32[]{:S(2)}, u32[]{:S(2)}) collective-permute-start(bf16[256,1024]{1,0:T(8,128)(2,1)} %collective-permute-done.17), channel_id=1, source_target_pairs={{8,0},{16,8},{24,16},{28,24},{20,28},{12,20},{4,12},{0,4},{9,1},{1... | collective-permute-start | bytes 1572872 | tf_op jit(solution)/shard_map/ppermute | solution.py:765
  135.3 86.6 %collective-permute-start.21 = (bf16[256,1024]{1,0:T(8,128)(2,1)}, bf16[256,1024]{1,0:T(8,128)(2,1)S(1)}, u32[]{:S(2)}, u32[]{:S(2)}) collective-permute-start(bf16[256,1024]{1,0:T(8,128)(2,1)} %collective-permute-done.20), channel_id=1, source_target_pairs={{0,8},{8,16},{16,24},{24,28},{28,20},{20,12},{12,4},{4,0},{1,9},{9... | collective-permute-start | bytes 1572872 | tf_op jit(solution)/shard_map/ppermute | solution.py:764
  145.0 81.7 %collective-permute-start.26 = (bf16[1024,256]{1,0:T(8,128)(2,1)}, bf16[1024,256]{1,0:T(8,128)(2,1)}, u32[]{:S(2)}, u32[]{:S(2)}) collective-permute-start(bf16[1024,256]{1,0:T(8,128)(2,1)} %collective-permute-done.25), channel_id=1, source_target_pairs={{8,0},{16,8},{24,16},{28,24},{20,28},{12,20},{4,12},{0,4},{9,1},{1... | collective-permute-start | bytes 1572872 | tf_op jit(solution)/shard_map/ppermute | solution.py:765
  146.5 78.5 %collective-permute-start.29 = (bf16[1024,256]{1,0:T(8,128)(2,1)}, bf16[1024,256]{1,0:T(8,128)(2,1)S(1)}, u32[]{:S(2)}, u32[]{:S(2)}) collective-permute-start(bf16[1024,256]{1,0:T(8,128)(2,1)} %collective-permute-done.28), channel_id=1, source_target_pairs={{0,8},{8,16},{16,24},{24,28},{28,20},{20,12},{12,4},{4,0},{1,9},{9... | collective-permute-start | bytes 1572872 | tf_op jit(solution)/shard_map/ppermute | solution.py:764
  221.9 126.8 %collective-permute-start.36 = (bf16[256,2816]{1,0:T(8,128)(2,1)S(1)}, bf16[256,2816]{1,0:T(8,128)(2,1)}, u32[]{:S(2)}, u32[]{:S(2)}) collective-permute-start(bf16[256,2816]{1,0:T(8,128)(2,1)S(1)} %copy-done.34), channel_id=1, source_target_pairs={{8,0},{16,8},{24,16},{28,24},{20,28},{12,20},{4,12},{0,4},{9,1},{1... | collective-permute-start | bytes 4325384 | tf_op jit(solution)/shard_map/ppermute | solution.py:765
  266.8 92.1 %collective-permute-start.39 = (bf16[256,2816]{1,0:T(8,128)(2,1)S(1)}, bf16[256,2816]{1,0:T(8,128)(2,1)}, u32[]{:S(2)}, u32[]{:S(2)}) collective-permute-start(bf16[256,2816]{1,0:T(8,128)(2,1)S(1)} %copy-done.34), channel_id=1, source_target_pairs={{0,8},{8,16},{16,24},{24,28},{28,20},{20,12},{12,4},{4,0},{1,9},{9... | collective-permute-start | bytes 4325384 | tf_op jit(solution)/shard_map/ppermute | solution.py:764
  266.9 60.0 %collective-permute-start.45 = (bf16[1408,256]{1,0:T(8,128)(2,1)S(1)}, bf16[1408,256]{1,0:T(8,128)(2,1)}, u32[]{:S(2)}, u32[]{:S(2)}) collective-permute-start(bf16[1408,256]{1,0:T(8,128)(2,1)S(1)} %copy-done.60), channel_id=1, source_target_pairs={{8,0},{16,8},{24,16},{28,24},{20,28},{12,20},{4,12},{0,4},{9,1},{1... | collective-permute-start | bytes 2162696 | tf_op jit(solution)/shard_map/ppermute | solution.py:765
  273.8 54.5 %collective-permute-start.48 = (bf16[1408,256]{1,0:T(8,128)(2,1)S(1)}, bf16[1408,256]{1,0:T(8,128)(2,1)}, u32[]{:S(2)}, u32[]{:S(2)}) collective-permute-start(bf16[1408,256]{1,0:T(8,128)(2,1)S(1)} %collective-permute-done.47), channel_id=1, source_target_pairs={{0,8},{8,16},{16,24},{24,28},{28,20},{20,12},{12,4},{4,0},{1,9},{9... | collective-permute-start | bytes 2162696 | tf_op jit(solution)/shard_map/ppermute | solution.py:764
  274.9 45.6 %collective-permute-start.14 = (bf16[4,128,256]{2,1,0:T(8,128)(2,1)S(1)}, bf16[4,128,256]{2,1,0:T(8,128)(2,1)S(1)}, u32[]{:S(2)}, u32[]{:S(2)}) collective-permute-start(bf16[4,128,256]{2,1,0:T(8,128)(2,1)S(1)} %fusion.34), channel_id=1, source_target_pairs={{0,8},{4,12},{8,16},{12,20},{16,24},{20,28},{1,9},{5,13},{9,17},{1... | collective-permute-start | bytes 786440 | tf_op jit(solution)/shard_map/ppermute | solution.py:698
  348.5 49.0 %collective-permute-start.32 = (bf16[2,2,128,2048]{3,2,0,1:T(8,128)(2,1)S(1)}, bf16[2,2,128,2048]{3,2,0,1:T(8,128)(2,1)S(1)}, u32[]{:S(2)}, u32[]{:S(2)}) collective-permute-start(bf16[2,2,128,2048]{3,2,0,1:T(8,128)(2,1)S(1)} %pad_maximum_fusion.11), channel_id=1, source_target_pairs={{0,1},{1,0},{2,3},{3,2},{4,5},{5,4},{6,7},{7,6},{8,9},{9,8},{10,11... | collective-permute-start | bytes 6291464 | tf_op jit(solution)/shard_map/ppermute | solution.py:702
  348.7 47.8 %collective-permute-start.37 = (bf16[256,2816]{1,0:T(8,128)(2,1)}, bf16[256,2816]{1,0:T(8,128)(2,1)}, u32[]{:S(2)}, u32[]{:S(2)}) collective-permute-start(bf16[256,2816]{1,0:T(8,128)(2,1)} %collective-permute-done.36), channel_id=1, source_target_pairs={{8,0},{16,8},{24,16},{28,24},{20,28},{12,20},{4,12},{0,4},{9,1},{1... | collective-permute-start | bytes 4325384 | tf_op jit(solution)/shard_map/ppermute | solution.py:765
  359.0 44.8 %collective-permute-start.55 = (bf16[2,2,128,2048]{3,2,0,1:T(8,128)(2,1)S(1)}, bf16[2,2,128,2048]{3,2,0,1:T(8,128)(2,1)S(1)}, u32[]{:S(2)}, u32[]{:S(2)}) collective-permute-start(bf16[2,2,128,2048]{3,2,0,1:T(8,128)(2,1)S(1)} %pad_maximum_fusion.14), channel_id=1, source_target_pairs={{0,1},{1,0},{2,3},{3,2},{4,5},{5,4},{6,7},{7,6},{8,9},{9,8},{10,11... | collective-permute-start | bytes 6291464 | tf_op jit(solution)/shard_map/ppermute | solution.py:702
  562.7 119.7 %collective-permute-start.52 = (bf16[2,2,128,2048]{3,2,0,1:T(8,128)(2,1)}, bf16[2,2,128,2048]{3,2,0,1:T(8,128)(2,1)}, u32[]{:S(2)}, u32[]{:S(2)}) collective-permute-start(bf16[2,2,128,2048]{3,2,0,1:T(8,128)(2,1)} %pad_maximum_fusion.13), channel_id=1, source_target_pairs={{0,1},{1,0},{2,3},{3,2},{4,5},{5,4},{6,7},{7,6},{8,9},{9,8},{10,11... | collective-permute-start | bytes 6291464 | tf_op jit(solution)/shard_map/ppermute | solution.py:702
  566.1 63.0 %collective-permute-start.105 = (bf16[1408,256]{1,0:T(8,128)(2,1)}, bf16[1408,256]{1,0:T(8,128)(2,1)}, u32[]{:S(2)}, u32[]{:S(2)}) collective-permute-start(bf16[1408,256]{1,0:T(8,128)(2,1)} %pad_maximum_fusion.24), channel_id=1, source_target_pairs={{8,0},{16,8},{24,16},{28,24},{20,28},{12,20},{4,12},{0,4},{9,1},{1... | collective-permute-start | bytes 2162696 | tf_op jit(solution)/shard_map/ppermute | solution.py:796
  581.6 64.4 %collective-permute-start.97 = (bf16[256,2816]{1,0:T(8,128)(2,1)S(1)}, bf16[256,2816]{1,0:T(8,128)(2,1)S(1)}, u32[]{:S(2)}, u32[]{:S(2)}) collective-permute-start(bf16[256,2816]{1,0:T(8,128)(2,1)S(1)} %pad_maximum_fusion.20), channel_id=1, source_target_pairs={{8,0},{16,8},{24,16},{28,24},{20,28},{12,20},{4,12},{0,4},{9,1},{1... | collective-permute-start | bytes 4325384 | tf_op jit(solution)/shard_map/ppermute | solution.py:796
  623.8 48.7 %collective-permute-start.94 = (bf16[256,2816]{1,0:T(8,128)(2,1)S(1)}, bf16[256,2816]{1,0:T(8,128)(2,1)}, u32[]{:S(2)}, u32[]{:S(2)}) collective-permute-start(bf16[256,2816]{1,0:T(8,128)(2,1)S(1)} %add_convert_fusion.3), channel_id=1, source_target_pairs={{0,8},{8,16},{16,24},{24,28},{28,20},{20,12},{12,4},{4,0},{1,9},{9... | collective-permute-start | bytes 4325384 | tf_op jit(solution)/shard_map/ppermute | solution.py:795
  629.1 48.7 %collective-permute-start.58 = (bf16[2,128,2048]{2,1,0:T(8,128)(2,1)S(1)}, bf16[2,128,2048]{2,1,0:T(8,128)(2,1)S(1)}, u32[]{:S(2)}, u32[]{:S(2)}) collective-permute-start(bf16[2,128,2048]{2,1,0:T(8,128)(2,1)S(1)} %fusion.65), channel_id=1, source_target_pairs={{0,2},{1,3},{2,0},{3,1},{4,6},{5,7},{6,4},{7,5},{8,10},{9,11},{10,... | collective-permute-start | bytes 3145736 | tf_op jit(solution)/shard_map/ppermute | solution.py:702
  679.5 45.9 %collective-permute-start.59 = (bf16[2,2,128,2048]{3,2,0,1:T(8,128)(2,1)}, bf16[2,2,128,2048]{3,2,0,1:T(8,128)(2,1)}, u32[]{:S(2)}, u32[]{:S(2)}) collective-permute-start(bf16[2,2,128,2048]{3,2,0,1:T(8,128)(2,1)} %pad_maximum_fusion.16), channel_id=1, source_target_pairs={{0,1},{1,0},{2,3},{3,2},{4,5},{5,4},{6,7},{7,6},{8,9},{9,8},{10,11... | collective-permute-start | bytes 6291464 | tf_op jit(solution)/shard_map/ppermute | solution.py:702
  685.6 386.0 %collective-permute-start.53 = (bf16[2,128,2048]{2,1,0:T(8,128)(2,1)}, bf16[2,128,2048]{2,1,0:T(8,128)(2,1)}, u32[]{:S(2)}, u32[]{:S(2)}) collective-permute-start(bf16[2,128,2048]{2,1,0:T(8,128)(2,1)} %fusion.40), channel_id=1, source_target_pairs={{0,2},{1,3},{2,0},{3,1},{4,6},{5,7},{6,4},{7,5},{8,10},{9,11},{10,... | collective-permute-start | bytes 3145736 | tf_op jit(solution)/shard_map/ppermute | solution.py:702
  720.1 48.0 %collective-permute-start.95 = (bf16[256,2816]{1,0:T(8,128)(2,1)}, bf16[256,2816]{1,0:T(8,128)(2,1)}, u32[]{:S(2)}, u32[]{:S(2)}) collective-permute-start(bf16[256,2816]{1,0:T(8,128)(2,1)} %get-tuple-element.131), channel_id=1, source_target_pairs={{0,8},{8,16},{16,24},{24,28},{28,20},{20,12},{12,4},{4,0},{1,9},{9... | collective-permute-start | bytes 4325384 | tf_op jit(solution)/shard_map/ppermute | solution.py:795
  723.6 44.8 %collective-permute-start.99 = (bf16[256,2816]{1,0:T(8,128)(2,1)}, bf16[256,2816]{1,0:T(8,128)(2,1)}, u32[]{:S(2)}, u32[]{:S(2)}) collective-permute-start(bf16[256,2816]{1,0:T(8,128)(2,1)} %add_convert_fusion), channel_id=1, source_target_pairs={{8,0},{16,8},{24,16},{28,24},{20,28},{12,20},{4,12},{0,4},{9,1},{1... | collective-permute-start | bytes 4325384 | tf_op jit(solution)/shard_map/ppermute | solution.py:796
  785.5 48.2 %collective-permute-start.81 = (bf16[256,1024]{1,0:T(8,128)(2,1)S(1)}, bf16[256,1024]{1,0:T(8,128)(2,1)S(1)}, u32[]{:S(2)}, u32[]{:S(2)}) collective-permute-start(bf16[256,1024]{1,0:T(8,128)(2,1)S(1)} %pad_maximum_fusion.28), channel_id=1, source_target_pairs={{8,0},{16,8},{24,16},{28,24},{20,28},{12,20},{4,12},{0,4},{9,1},{1... | collective-permute-start | bytes 1572872 | tf_op jit(solution)/shard_map/ppermute | solution.py:796
  833.6 105.6 %collective-permute-start.90 = (bf16[1024,256]{1,0:T(8,128)(2,1)}, bf16[1024,256]{1,0:T(8,128)(2,1)}, u32[]{:S(2)}, u32[]{:S(2)}) collective-permute-start(bf16[1024,256]{1,0:T(8,128)(2,1)} %get-tuple-element.159), channel_id=1, source_target_pairs={{8,0},{16,8},{24,16},{28,24},{20,28},{12,20},{4,12},{0,4},{9,1},{1... | collective-permute-start | bytes 1572872 | tf_op jit(solution)/shard_map/ppermute | solution.py:796
  839.5 101.9 %collective-permute-start.82 = (bf16[256,1024]{1,0:T(8,128)(2,1)}, bf16[256,1024]{1,0:T(8,128)(2,1)}, u32[]{:S(2)}, u32[]{:S(2)}) collective-permute-start(bf16[256,1024]{1,0:T(8,128)(2,1)} %get-tuple-element.167), channel_id=1, source_target_pairs={{8,0},{16,8},{24,16},{28,24},{20,28},{12,20},{4,12},{0,4},{9,1},{1... | collective-permute-start | bytes 1572872 | tf_op jit(solution)/shard_map/ppermute | solution.py:796
  941.4 47.2 %collective-permute-start.79 = (bf16[256,1024]{1,0:T(8,128)(2,1)S(1)}, bf16[256,1024]{1,0:T(8,128)(2,1)S(1)}, u32[]{:S(2)}, u32[]{:S(2)}) collective-permute-start(bf16[256,1024]{1,0:T(8,128)(2,1)S(1)} %copy-done.67), channel_id=1, source_target_pairs={{0,8},{8,16},{16,24},{24,28},{28,20},{20,12},{12,4},{4,0},{1,9},{9... | collective-permute-start | bytes 1572872 | tf_op jit(solution)/shard_map/ppermute | solution.py:795
  1008.1 70.8 %collective-permute-start.74 = (bf16[256,2176]{1,0:T(8,128)(2,1)}, bf16[256,2176]{1,0:T(8,128)(2,1)}, u32[]{:S(2)}, u32[]{:S(2)}) collective-permute-start(bf16[256,2176]{1,0:T(8,128)(2,1)} %get-tuple-element.143), channel_id=1, source_target_pairs={{8,0},{16,8},{24,16},{28,24},{20,28},{12,20},{4,12},{0,4},{9,1},{1... | collective-permute-start | bytes 3342344 | tf_op jit(solution)/shard_map/ppermute | solution.py:796
  1009.7 71.9 %collective-permute-start.71 = (bf16[256,2176]{1,0:T(8,128)(2,1)}, bf16[256,2176]{1,0:T(8,128)(2,1)}, u32[]{:S(2)}, u32[]{:S(2)}) collective-permute-start(bf16[256,2176]{1,0:T(8,128)(2,1)} %get-tuple-element.142), channel_id=1, source_target_pairs={{0,8},{8,16},{16,24},{24,28},{28,20},{20,12},{12,4},{4,0},{1,9},{9... | collective-permute-start | bytes 3342344 | tf_op jit(solution)/shard_map/ppermute | solution.py:795
  (173 other events, 4088.4 us)

commit v3 on v2

--- a/solution.py
+++ b/solution.py
@@ -137,7 +137,6 @@
     info_ref,
     x_ref,
     rim_ref,
-    dec_ref,
     taps_ref,
     par_ref,
     out_ref,
@@ -156,9 +155,11 @@
     micro, chunk = pl.program_id(0), pl.program_id(1)
     span = range(heads)
 
+    width = halo.shape[1]
+
     @pl.when(chunk == 0)
     def _():
-        halo[...] = rim_ref[0]
+        halo[...] = rim_ref[:, :width].astype(BF16)
         row_ids = lax.broadcasted_iota(jnp.int32, (key_size, key_size), 0)
         col_ids = lax.broadcasted_iota(jnp.int32, (key_size, key_size), 1)
         eye = jnp.where(row_ids == col_ids, 1.0, 0.0).astype(F32)
@@ -166,7 +167,7 @@
             state[head] = jnp.concatenate([jnp.zeros((key_size, value_size), F32), eye], axis=1)
 
     places = chunk_places(info_ref, micro, chunk, seq_count)
-    dec = dec_ref[...]
+    dec = x_ref[:, width:]
     beta_all = jax.nn.sigmoid(dec)
     g_all = par_ref[0:1, :] * softplus(dec + par_ref[1:2, :])
     scale = key_size**-0.5
@@ -174,17 +175,17 @@
     queries, keys, values = [], [], []
     for head in span:
         rows = []
-        for begin, width in head_columns(head, heads, key_size, value_size):
-            cut = slice(begin, begin + width)
+        for begin, size in head_columns(head, heads, key_size, value_size):
+            cut = slice(begin, begin + size)
             extended = jnp.concatenate(
-                [halo[:, cut].astype(F32), x_ref[:, cut].astype(F32)], axis=0
+                [halo[:, cut].astype(F32), x_ref[:, cut].astype(BF16).astype(F32)], axis=0
             )
             summed = conv_rows(extended, taps_ref[0:KCONV, cut], places["lags"])
             rows.append(summed * jax.nn.sigmoid(summed))
         queries.append(unit_rows(rows[0]) * scale)
         keys.append(unit_rows(rows[1]))
         values.append(rows[2])
-    halo[...] = x_ref[CHUNK - HALO :, :]
+    halo[...] = x_ref[CHUNK - HALO :, :width].astype(BF16)
 
     betas = [beta_all[:, heads + head : heads + head + 1] for head in span]
     decays = [decay_parts(g_all[:, head : head + 1], places) for head in span]
@@ -236,7 +237,6 @@
     x_ref,
     before_ref,
     rim_ref,
-    dec_ref,
     taps_ref,
     par_ref,
     grad_ref,
@@ -247,7 +247,6 @@
     dx_ref,
     rim_grad_ref,
     tail_ref,
-    ddec_ref,
     dtaps_ref,
     dpar_ref,
     carry,
@@ -261,6 +260,7 @@
     micro, step = pl.program_id(0), pl.program_id(1)
     chunk = pl.num_programs(1) - 1 - step
     span = range(heads)
+    width = carry.shape[1]
 
     @pl.when(step == 0)
     def _():
@@ -275,21 +275,28 @@
     places = chunk_places(info_ref, micro, chunk, seq_count)
     row_ids, col_ids = places["row_ids"], places["col_ids"]
     lags = places["lags"]
-    dec = dec_ref[...]
+    dec = x_ref[:, width:]
     beta_all = jax.nn.sigmoid(dec)
     shifted_dec = dec + par_ref[1:2, :]
     g_all = par_ref[0:1, :] * softplus(shifted_dec)
     scale = key_size**-0.5
-    opening = jnp.where(chunk == 0, rim_ref[0].astype(F32), before_ref[...].astype(F32))
+    opening = jnp.where(chunk == 0, rim_ref[:, :width], before_ref[:, :width])
+    opening = opening.astype(BF16).astype(F32)
 
     def extended_rows(cut):
-        return jnp.concatenate([opening[:, cut], x_ref[:, cut].astype(F32)], axis=0)
+        return jnp.concatenate(
+            [opening[:, cut], x_ref[:, cut].astype(BF16).astype(F32)], axis=0
+        )
 
     sums, norms, unit = [], [], []
     for head in span:
         mine = [
-            conv_rows(extended_rows(slice(begin, begin + width)), taps_ref[0:KCONV, begin : begin + width], lags)
-            for begin, width in head_columns(head, heads, key_size, value_size)
+            conv_rows(
+                extended_rows(slice(begin, begin + size)),
+                taps_ref[0:KCONV, begin : begin + size],
+                lags,
+            )
+            for begin, size in head_columns(head, heads, key_size, value_size)
         ]
         active = [value * jax.nn.sigmoid(value) for value in mine]
         inverse_norms = [
@@ -403,11 +410,10 @@
         )
     dstep = dg_all * par_ref[0:1, :] * jax.nn.sigmoid(shifted_dec)
     ddec = ddec + dstep
-    ddec_ref[...] = ddec.astype(BF16)
+    dx_ref[:, width:] = ddec.astype(BF16)
     dpar_ref[0:1, :] += jnp.sum(dg_all * g_all, axis=0, keepdims=True)
     dpar_ref[1:2, :] += jnp.sum(dstep, axis=0, keepdims=True)
 
-    edge = jnp.zeros((8, 1), F32)
     for head in span:
         dunit = [dquery[head] * scale, dkey[head]]
         dactive = [
@@ -419,13 +425,13 @@
             for at in range(2)
         ]
         dactive.append(betas[head] * dresidue[head])
-        for at, (begin, width) in enumerate(head_columns(head, heads, key_size, value_size)):
-            cut = slice(begin, begin + width)
+        for at, (begin, size) in enumerate(head_columns(head, heads, key_size, value_size)):
+            cut = slice(begin, begin + size)
             sig = jax.nn.sigmoid(sums[head][at])
             dsum = dactive[at] * sig * (1.0 + sums[head][at] * (1.0 - sig))
             extended = extended_rows(cut)
             taps = taps_ref[0:KCONV, cut]
-            zeros = jnp.zeros((8, width), F32)
+            zeros = jnp.zeros((8, size), F32)
             dtaps_ref[KCONV - 1 : KCONV, cut] += jnp.sum(
                 dsum * extended[HALO:], axis=0, keepdims=True
             )
@@ -519,15 +525,23 @@
 
 
 VMEM_BYTES = 48 * 1024 * 1024
-
-
-def kernel_call(kernel, info, arrays, grid, in_specs, out_specs, out_shape, scratch, name, **sizes):
+PIECES = 4
+
+
+def kernel_call(
+    kernel, info, arrays, grid, in_specs, out_specs, out_shape, scratch, name, after=(), **sizes
+):
+    count = 1 + len(arrays)
+
+    def body(*refs):
+        kernel(*refs[:count], *refs[count + len(after) :], **sizes)
+
     return pl.pallas_call(
-        partial(kernel, **sizes),
+        body,
         grid_spec=pltpu.PrefetchScalarGridSpec(
             num_scalar_prefetch=1,
             grid=grid,
-            in_specs=in_specs,
+            in_specs=list(in_specs) + [pl.BlockSpec(memory_space=pl.ANY)] * len(after),
             out_specs=out_specs,
             scratch_shapes=scratch,
         ),
@@ -536,7 +550,290 @@
             dimension_semantics=("arbitrary",) * len(grid), vmem_limit_bytes=VMEM_BYTES
         ),
         name=name,
-    )(info, *arrays)
+    )(info, *arrays, *after)
+
+
+def tie(value, *earlier):
+    if not earlier:
+        return value
+    return pl.pallas_call(
+        lambda *refs: None,
+        out_shape=jax.ShapeDtypeStruct(value.shape, value.dtype),
+        in_specs=[pl.BlockSpec(memory_space=pl.ANY)] * (1 + len(earlier)),
+        out_specs=pl.BlockSpec(memory_space=pl.ANY),
+        input_output_aliases={0: 0},
+        name="tie",
+    )(value, *earlier)
+
+
+ANYWHERE = pl.BlockSpec(memory_space=pl.ANY)
+
+
+def assemble(plan, arrays, after=()):
+    count = len(arrays)
+    steps = [(out, *part) for out, (_, parts) in enumerate(plan) for part in parts]
+
+    def kernel(*refs):
+        targets = refs[count + len(after) :][: len(plan)]
+        held = refs[count + len(after) + len(plan) : -2]
+        into, back = refs[-2:]
+
+        def place(buffers, out, rows, columns, row, column):
+            return buffers[out].at[
+                row : row + rows[1] - rows[0], column : column + columns[1] - columns[0]
+            ]
+
+        loads, stores = [], []
+        for at, (out, which, rows, columns, row, column) in enumerate(steps):
+            source = refs[which].at[rows[0] : rows[1], columns[0] : columns[1]]
+            target = place(held, out, rows, columns, row, column)
+            loads.append(pltpu.make_async_copy(source, target, into.at[at]))
+            loads[-1].start()
+        for at, (out, _, rows, columns, row, column) in enumerate(steps):
+            loads[at].wait()
+            source = place(held, out, rows, columns, row, column)
+            target = place(targets, out, rows, columns, row, column)
+            stores.append(pltpu.make_async_copy(source, target, back.at[at]))
+            stores[-1].start()
+        for store in stores:
+            store.wait()
+
+    return pl.pallas_call(
+        kernel,
+        out_shape=[jax.ShapeDtypeStruct(shape, arrays[0].dtype) for shape, _ in plan],
+        in_specs=[ANYWHERE] * (count + len(after)),
+        out_specs=[ANYWHERE] * len(plan),
+        scratch_shapes=[pltpu.VMEM(shape, arrays[0].dtype) for shape, _ in plan]
+        + [pltpu.SemaphoreType.DMA((len(steps),))] * 2,
+        compiler_params=pltpu.CompilerParams(vmem_limit_bytes=VMEM_BYTES),
+        name="assemble",
+    )(*arrays, *after)
+
+
+def stacked(arrays, after=()):
+    rows, parts = 0, []
+    for at, array in enumerate(arrays):
+        parts.append((at, (0, array.shape[0]), (0, array.shape[1]), rows, 0))
+        rows += array.shape[0]
+    return assemble([((rows, arrays[0].shape[1]), parts)], arrays, after)[0]
+
+
+def ring_add(ups, downs, left, right, partly, after=()):
+    count = len(ups)
+    total = sum(grad.shape[1] for grad, _ in ups)
+    tile = left.shape[0] if partly else left.shape[0] // 2
+
+    def kernel(*refs):
+        mine_up, mine_down = refs[:count], refs[count : 2 * count]
+        came_up, came_down = refs[2 * count : 2 * count + 2]
+        out_up, out_down = refs[-2:]
+        step = pl.program_id(0)
+        column = 0
+        for up, down in zip(mine_up, mine_down):
+            cut = slice(column, column + up.shape[1])
+            column += up.shape[1]
+            for mine, came, out, when in ((up, came_up, out_up, 0), (down, came_down, out_down, 1)):
+
+                def add(mine=mine, came=came, out=out, cut=cut):
+                    out[:, cut] = (mine[...].astype(F32) + came[:, cut].astype(F32)).astype(BF16)
+
+                def keep(mine=mine, out=out, cut=cut):
+                    out[:, cut] = mine[...]
+
+                if partly:
+                    pl.when(step == when)(add)
+                    pl.when(step != when)(keep)
+                else:
+                    add()
+
+    def of_block(grad, at):
+        return pl.BlockSpec((tile, grad.shape[1]), lambda i: (2 * at + i, 0))
+
+    came = pl.BlockSpec((tile, total), lambda i: (0 if partly else i, 0))
+    out = pl.BlockSpec((tile, total), lambda i: (i, 0))
+    shape = jax.ShapeDtypeStruct((2 * tile, total), BF16)
+    return pl.pallas_call(
+        kernel,
+        grid=(2,),
+        out_shape=[shape, shape],
+        in_specs=[of_block(*block) for block in ups]
+        + [of_block(*block) for block in downs]
+        + [came, came]
+        + [ANYWHERE] * len(after),
+        out_specs=[out, out],
+        compiler_params=pltpu.CompilerParams(
+            dimension_semantics=("arbitrary",), vmem_limit_bytes=VMEM_BYTES
+        ),
+        name="ring_add",
+    )(*[grad for grad, _ in ups], *[grad for grad, _ in downs], left, right, *after)
+
+
+def row_blocks(left, right, blocks, count, after=()):
+    size = left.shape[1] // count
+
+    def kernel(left_ref, right_ref, *refs):
+        refs[-1][...] = lax.dot_general(
+            left_ref[...], right_ref[...], TN, preferred_element_type=F32
+        ).astype(BF16)
+
+    def block(i):
+        found = blocks[0]
+        for at, wanted in enumerate(blocks[1:], 1):
+            found = jnp.where(i >= at, wanted, found)
+        return 0, found
+
+    return pl.pallas_call(
+        kernel,
+        grid=(len(blocks),),
+        in_specs=[
+            pl.BlockSpec((left.shape[0], size), block),
+            pl.BlockSpec(right.shape, lambda i: (0, 0)),
+        ]
+        + [ANYWHERE] * len(after),
+        out_specs=pl.BlockSpec((size, right.shape[1]), lambda i: (i, 0)),
+        out_shape=jax.ShapeDtypeStruct((len(blocks) * size, right.shape[1]), BF16),
+        compiler_params=pltpu.CompilerParams(
+            dimension_semantics=("arbitrary",), vmem_limit_bytes=VMEM_BYTES
+        ),
+        name="row_blocks",
+    )(left, right, *after)
+
+
+def matmul(pairs, dims, dtype, after=(), pieces=0):
+    if dims == NT:
+        rows, columns = pairs[0][0].shape[0], pairs[0][1].shape[0]
+        tile = 512 if columns % 512 == 0 else columns
+        grid, pick = columns // tile, lambda i: (0, i)
+        specs = [
+            (pl.BlockSpec(left.shape, lambda i: (0, 0)),
+             pl.BlockSpec((tile, right.shape[1]), lambda i: (i, 0)))
+            for left, right in pairs
+        ]
+        shape = (rows, tile)
+    else:
+        over = 1 if dims == TN else 0
+        rows, columns = pairs[0][0].shape[over], pairs[0][1].shape[1]
+        tile = 256
+        grid, pick = rows // tile, lambda i: (i, 0)
+        specs = [
+            (pl.BlockSpec((left.shape[0], tile), lambda i: (0, i)) if dims == TN
+             else pl.BlockSpec((tile, left.shape[1]), lambda i: (i, 0)),
+             pl.BlockSpec(right.shape, lambda i: (0, 0)))
+            for left, right in pairs
+        ]
+        shape = (tile, columns)
+    count = 2 * len(pairs)
+    half = rows // 2
+
+    def kernel(*refs):
+        total = None
+        for at in range(0, count, 2):
+            product = lax.dot_general(
+                refs[at][...], refs[at + 1][...], dims, preferred_element_type=F32
+            )
+            total = product if total is None else total + product
+        outs = refs[count + len(after) :]
+        if pieces:
+            outs[0][...] = total[:half].astype(dtype)
+            for at in range(pieces):
+                first = half + at * (half // pieces)
+                outs[1 + at][...] = total[first : first + half // pieces].astype(dtype)
+        else:
+            outs[0][...] = total.astype(dtype)
+
+    if pieces:
+        heights = [half] + [half // pieces] * pieces
+        out_specs = [pl.BlockSpec((height, tile), pick) for height in heights]
+        out_shape = [jax.ShapeDtypeStruct((height, columns), dtype) for height in heights]
+    else:
+        out_specs = [pl.BlockSpec(shape, pick)]
+        out_shape = [jax.ShapeDtypeStruct((rows, columns), dtype)]
+    found = pl.pallas_call(
+        kernel,
+        grid=(grid,),
+        in_specs=[spec for both in specs for spec in both] + [ANYWHERE] * len(after),
+        out_specs=out_specs,
+        out_shape=out_shape,
+        compiler_params=pltpu.CompilerParams(
+            dimension_semantics=("arbitrary",), vmem_limit_bytes=VMEM_BYTES
+        ),
+        name="matmul",
+    )(*[array for both in pairs for array in both], *after)
+    return found if pieces else found[0]
+
+
+def project(rows, rim, weights, after=()):
+    tile = 256
+
+    def kernel(rows_ref, rim_ref, weights_ref, *refs):
+        out, out_rim = refs[-2:]
+        out[...] = jnp.dot(rows_ref[...], weights_ref[...], preferred_element_type=F32)
+
+        @pl.when(pl.program_id(0) == 0)
+        def _():
+            out_rim[...] = jnp.dot(rim_ref[...], weights_ref[...], preferred_element_type=F32)
+
+    columns = weights.shape[1]
+    return pl.pallas_call(
+        kernel,
+        grid=(rows.shape[0] // tile,),
+        in_specs=[
+            pl.BlockSpec((tile, rows.shape[1]), lambda i: (i, 0)),
+            pl.BlockSpec(rim.shape, lambda i: (0, 0)),
+            pl.BlockSpec(weights.shape, lambda i: (0, 0)),
+        ]
+        + [ANYWHERE] * len(after),
+        out_specs=[
+            pl.BlockSpec((tile, columns), lambda i: (i, 0)),
+            pl.BlockSpec((rim.shape[0], columns), lambda i: (0, 0)),
+        ],
+        out_shape=[
+            jax.ShapeDtypeStruct((rows.shape[0], columns), F32),
+            jax.ShapeDtypeStruct((rim.shape[0], columns), F32),
+        ],
+        compiler_params=pltpu.CompilerParams(
+            dimension_semantics=("arbitrary",), vmem_limit_bytes=VMEM_BYTES
+        ),
+        name="project",
+    )(rows, rim, weights, *after)
+
+
+def feed_forward(rows, cotangent, w_ffn, w_down, after=()):
+    tile = 256
+    model, width = w_down.shape
+
+    def kernel(rows_ref, cotangent_ref, ffn_ref, down_ref, *refs):
+        hidden_ref, grad_ref = refs[-2:]
+        gate = jnp.dot(rows_ref[...], ffn_ref[:, :width], preferred_element_type=F32)
+        up = jnp.dot(rows_ref[...], ffn_ref[:, width:], preferred_element_type=F32)
+        grad = jnp.dot(cotangent_ref[...], down_ref[...], preferred_element_type=F32)
+        sig = jax.nn.sigmoid(gate)
+        active = gate * sig
+        hidden_ref[...] = (active * up).astype(BF16)
+        grad_ref[:, :width] = (grad * up * sig * (1.0 + gate * (1.0 - sig))).astype(BF16)
+        grad_ref[:, width:] = (grad * active).astype(BF16)
+
+    def by_rows(columns):
+        return pl.BlockSpec((tile, columns), lambda i: (i, 0))
+
+    def once(array):
+        return pl.BlockSpec(array.shape, lambda i: (0, 0), pipeline_mode=pl.Buffered(1))
+
+    return pl.pallas_call(
+        kernel,
+        grid=(rows.shape[0] // tile,),
+        in_specs=[by_rows(model), by_rows(model), once(w_ffn), once(w_down)]
+        + [ANYWHERE] * len(after),
+        out_specs=[by_rows(width), by_rows(2 * width)],
+        out_shape=[
+            jax.ShapeDtypeStruct((rows.shape[0], width), BF16),
+            jax.ShapeDtypeStruct((rows.shape[0], 2 * width), BF16),
+        ],
+        compiler_params=pltpu.CompilerParams(
+            dimension_semantics=("arbitrary",), vmem_limit_bytes=VMEM_BYTES
+        ),
+        name="feed_forward",
+    )(rows, cotangent, w_ffn, w_down, *after)
 
 
 class Mix:
@@ -549,7 +846,7 @@
         self.sizes = dict(heads=heads, key_size=key_size, value_size=value_size)
 
     def block(self, m, c, info):
-        return m * self.chunks + jnp.bitwise_xor(c, info[0, info.shape[1] - 1])
+        return rank_block(c, info[0, info.shape[1] - 1]) * self.micros + m
 
     def by_rows(self, columns, turned=False):
         def place(m, c, info):
@@ -572,7 +869,7 @@
     def like(self, dtype, *dims):
         return jax.ShapeDtypeStruct(dims, dtype)
 
-    def call(self, kernel, arrays, in_specs, outs, scratch, name, **more):
+    def call(self, kernel, arrays, in_specs, outs, scratch, name, after, **more):
         return kernel_call(
             kernel,
             self.info,
@@ -583,20 +880,20 @@
             [shape for _, shape in outs],
             scratch,
             name,
+            after,
             **self.sizes,
             **more,
         )
 
-    def forward(self, pre_conv, rim, dec, taps, par):
+    def forward(self, projected, rim, taps, par, after=()):
         h, dk, dv, wide, width = self.heads, self.key_size, self.value_size, self.wide, self.width
         steps = self.micros * self.chunks
         return self.call(
             mix_forward_kernel,
-            (pre_conv, rim, dec, taps, par),
+            (projected, rim, taps, par),
             [
-                self.by_rows(width),
-                self.by_micro(HALO, width),
-                self.by_rows(LANES),
+                self.by_rows(width + LANES),
+                pl.BlockSpec((HALO, width + LANES), lambda m, c, info: (m, 0)),
                 self.whole(8, width),
                 self.whole(8, LANES),
             ],
@@ -609,10 +906,13 @@
             ],
             [pltpu.VMEM((HALO, width), BF16), pltpu.VMEM((h, dk, wide), F32)],
             "mix_forward",
+            after,
             seq_count=self.info.shape[1] - 2,
         )
 
-    def backward(self, pre_conv, rim, dec, taps, par, grad, inverses, starts, incoming, leaving):
+    def backward(
+        self, projected, rim, taps, par, grad, inverses, starts, incoming, leaving, after=()
+    ):
         h, dk, dv, wide, width = self.heads, self.key_size, self.value_size, self.wide, self.width
         halo_blocks = CHUNK // HALO
 
@@ -622,12 +922,11 @@
 
         return self.call(
             mix_backward_kernel,
-            (pre_conv, pre_conv, rim, dec, taps, par, grad, inverses, starts, incoming, leaving),
+            (projected, projected, rim, taps, par, grad, inverses, starts, incoming, leaving),
             [
-                self.by_rows(width, True),
-                pl.BlockSpec((HALO, width), before),
-                self.by_micro(HALO, width),
-                self.by_rows(LANES, True),
+                self.by_rows(width + LANES, True),
+                pl.BlockSpec((HALO, width + LANES), before),
+                pl.BlockSpec((HALO, width + LANES), lambda m, c, info: (m, 0)),
                 self.whole(8, width),
                 self.whole(8, LANES),
                 self.by_rows(h * dv, True),
@@ -637,19 +936,19 @@
                 self.by_micro(h, dk, dv),
             ],
             [
-                (self.by_rows(width, True), self.like(BF16, self.rows, width)),
+                (self.by_rows(width + LANES, True), self.like(BF16, self.rows, width + LANES)),
                 (self.by_micro(8, width), self.like(F32, self.micros, 8, width)),
                 (self.by_micro(HALO, width), self.like(F32, self.micros, HALO, width)),
-                (self.by_rows(LANES, True), self.like(BF16, self.rows, LANES)),
                 (self.whole(8, width), self.like(F32, 8, width)),
                 (self.whole(8, LANES), self.like(F32, 8, LANES)),
             ],
             [pltpu.VMEM((8, width), F32), pltpu.VMEM((h, dk, dv), F32)],
             "mix_backward",
+            after,
             seq_count=self.info.shape[1] - 2,
         )
 
-    def gate_forward(self, plain, cmap, incoming, gate, gain):
+    def gate_forward(self, plain, cmap, incoming, gate, gain, after=()):
         h, dk, dv = self.heads, self.key_size, self.value_size
         return self.call(
             gate_forward_kernel,
@@ -667,9 +966,10 @@
             ],
             [],
             "gate_forward",
-        )
-
-    def gate_backward(self, grad, mixed, cmap, gate, gain):
+            after,
+        )
+
+    def gate_backward(self, grad, mixed, cmap, gate, gain, after=()):
         h, dk, dv = self.heads, self.key_size, self.value_size
         return self.call(
             gate_backward_kernel,
@@ -689,6 +989,7 @@
             ],
             [],
             "gate_backward",
+            after,
         )
 
 
@@ -702,17 +1003,89 @@
     return lax.ppermute(value, axis, [(at, at ^ bit) for at in range(lax.axis_size(axis))])
 
 
-def head_gather(value):
-    across = swap(value, "head", 2)
-    both = swap(jnp.stack([value, across], axis=1), "head", 1)
-    return jnp.stack([value, both[:, 0], across, both[:, 1]], axis=1)
-
-
-def head_scatter(parts):
-    near = swap(jnp.stack([parts[:, 1], parts[:, 3]], axis=1).astype(BF16), "head", 1)
-    mine = parts[:, 0].astype(F32) + near[:, 0].astype(F32)
-    theirs = parts[:, 2].astype(F32) + near[:, 1].astype(F32)
-    return mine + swap(theirs.astype(BF16), "head", 2).astype(F32)
+def rank_block(rank, mine):
+    apart = jnp.bitwise_xor(rank, mine)
+    return 2 * jnp.bitwise_and(apart, 1) + jnp.right_shift(apart, 1)
+
+
+def cut_rows(value, count):
+    size = value.shape[0] // count
+    return [value[at * size : (at + 1) * size] for at in range(count)]
+
+
+class HeadGather:
+    def __init__(self, value):
+        self.value = value
+        self.across = [swap(part, "head", 2) for part in cut_rows(value, PIECES // 2)]
+
+    def pass_on(self, *after):
+        self.pair = stacked([self.value, *self.across], after)
+        self.near = [swap(part, "head", 1) for part in cut_rows(self.pair, PIECES)]
+        return (self.pair,)
+
+    def rows(self, *after):
+        return stacked([self.pair, *self.near], after)
+
+
+class HeadScatter:
+    def __init__(self, mine, *sent):
+        self.pieces = max(len(sent), 2)
+        self.mine, self.sent = cut_rows(mine, self.pieces), sent
+        self.near = [swap(part, "head", 1) for part in sent]
+
+    def pass_on(self, *after):
+        half = self.pieces // 2
+        self.near = [tie(part, *after) for part in self.near]
+        if len(self.near) == 1:
+            self.near = cut_rows(self.near[0], 2)
+        theirs = [
+            (mine.astype(F32) + near.astype(F32)).astype(BF16)
+            for mine, near in zip(self.mine[half:], self.near[half:])
+        ]
+        self.across = [swap(part, "head", 2) for part in theirs]
+        return tuple(theirs)
+
+    def total(self, *after):
+        parts = zip(self.mine, self.near, self.across)
+        return jnp.concatenate(
+            [
+                mine.astype(F32) + near.astype(F32) + tie(across, *after).astype(F32)
+                for mine, near, across in parts
+            ],
+            axis=0,
+        )
+
+
+class Summed:
+    def __init__(self, value, hops):
+        self.value, self.hops, self.came = value, list(hops), []
+
+    def step(self, *after):
+        if not self.came and after:
+            self.value = tie(self.value, *after)
+        for came in self.came:
+            self.value = self.value + tie(came, *after)
+        self.came = []
+        if self.hops:
+            axis, turns = self.hops.pop(0)
+            self.came = [swap(self.value, axis, turn) for turn in turns]
+        return (self.value,)
+
+    def total(self):
+        while self.came:
+            self.step()
+        return self.value
+
+
+def head_hops():
+    return [("head", [1 << at]) for at in range((lax.axis_size("head") - 1).bit_length())]
+
+
+def dp_hops():
+    count = lax.axis_size("dp")
+    if count <= 8:
+        return [("dp", [1]), ("dp", list(range(2, count, 2)))]
+    return [("dp", [1 << at]) for at in range((count - 1).bit_length())]
 
 
 def ring_order():
@@ -731,80 +1104,171 @@
     return ahead, [(after, before) for before, after in ahead]
 
 
-def to_ring(value):
+def reorder_kernel(order_ref, *refs, size, outward):
+    count = len(refs) // 2
+    for source, target in zip(refs[:count], refs[count:]):
+        for at in range(order_ref.shape[0]):
+            moved = pl.ds(pl.multiple_of(order_ref[at] * size, size), size)
+            here = slice(at * size, (at + 1) * size)
+            if outward:
+                target[:, moved] = source[:, here]
+            else:
+                target[:, here] = source[:, moved]
+
+
+def reorder(arrays, outward, after=()):
     ring = ring_order()
-    size = value.shape[-1] // len(ring)
-    parts = [value[..., rank * size : (rank + 1) * size] for rank in ring]
-    twice = jnp.concatenate(parts + parts[:-1], axis=-1)
-    return lax.dynamic_slice_in_dim(twice, ring_place() * size, value.shape[-1], value.ndim - 1)
-
-
-def from_ring(value):
-    ring = ring_order()
-    count = len(ring)
-    size = value.shape[-1] // count
-    start = jnp.where(ring_place() == 0, 0, count - ring_place())
-    turned = lax.dynamic_slice_in_dim(
-        jnp.concatenate([value, value[..., : (count - 1) * size]], axis=-1),
-        start * size,
-        value.shape[-1],
-        value.ndim - 1,
-    )
-    parts = [None] * count
-    for at, rank in enumerate(ring):
-        parts[rank] = turned[..., at * size : (at + 1) * size]
-    return jnp.concatenate(parts, axis=-1)
-
-
-def ring_gather(shard, axis):
-    ahead, back = ring_steps()
-    count = len(ahead)
-    from_left, from_right = [shard], [shard]
-    for _ in range(1, count // 2):
-        from_left.append(lax.ppermute(from_left[-1], "dp", ahead))
-        from_right.append(lax.ppermute(from_right[-1], "dp", back))
-    half = shard.shape[0] // 2
-    far = jnp.concatenate(
-        [
-            lax.ppermute(from_left[-1][:half], "dp", ahead),
-            lax.ppermute(from_right[-1][half:], "dp", back),
-        ],
-        axis=0,
-    )
-    return jnp.concatenate(from_right + [far] + from_left[:0:-1], axis=axis), far
-
-
-def ring_scatter(blocks):
-    ahead, back = ring_steps()
-    count = len(ahead)
-    half = blocks[0].shape[0] // 2
-    middle = count // 2
-
-    def add(one, other):
-        return one.astype(F32) + other.astype(F32)
-
-    left = lax.ppermute(blocks[middle][:half], "dp", ahead)
-    right = lax.ppermute(blocks[middle][half:], "dp", back)
-    for at in range(middle - 1, 0, -1):
-        up, down = blocks[at], blocks[count - at]
-        if at == middle - 1:
-            up = jnp.concatenate([add(up[:half], left).astype(BF16), up[half:]], axis=0)
-            down = jnp.concatenate([down[:half], add(down[half:], right).astype(BF16)], axis=0)
+    count, place = len(ring), ring_place()
+    size = arrays[0].shape[1] // count
+    around = jnp.asarray(ring + ring, jnp.int32)
+    order = lax.dynamic_slice(around, (place,), (count,))
+    if size % LANES == 0:
+        return kernel_call(
+            reorder_kernel,
+            order,
+            arrays,
+            (1,),
+            [pl.BlockSpec(a.shape, lambda i, info: (0, 0)) for a in arrays],
+            [pl.BlockSpec(a.shape, lambda i, info: (0, 0)) for a in arrays],
+            [jax.ShapeDtypeStruct(a.shape, a.dtype) for a in arrays],
+            [],
+            "reorder",
+            after,
+            size=size,
+            outward=outward,
+        )
+    if outward:
+        ranks = jnp.arange(count, dtype=jnp.int32)
+        order = jnp.sum(jnp.where(order[None, :] == ranks[:, None], ranks[None, :], 0), axis=1)
+    return [
+        jnp.take(a.reshape(-1, count, size), order, axis=1).reshape(a.shape) for a in arrays
+    ]
+
+
+class Gather:
+    def __init__(self, shard):
+        self.ahead, self.back = ring_steps()
+        self.left, self.right, self.far = [shard], [shard], None
+
+    def step(self, *after):
+        if len(self.left) > 1 or after:
+            self.left[-1] = tie(self.left[-1], *after)
+            self.right[-1] = self.left[0] if len(self.left) == 1 else tie(self.right[-1], *after)
+        sent = self.left[-1], self.right[-1]
+        if len(self.left) < len(self.ahead) // 2:
+            self.left.append(lax.ppermute(self.left[-1], "dp", self.ahead))
+            self.right.append(lax.ppermute(self.right[-1], "dp", self.back))
         else:
-            up, down = add(up, left).astype(BF16), add(down, right).astype(BF16)
-        left = lax.ppermute(up, "dp", ahead)
-        right = lax.ppermute(down, "dp", back)
-    return add(blocks[0], left) + right.astype(F32)
-
-
-def scatter_rows(grad):
-    size = grad.shape[0] // lax.axis_size("dp")
-    return ring_scatter([grad[at : at + size] for at in range(0, grad.shape[0], size)])
-
-
-def scatter_columns(grad):
-    size = grad.shape[1] // lax.axis_size("dp")
-    return ring_scatter([grad[:, at : at + size] for at in range(0, grad.shape[1], size)])
+            half = self.left[0].shape[0] // 2
+            self.far = [
+                lax.ppermute(self.left[-1][:half], "dp", self.ahead),
+                lax.ppermute(self.right[-1][half:], "dp", self.back),
+            ]
+        return sent
+
+    def run(self, *after):
+        while self.far is None:
+            after = self.step(*after)
+        return after
+
+    def came(self):
+        return self.left[-1], self.right[-1]
+
+    def parts(self):
+        return [self.left[0]] + self.right[1:] + self.far + self.left[:0:-1]
+
+
+def gathered(wanted, after=()):
+    rings = []
+    for cuts in wanted:
+        rings += [ring for ring, _, _ in cuts if ring not in rings]
+    arrays, first = [], {}
+    for ring in rings:
+        first[ring] = len(arrays)
+        arrays += ring.parts()
+    plan = []
+    for cuts in wanted:
+        column, items = 0, []
+        for ring, low, high in cuts:
+            row = 0
+            for at, part in enumerate(ring.parts()):
+                items.append((first[ring] + at, (0, part.shape[0]), (low, high), row, column))
+                row += part.shape[0]
+            column += high - low
+        plan.append(((row, column), items))
+    return assemble(plan, arrays, after)
+
+
+class Scatter:
+    def __init__(self, *pairs, after=()):
+        self.ahead, self.back = ring_steps()
+        self.pairs, self.count = pairs, len(self.ahead)
+        self.size = pairs[0][0].shape[1] // self.count
+        self.apart = self.size % LANES == 0
+        self.at = middle = self.count // 2
+        self.left = self.right = None
+        self.blocks = [{} for _ in pairs]
+        self.groups = [[middle]]
+        if self.count > 4:
+            self.groups.append([middle - 1, middle + 1])
+        self.groups.append([at for at in range(self.count) if all(at not in g for g in self.groups)])
+        if self.apart:
+            self.work(0, after=after)
+        else:
+            for which, pair in enumerate(pairs):
+                whole = matmul([pair], TN, BF16, after)
+                self.blocks[which] = {at: (whole, at) for at in range(self.count)}
+
+    def work(self, group, only=None, after=()):
+        found = []
+        for which, pair in enumerate(self.pairs):
+            if self.apart and only in (None, which):
+                found.append(row_blocks(*pair, self.groups[group], self.count, after))
+                for place, at in enumerate(self.groups[group]):
+                    self.blocks[which][at] = (found[-1], place)
+        return tuple(found) or tuple(after)
+
+    def of(self, at):
+        return [blocks[at] for blocks in self.blocks]
+
+    def step(self, *after):
+        middle, half = self.count // 2, self.size // 2
+        if self.at == middle:
+            plan, arrays = [], [grad for grad, _ in self.of(middle)]
+            for start in (0, half):
+                column, items = 0, []
+                for at, (grad, place) in enumerate(self.of(middle)):
+                    first, width = place * self.size + start, grad.shape[1]
+                    items.append((at, (first, first + half), (0, width), 0, column))
+                    column += width
+                plan.append(((half, column), items))
+            up, down = assemble(plan, arrays, after)
+        else:
+            up, down = ring_add(
+                self.of(self.at),
+                self.of(self.count - self.at),
+                self.left,
+                self.right,
+                self.at == middle - 1,
+                after,
+            )
+        self.left = lax.ppermute(up, "dp", self.ahead)
+        self.right = lax.ppermute(down, "dp", self.back)
+        self.at -= 1
+        return up, down
+
+    def came(self):
+        return self.left, self.right
+
+    def total(self, *after):
+        while self.at > 0:
+            after = self.step(*after)
+        mine = [
+            grad[place * self.size : (place + 1) * self.size] for grad, place in self.of(0)
+        ]
+        mine = mine[0] if len(mine) == 1 else jnp.concatenate(mine, axis=1)
+        left, right = tie(self.left, *after), tie(self.right, *after)
+        return mine.astype(F32) + left.astype(F32) + right.astype(F32)
 
 
 def apply_map(moves, state, turned=False):
@@ -817,51 +1281,86 @@
 
 
 def own_and_swapped(value, bit):
-    theirs = swap(jnp.where(bit == 0, value[1], value[0]).astype(BF16), "dp", 1)
+    sent = jnp.where(bit == 0, value[1], value[0]).astype(BF16)
+    theirs = swap(sent, "dp", 1).astype(F32)
     mine = jnp.where(bit == 0, value[0], value[1]).astype(F32)
-    theirs = theirs.astype(F32)
-    return jnp.where(bit == 0, mine, theirs), jnp.where(bit == 0, theirs, mine)
+    return jnp.where(bit == 0, mine, theirs), jnp.where(bit == 0, theirs, mine), sent
 
 
 def hand_back(first, second, bit):
     mine = jnp.where(bit == 0, first, second).astype(BF16)
-    theirs = swap(jnp.where(bit == 0, second, first).astype(BF16), "dp", 1)
-    return jnp.stack([jnp.where(bit == 0, mine, theirs), jnp.where(bit == 0, theirs, mine)])
-
-
-def scan_forward(final, value_size):
-    bit, pairs = lax.axis_index("dp") % 2, lax.axis_size("dp") // 2
-    first, second = own_and_swapped(final, bit)
-    first_map, second_map = first[..., value_size:], second[..., value_size:]
-    pair_map = apply_map(second_map, first_map)
-    pair_sum = apply_map(second_map, first[..., :value_size]) + second[..., :value_size]
-    state = jnp.zeros(pair_sum.shape, F32)
-    for _ in range(pairs - 1):
-        state = from_behind((apply_map(pair_map, state) + pair_sum).astype(BF16), "dp", 2).astype(F32)
-    after_first = apply_map(first_map, state) + first[..., :value_size]
-    return hand_back(state, after_first, bit), (first_map, second_map, pair_map)
-
-
-def scan_backward(local, maps):
-    bit, pairs = lax.axis_index("dp") % 2, lax.axis_size("dp") // 2
-    first_map, second_map, pair_map = maps
-    first, second = own_and_swapped(local, bit)
-    pair_sum = apply_map(first_map, second, True) + first
-    state = jnp.zeros(pair_sum.shape, F32)
-    for _ in range(pairs - 1):
-        state = from_behind(
-            (apply_map(pair_map, state, True) + pair_sum).astype(BF16), "dp", -2
-        ).astype(F32)
-    before_second = apply_map(second_map, state, True) + second
-    return hand_back(before_second, state, bit)
-
-
-def contract_rows(left, right):
-    return lax.dot_general(left, right, TN, preferred_element_type=F32)
-
-
-def contract_cols(left, right):
-    return lax.dot_general(left, right, NT, preferred_element_type=F32)
+    sent = jnp.where(bit == 0, second, first).astype(BF16)
+    theirs = swap(sent, "dp", 1)
+    return jnp.stack([jnp.where(bit == 0, mine, theirs), jnp.where(bit == 0, theirs, mine)]), sent
+
+
+class Scan:
+    def __init__(self, final, value_size):
+        self.bit, self.pairs = lax.axis_index("dp") % 2, lax.axis_size("dp") // 2
+        self.cut = value_size
+        self.sent = jnp.where(self.bit == 0, final[1], final[0]).astype(BF16)
+        self.mine = jnp.where(self.bit == 0, final[0], final[1]).astype(F32)
+        self.theirs = swap(self.sent, "dp", 1)
+
+    def ordered(self, *after):
+        theirs = tie(self.theirs, *after).astype(F32)
+        return (
+            jnp.where(self.bit == 0, self.mine, theirs),
+            jnp.where(self.bit == 0, theirs, self.mine),
+        )
+
+    def shifted(self, value, steps):
+        return [from_behind(value, "dp", 2 * sign) for sign in steps]
+
+    def send(self, *after):
+        self.first, self.second = self.ordered(*after)
+        cut = self.cut
+        self.first_map, self.second_map = self.first[..., cut:], self.second[..., cut:]
+        pair_map = apply_map(self.second_map, self.first_map)
+        self.pair_map = pair_map.astype(BF16)
+        pair_sum = apply_map(self.second_map, self.first[..., :cut]) + self.second[..., :cut]
+        both = jnp.concatenate([pair_sum, pair_map], axis=-1).astype(BF16)
+        self.before = self.shifted(both, range(1, self.pairs))
+        return (both,)
+
+    def finish(self, *after):
+        state = jnp.zeros(self.first[..., : self.cut].shape, F32)
+        for both in self.before[::-1]:
+            both = tie(both, *after)
+            after = ()
+            state = apply_map(both[..., self.cut :], state) + both[..., : self.cut].astype(F32)
+        after_first = apply_map(self.first_map, state) + self.first[..., : self.cut]
+        return self.hand_back(state, after_first)
+
+    def hand_back(self, first, second):
+        mine = jnp.where(self.bit == 0, first, second).astype(BF16)
+        sent = jnp.where(self.bit == 0, second, first).astype(BF16)
+        theirs = swap(sent, "dp", 1)
+        states = [jnp.where(self.bit == 0, *pair) for pair in ((mine, theirs), (theirs, mine))]
+        return jnp.stack(states), (sent,)
+
+
+class ScanBack(Scan):
+    def __init__(self, local, ahead):
+        self.of = ahead
+        super().__init__(local, local.shape[-1])
+
+    def send(self, *after):
+        self.first, self.second = self.ordered(*after)
+        pair_sum = (apply_map(self.of.first_map, self.second, True) + self.first).astype(BF16)
+        both = jnp.concatenate([pair_sum, self.of.pair_map], axis=-1)
+        self.behind = self.shifted(both, [-step for step in range(1, self.pairs)])
+        return (both,)
+
+    def finish(self, *after):
+        state = jnp.zeros(self.first.shape, F32)
+        for both in self.behind[::-1]:
+            both = tie(both, *after)
+            after = ()
+            moves = both[..., self.cut :]
+            state = apply_map(moves, state, True) + both[..., : self.cut].astype(F32)
+        before_second = apply_map(self.of.second_map, state, True) + self.second
+        return self.hand_back(before_second, state)
 
 
 def norm_backward(grad_in, normed_rows, scale):
@@ -903,25 +1402,13 @@
     assert part_rows == CHUNK and micros == 2 and ranks == 4
 
     decay_pad = jnp.zeros((decay_proj.shape[0], LANES - 2 * heads), decay_proj.dtype)
-    w_conv, sent = ring_gather(
+    conv_ring = Gather(
         jnp.concatenate(
             [query_proj, key_proj, value_proj, decay_proj, beta_proj, decay_pad], axis=1
-        ),
-        0,
-    )
-    gate_shard, out_shard, _ = lax.optimization_barrier((gate_proj, out_proj, sent[:8, :LANES]))
-    w_gate, sent = ring_gather(gate_shard, 0)
-    w_out, also_sent = ring_gather(out_shard, 1)
-    ffn_shard, down_shard, _, _ = lax.optimization_barrier(
-        (
-            jnp.concatenate([ffn_gate, ffn_up], axis=1),
-            ffn_down,
-            sent[:8, :LANES],
-            also_sent[:8, :LANES],
-        )
-    )
-    w_ffn, _ = ring_gather(ffn_shard, 0)
-    w_down, _ = ring_gather(down_shard, 1)
+        )
+    )
+    gate_ring = Gather(jnp.concatenate([gate_proj, out_proj.T], axis=1))
+    ffn_ring = Gather(jnp.concatenate([ffn_gate, ffn_up, ffn_down.T], axis=1))
 
     def of_mine(whole, width):
         return lax.dynamic_slice_in_dim(whole, head_rank * width, width, whole.ndim - 1)
@@ -936,20 +1423,39 @@
         ((0, 6), (0, LANES - heads)),
     )
     gain = jnp.broadcast_to(head_norm, (8, value_size))
-    attn_gain, ffn_gain = to_ring(attn_norm), to_ring(ffn_norm)
 
     def flat(value):
         return value.reshape(-1, value.shape[-1])
 
     def ranked(value):
-        return value.reshape(micros, ranks, part_rows, model)
-
-    residual = to_ring(tokens).astype(F32)
+        return value.reshape(ranks, micros, part_rows, value.shape[-1])
+
+    conv_ring.step()
+    turned, cotangent, attn_gain, ffn_gain = reorder(
+        [
+            flat(tokens),
+            flat(out_grad),
+            jnp.broadcast_to(attn_norm, (8, model)),
+            jnp.broadcast_to(ffn_norm, (8, model)),
+        ],
+        False,
+    )
+    attn_gain, ffn_gain = attn_gain[0], ffn_gain[0]
+    residual = turned.astype(F32)
     scale_one = lax.rsqrt(jnp.mean(residual * residual, axis=-1, keepdims=True) + EPSILON)
     normed_one = residual * scale_one
-    normed_all = flat(head_gather((normed_one * attn_gain).astype(BF16)))
-    cotangent = to_ring(out_grad)
-    cotangent_all = flat(head_gather(cotangent))
+    normed_rows = HeadGather((normed_one * attn_gain).astype(BF16))
+    conv_ring.step()
+    (pair,) = normed_rows.pass_on(*conv_ring.came(), gate_ring.left[0], ffn_ring.left[0])
+    conv_ring.step()
+    normed_all = normed_rows.rows(*conv_ring.came())
+    last_chunk = rank_block(ranks - 1, head_rank)
+    last_rows = lax.dynamic_slice(
+        ranked(normed_all), (last_chunk, 0, part_rows - HALO, 0), (1, micros, HALO, model)
+    )
+    conv_ring.run()
+    rim_rows = from_behind(reorder([flat(last_rows)], True)[0], "dp", 1)
+    rim_rows = reorder([rim_rows], False)[0]
     first_row = lax.axis_index("dp") * ranks * part_rows
     ends = jnp.cumsum(seq_lengths, axis=1)
     info = jnp.concatenate(
@@ -961,88 +1467,137 @@
         axis=1,
     ).astype(jnp.int32)
     mix = Mix(info, micros, ranks, heads, key_size, value_size)
-    projected = jnp.dot(normed_all, w_conv, preferred_element_type=F32)
-    pre_conv = projected[:, :conv_width].astype(BF16)
-    dec = projected[:, conv_width:]
-    last_chunk = jnp.bitwise_xor(ranks - 1, head_rank)
-    last_rows = lax.dynamic_slice(
-        pre_conv.reshape(micros, ranks, part_rows, conv_width),
-        (0, last_chunk, part_rows - HALO, 0),
-        (micros, 1, HALO, conv_width),
-    )[:, 0]
-    rim = from_behind(last_rows, "dp", 1)
-
-    plain, carried_map, inverses, starts, final = mix.forward(pre_conv, rim, dec, taps, par)
-    incoming, maps = scan_forward(final, value_size)
-    gate_lin = jnp.dot(normed_all, w_gate, preferred_element_type=F32)
+    now = gate_ring.step(rim_rows, *conv_ring.far)
+    (w_conv,) = gathered([[(conv_ring, 0, conv_width + LANES)]], now)
+    projected, rim = project(normed_all, rim_rows, w_conv)
+    now = gate_ring.step(rim)
+    now = ffn_ring.step(*now)
+
+    plain, carried_map, inverses, starts, final = mix.forward(projected, rim, taps, par, now)
+    scan = Scan(final, value_size)
+    now = scan.send(scan.sent, *gate_ring.came(), *ffn_ring.came())
+    cotangent_rows = HeadGather(tie(cotangent, *now))
+    now = gate_ring.step(*now, *scan.before)
+    now = cotangent_rows.pass_on(*now)
+    incoming, now = scan.finish(*now)
+    cotangent_all = cotangent_rows.rows(*now)
+    now = gate_ring.run(*now)
+    now = ffn_ring.step(incoming, *gate_ring.far, cotangent_all)
+    w_gate, w_out = gathered(
+        [[(gate_ring, 0, v_width)], [(gate_ring, v_width, 2 * v_width)]], now
+    )
+    gate_lin = matmul([(normed_all, w_gate)], NN, F32)
     mixed, gated = mix.gate_forward(plain, carried_map, incoming, gate_lin, gain)
 
-    mix_part = jnp.dot(gated, w_out, preferred_element_type=F32)
-    after_mix = residual + head_scatter(ranked(mix_part))
+    mix_sum = HeadScatter(*matmul([(gated, w_out)], NT, BF16, pieces=PIECES))
+    now = ffn_ring.step(*mix_sum.sent)
+    now = mix_sum.pass_on(*now)
+    after_mix = residual + mix_sum.total(*now)
     scale_two = lax.rsqrt(jnp.mean(after_mix * after_mix, axis=-1, keepdims=True) + EPSILON)
     normed_two = after_mix * scale_two
-    ffn_all = flat(head_gather((normed_two * ffn_gain).astype(BF16)))
-    gate_ffn = jnp.dot(ffn_all, w_ffn[:, :ffn_width], preferred_element_type=F32)
-    up_ffn = jnp.dot(ffn_all, w_ffn[:, ffn_width:], preferred_element_type=F32)
-    ffn_sigmoid = jax.nn.sigmoid(gate_ffn)
-    ffn_active = gate_ffn * ffn_sigmoid
-    hidden = (ffn_active * up_ffn).astype(BF16)
-
-    hidden_grad = contract_cols(cotangent_all, w_down)
-    gate_ffn_grad = hidden_grad * up_ffn * ffn_sigmoid * (1.0 + gate_ffn * (1.0 - ffn_sigmoid))
-    up_ffn_grad = hidden_grad * ffn_active
-    gate_up_grad = jnp.concatenate([gate_ffn_grad, up_ffn_grad], axis=1).astype(BF16)
-    ffn_in_part = contract_cols(gate_up_grad, w_ffn)
-    ffn_in_grad = head_scatter(ranked(ffn_in_part))
-    shard_ffn = scatter_rows(contract_rows(ffn_all, gate_up_grad).astype(BF16))
-    shard_down = scatter_columns(contract_rows(hidden, cotangent_all).astype(BF16))
-    grad_norm_two = jnp.sum(ffn_in_grad * normed_two, axis=(0, 1))
+    ffn_rows = HeadGather((normed_two * ffn_gain).astype(BF16))
+    now = ffn_ring.run(ffn_rows.across[0])
+    now = ffn_rows.pass_on(*now)
+    ffn_all = ffn_rows.rows(*now)
+    w_ffn, w_down = gathered(
+        [[(ffn_ring, 0, 2 * ffn_width)], [(ffn_ring, 2 * ffn_width, 3 * ffn_width)]], (ffn_all,)
+    )
+
+    hidden, gate_up_grad = feed_forward(ffn_all, cotangent_all, w_ffn, w_down)
+    ffn_in_sum = HeadScatter(*matmul([(gate_up_grad, w_ffn)], NT, BF16, pieces=PIECES))
+    ffn_sums = Scatter(
+        (ffn_all, gate_up_grad), (cotangent_all, hidden), after=ffn_in_sum.sent
+    )
+    now = ffn_sums.step()
+    now = ffn_in_sum.pass_on(*now)
+    now = ffn_sums.work(1, after=now)
+    now = ffn_sums.step(*now)
+    ffn_in_grad = ffn_in_sum.total(*now)
+    grad_norm_two = jnp.sum(ffn_in_grad * normed_two, axis=0)
     after_mix_grad = cotangent.astype(F32) + norm_backward(
         ffn_in_grad * ffn_gain, normed_two, scale_two
     )
-
-    ffn_part = jnp.dot(hidden, w_down, preferred_element_type=F32)
-    block_out = (after_mix + head_scatter(ranked(ffn_part))).astype(BF16)
-
-    branch_grad = flat(head_gather(after_mix_grad.astype(BF16)))
-    gated_grad = contract_cols(branch_grad, w_out)
+    branch_rows = HeadGather(after_mix_grad.astype(BF16))
+    now = ffn_sums.work(2, after=(branch_rows.value,))
+    now = branch_rows.pass_on(*now)
+    branch_grad = branch_rows.rows(*now)
+    now = (branch_grad,)
+
+    gated_grad = matmul([(branch_grad, w_out)], NN, F32, now)
     gate_grad, mixed_grad, local_grad, grad_head_norm = mix.gate_backward(
-        gated_grad, mixed, carried_map, gate_lin, gain
-    )
-    shard_out = scatter_columns(contract_rows(gated, branch_grad).astype(BF16))
-
-    leaving = scan_backward(local_grad, maps)
-    shard_gate = scatter_rows(contract_rows(normed_all, gate_grad).astype(BF16))
-    pre_grad, rim_grad, tail, dec_grad, taps_grad, par_grad = mix.backward(
-        pre_conv, rim, dec, taps, par, mixed_grad, inverses, starts, incoming, leaving
+        gated_grad, mixed, carried_map, gate_lin, gain, ffn_sums.came()
+    )
+
+    back = ScanBack(local_grad, scan)
+    gate_sums = Scatter(
+        (normed_all, gate_grad), (branch_grad, gated), after=(back.sent, *ffn_sums.came())
+    )
+    now = gate_sums.work(1, after=(back.sent,)) + gate_sums.work(2, 1, (back.sent,))
+    now = back.send(*now)
+    now = gate_sums.work(2, 0, now)
+    now = gate_sums.step(*now, back.behind[-1])
+    ffn_part = matmul([(hidden, w_down)], NT, BF16, now, pieces=PIECES)
+    leaving, now = back.finish(ffn_part[0])
+    now = ffn_sums.step(leaving, *gate_sums.came())
+    now = gate_sums.step(*now)
+    conv_grad, rim_grad, tail, taps_grad, par_grad = mix.backward(
+        projected, rim, taps, par, mixed_grad, inverses, starts, incoming, leaving, now
     )
     back_rim = from_behind(rim_grad, "dp", -1)
-    tail = jnp.concatenate([tail[:, :8], tail[:, 8:] + back_rim], axis=1).astype(BF16)
-    pre_grad = lax.dynamic_update_slice(
-        pre_grad.reshape(micros, ranks, part_rows, conv_width),
-        tail[:, None],
-        (0, last_chunk, part_rows - HALO, 0),
-    ).reshape(-1, conv_width)
-
-    conv_grad = jnp.concatenate([pre_grad, dec_grad], axis=1)
-    shard_conv = scatter_rows(contract_rows(normed_all, conv_grad).astype(BF16))
-    normed_part = contract_cols(conv_grad, w_conv) + contract_cols(gate_grad, w_gate)
-    normed_grad = head_scatter(ranked(normed_part))
-    grad_norm_one = jnp.sum(normed_grad * normed_one, axis=(0, 1))
-    input_grad = after_mix_grad + norm_backward(normed_grad * attn_gain, normed_one, scale_one)
-
     small = jnp.concatenate(
         [
             taps_grad[:KCONV].reshape(-1),
             jnp.pad(par_grad[0, :heads], (0, LANES - heads)),
             jnp.pad(par_grad[1, :heads], (0, LANES - heads)),
             grad_head_norm[0],
-            from_ring(grad_norm_one),
-            from_ring(grad_norm_two),
         ]
     ).reshape(-1, LANES)
-    small = jnp.sum(lax.all_gather(small, "dp"), axis=0)
-    small = lax.all_gather(small, "head")
+    ffn_sum = HeadScatter(ffn_part[0], *[tie(part, rim_grad) for part in ffn_part[1:]])
+    now = ffn_sums.step(back_rim, *gate_sums.came())
+    now = ffn_sum.pass_on(*now)
+    tail = tie(tail, back_rim)
+    tail = jnp.concatenate([tail[:, :8], tail[:, 8:] + back_rim], axis=1).astype(BF16)
+    conv_grad = lax.dynamic_update_slice(
+        ranked(conv_grad), tail[None], (last_chunk, 0, part_rows - HALO, 0)
+    ).reshape(-1, conv_width + LANES)
+
+    conv_sums = Scatter((normed_all, conv_grad), after=now)
+    now = conv_sums.step()
+    now = conv_sums.work(1, after=now) + conv_sums.work(2, after=now)
+    normed_part = matmul(
+        [(conv_grad, w_conv), (gate_grad, w_gate)], NT, BF16, now, pieces=PIECES
+    )
+    normed_sum = HeadScatter(*normed_part)
+    now = gate_sums.step(*normed_sum.sent, *ffn_sums.came(), *conv_sums.came())
+    now = normed_sum.pass_on(*now)
+    now = conv_sums.step(*now, *gate_sums.came())
+    now = gate_sums.step(*now)
+    now = conv_sums.step(*now)
+    normed_grad = normed_sum.total(*now)
+    now = conv_sums.step(*now, *gate_sums.came())
+    grad_norm_one = jnp.sum(normed_grad * normed_one, axis=0)
+    norm_grads = jnp.pad(jnp.stack([grad_norm_one, grad_norm_two]), ((0, 6), (0, 0)))
+    (norm_grads,) = reorder([norm_grads], True, now)
+    norm_sum = Summed(norm_grads[:2].reshape(-1, LANES), head_hops())
+    norm_sum.step()
+    norm_sum.step()
+    input_grad = after_mix_grad + norm_backward(normed_grad * attn_gain, normed_one, scale_one)
+    block_out = (after_mix + ffn_sum.total(*now)).astype(BF16)
+    small_sum = Summed(jnp.concatenate([small, norm_sum.total()], axis=0), dp_hops())
+    small_sum.step(*now)
+    small_sum.step()
+    block_out, input_grad = reorder([block_out, input_grad], True, now)
+    block_out, input_grad = block_out.reshape(tokens.shape), input_grad.reshape(tokens.shape)
+    shard_ffn = ffn_sums.total(*now)
+    shard_gate = gate_sums.total(*now)
+    shard_conv = conv_sums.total()
+    small, norm_grads = small_sum.total()[: small.shape[0]], small_sum.total()[small.shape[0] :]
+    norm_grads = norm_grads.reshape(2, model)
+
+    across = jnp.stack([small, swap(small, "head", 2)])
+    near = swap(across, "head", 1)
+    small = jnp.stack([across[0], near[0], across[1], near[1]])
+    small = jnp.stack([small[jnp.bitwise_xor(at, head_rank)] for at in range(ranks)])
     tap_rows = KCONV * conv_width // LANES
     taps_all = small[:, :tap_rows].reshape(ranks, KCONV, conv_width).transpose(1, 0, 2)
 
@@ -1051,13 +1606,13 @@
 
     rest = jnp.sum(small[:, tap_rows + 2 :], axis=0).reshape(-1)
     return (
-        from_ring(block_out),
-        from_ring(input_grad),
-        rest[value_size : value_size + model],
+        block_out,
+        input_grad,
+        norm_grads[0],
         shard_conv[:, :qk_width],
         shard_conv[:, qk_width : 2 * qk_width],
         shard_conv[:, 2 * qk_width : conv_width],
-        shard_gate,
+        shard_gate[:, :v_width],
         shard_conv[:, conv_width : conv_width + heads],
         shard_conv[:, conv_width + heads : conv_width + 2 * heads],
         joined(0, qk_width),
@@ -1066,11 +1621,11 @@
         small[:, tap_rows, :heads].reshape(-1),
         small[:, tap_rows + 1, :heads].reshape(-1),
         rest[:value_size],
-        shard_out,
-        rest[value_size + model :],
+        shard_gate[:, v_width:].T,
+        norm_grads[1],
         shard_ffn[:, :ffn_width],
-        shard_ffn[:, ffn_width:],
-        shard_down,
+        shard_ffn[:, ffn_width : 2 * ffn_width],
+        shard_ffn[:, 2 * ffn_width :].T,
     )
 
 

time: 1120 us -> 991 us (0.88)
  Pallas kernels: 102 us -> 373 us
  matrix products: 173 us -> 11 us
  waiting for transfers between devices: 442 us -> 335 us
  blocking collectives: 52.8 us -> 0 us
  starting transfers between devices: 147 us -> 110 us
  other arithmetic: 76.7 us -> 48.1 us
  local copies, waits for them, and re-layouts: 117 us -> 101 us
    pallas_call x4 -> x108, Pallas kernels: 102 us -> 373 us  [the longest x9 107 us: kernel_call(): pl.pallas_call(body, grid_spec=pltpu.PrefetchScalarGridSpec(num_scalar_pr...]
    dot_general x16 -> x0, matrix products: 169 us -> none  [the longest x5 57.2 us: contract_cols(): return lax.dot_general(left, right, NT, preferred_element_type=F32)]
    ppermute x80 -> x48, waiting for transfers between devices: 336 us -> 190 us  [the longest x12 87.9 us: step(): self.left = lax.ppermute(up, 'dp', self.ahead)]
    ppermute x20 -> x60, waiting for transfers between devices: 34.2 us -> 97.4 us  [swap(): lax.ppermute(value, axis, [(at, at ^ bit) for at in range(lax.axis_size(a...]
    all_gather x2 -> x0, blocking collectives: 52.8 us -> none  [the longest x1 43 us: body(): small = jnp.sum(lax.all_gather(small, 'dp'), axis=0)]
    ppermute x80 -> x48, starting transfers between devices: 101 us -> 58.1 us  [the longest x9 22.2 us: step(): self.left.append(lax.ppermute(self.left[-1], 'dp', self.ahead))]
    ppermute x8, waiting for transfers between devices: 71.2 us -> 47.6 us  [from_behind(): lax.ppermute(value, axis, [(source, source + steps) for source in range(l...]
    convert_element_type x29 -> x10, other arithmetic: 33.7 us -> 13.3 us  [the longest x4 10.3 us: pass_on(): (mine.astype(F32) + near.astype(F32)).astype(BF16)]
  transfers between devices with their start and end apart: 108 -> 116, of which waited for: 43 -> 55; matrix products, arithmetic and copies ran while one was open for 23% -> 9% of each run, Pallas kernels for 9% -> 30%
where the time goes in v3:
time: 991 us; the launch traced here: 982 us
  Pallas kernels  373 us (38%)
  waiting for transfers between devices  335 us (34%)
  starting transfers between devices  110 us (11%)
  local copies, waits for them, and re-layouts  101 us (10%)
  other arithmetic  48.1 us (5%)
  matrix products  11 us (1%)
    pallas_call x9, Pallas kernels, kernel_call(): pl.pallas_call(body, grid_spec=pltpu.PrefetchScalarGridSpec(num_scalar_pr...  107 us
    ppermute x60, waiting for transfers between devices, swap(): lax.ppermute(value, axis, [(at, at ^ bit) for at in range(lax.axis_size(a...  97.4 us
    ppermute x12, waiting for transfers between devices, step(): self.left = lax.ppermute(up, 'dp', self.ahead)  87.9 us
    pallas_call x15, Pallas kernels, row_blocks(): pl.pallas_call(kernel, grid=(len(blocks),), in_specs=[pl.BlockSpec((left....  76.5 us
    pallas_call x6, Pallas kernels, matmul(): pl.pallas_call(kernel, grid=(grid,), in_specs=[spec for both in specs for...  70.7 us
    unnamed x313, local copies, waits for them, and re-layouts  65.6 us
    ppermute x9, waiting for transfers between devices, step(): self.left.append(lax.ppermute(self.left[-1], 'dp', self.ahead))  53.1 us
    ppermute x8, waiting for transfers between devices, from_behind(): lax.ppermute(value, axis, [(source, source + steps) for source in range(l...  47.6 us
  transfers between devices with their start and end apart: 116, of which 55 were waited for; matrix products, arithmetic and copies ran while one was open for 9% of the time, Pallas kernels for 30%

profile of v3, /device:TPU:0, one launch (start us, length us, event | category | flops | bytes accessed | tf_op | source)
XLA Modules:
  0.0 982.1 jit_solution(6116661312084058789)
XLA Ops:
  11.2 22.2 %collective-permute-done.2.refs_8_ = bf16[256,2176]{1,0:T(8,128)(2,1)} collective-permute-done((bf16[256,2176]{1,0:T(8,128)(2,1)}, bf16[256,2176]{1,0:T(8,128)(2,1)}, u32[]{:S(2)}, u32[]{:S(2)}) %collective-permute-start.2) | collective-permute-done | bytes 1114144 | tf_op jit(solution)/shard_map/ppermute | solution.py:1159
  40.4 19.1 %collective-permute-done.3.refs_3_.refs_7_ = bf16[256,2176]{1,0:T(8,128)(2,1)} collective-permute-done((bf16[256,2176]{1,0:T(8,128)(2,1)}, bf16[256,2176]{1,0:T(8,128)(2,1)}, u32[]{:S(2)}, u32[]{:S(2)}) %collective-permute-start.3) | collective-permute-done | bytes 1114144 | tf_op jit(solution)/shard_map/ppermute | solution.py:1159
  73.7 10.9 %collective-permute-done.10.refs_5_.refs_6_ = bf16[256,2176]{1,0:T(8,128)(2,1)} collective-permute-done((bf16[256,2176]{1,0:T(8,128)(2,1)}, bf16[256,2176]{1,0:T(8,128)(2,1)}, u32[]{:S(2)}, u32[]{:S(2)}) %collective-permute-start.10) | collective-permute-done | bytes 1114144 | tf_op jit(solution)/shard_map/ppermute | solution.py:1159
  123.8 16.9 %project.1 = (f32[1024,2176]{1,0:T(8,128)}, f32[32,2176]{1,0:T(8,128)S(1)}) custom-call(bf16[1024,2048]{1,0:T(8,128)(2,1)S(1)} %copy-done.2, bf16[32,2048]{1,0:T(8,128)(2,1)S(1)} %copy-done.94, bf16[2048,2176]{1,0:T(8,128)(2,1)} %assemble.16.weights_ref.refs_1_), custom_call_target="tpu_custom_call" | custom-call | tf_op jit(solution)/shard_map/project/pallas_call | solution.py:777
  149.6 36.0 %mix_forward.1 = (f32[1024,1024]{1,0:T(8,128)}, bf16[1024,512]{1,0:T(8,128)(2,1)S(1)}, bf16[8,4,128,128]{3,2,1,0:T(8,128)(2,1)S(1)}, bf16[8,4,128,384]{3,2,1,0:T(8,128)(2,1)}, f32[2,4,128,384]{3,2,1,0:T(8,128)S(1)}) custom-call(s32[2,6]{1,0:T(2,128)S(1)} %add_add_fusion.1.refs_0_, f32[1024,2176]{1,0:T(8,128)} %get-tuple-element.96.refs_1_.refs_2_, ...), custom_call_target="tpu_custom_call" | custom-call | tf_op jit(solution)/shard_map/mix_forward/pallas_call | solution.py:539
  188.6 30.3 %collective-permute-done.17.refs_0_ = bf16[4,128,384]{2,1,0:T(8,128)(2,1)S(1)} collective-permute-done((bf16[4,128,384]{2,1,0:T(8,128)(2,1)S(1)}, bf16[4,128,384]{2,1,0:T(8,128)(2,1)S(1)}, u32[]{:S(2)}, u32[]{:S(2)}) %collective-permute-start.17) | collective-permute-done | bytes 393248 | tf_op jit(solution)/shard_map/ppermute | solution.py:1003
  238.6 8.5 collective-permute-done.23.refs_3_
  308.3 7.7 matmul.6.refs_4_
  318.0 8.9 gate_forward.1
  337.6 9.6 collective-permute-done.38.refs_0_
  354.4 9.7 collective-permute-done.43.refs_0_
  364.1 10.8 %collective-permute-done.40.refs_0_ = bf16[128,2048]{1,0:T(8,128)(2,1)} collective-permute-done((bf16[128,2048]{1,0:T(8,128)(2,1)S(1)}, bf16[128,2048]{1,0:T(8,128)(2,1)}, u32[]{:S(2)}, u32[]{:S(2)}) %collective-permute-start.40) | collective-permute-done | bytes 524320 | tf_op jit(solution)/shard_map/ppermute | solution.py:1003
  381.1 12.8 %collective-permute-done.44.refs_1_ = bf16[128,2048]{1,0:T(8,128)(2,1)S(1)} collective-permute-done((bf16[128,2048]{1,0:T(8,128)(2,1)S(1)}, bf16[128,2048]{1,0:T(8,128)(2,1)S(1)}, u32[]{:S(2)}, u32[]{:S(2)}) %collective-permute-start.44) | collective-permute-done | bytes 524320 | tf_op jit(solution)/shard_map/ppermute | solution.py:1003
  414.2 14.5 %collective-permute-done.53.refs_5_ = bf16[128,4224]{1,0:T(8,128)(2,1)S(1)} collective-permute-done((bf16[128,4224]{1,0:T(8,128)(2,1)}, bf16[128,4224]{1,0:T(8,128)(2,1)S(1)}, u32[]{:S(2)}, u32[]{:S(2)}) %collective-permute-start.53) | collective-permute-done | bytes 1081376 | tf_op jit(solution)/shard_map/ppermute | solution.py:1165
  429.9 11.4 %assemble.22 = (bf16[2048,2816]{1,0:T(8,128)(2,1)}, bf16[2048,1408]{1,0:T(8,128)(2,1)}) custom-call(bf16[256,4224]{1,0:T(8,128)(2,1)S(1)} %copy-done.8, bf16[256,4224]{1,0:T(8,128)(2,1)} %tie.65.refs_10_.refs_1_, bf16[256,4224]{1,0:T(8,128)(2,1)} %tie.67.refs_2_, bf16[256,4224]{1,0:T(8,128)(2,1)} %tie.75.refs_4_.refs_3_, ...), custom_call_target="tpu_custom_call" | custom-call | tf_op jit(solution)/shard_map/assemble/pallas_call | solution.py:601
  441.3 29.1 %feed_forward.1 = (bf16[1024,1408]{1,0:T(8,128)(2,1)S(1)}, bf16[1024,2816]{1,0:T(8,128)(2,1)}) custom-call(bf16[1024,2048]{1,0:T(8,128)(2,1)} %assemble.21.refs_9_.rows_ref.left_ref, bf16[1024,2048]{1,0:T(8,128)(2,1)} %assemble.18.refs_4_.cotangent_ref.left_ref, bf16[2048,2816]{1,0:T(8,128)(2,1)} %get-tuple-element.111.ffn_ref.refs_1_, ...), custom_call_target="tpu_custom_call" | custom-call | tf_op jit(solution)/shard_map/feed_forward/pallas_call | solution.py:822
  470.4 18.1 %matmul.8 = (bf16[512,2048]{1,0:T(8,128)(2,1)S(1)}, bf16[128,2048]{1,0:T(8,128)(2,1)}, bf16[128,2048]{1,0:T(8,128)(2,1)}, bf16[128,2048]{1,0:T(8,128)(2,1)S(1)}, bf16[128,2048]{1,0:T(8,128)(2,1)S(1)}) custom-call(bf16[1024,2816]{1,0:T(8,128)(2,1)} %get-tuple-element.114.refs_0_.right_ref, bf16[2048,2816]{1,0:T(8,128)(2,1)} %get-tuple-element.111.ffn_ref.refs_1_), custom_call_target="tpu_custom_call" | custom-call | tf_op jit(solution)/shard_map/matmul/pallas_call | solution.py:751
  542.2 7.7 row_blocks.20.refs_4_.refs_1_.refs_3_
  550.0 12.7 %row_blocks.19.refs_3_.refs_0_.refs_2_ = bf16[1280,2816]{1,0:T(8,128)(2,1)} custom-call(bf16[1024,2048]{1,0:T(8,128)(2,1)S(1)} %copy-done.4, bf16[1024,2816]{1,0:T(8,128)(2,1)} %get-tuple-element.114.refs_0_.right_ref, bf16[256,2048]{1,0:T(8,128)(2,1)S(1)} %get-tuple-element.196.refs_0_), custom_call_target="tpu_custom_call" | custom-call | tf_op jit(solution)/shard_map/row_blocks/pallas_call | solution.py:685
  570.7 7.6 matmul.9.refs_1_
  581.8 10.5 %gate_backward.1 = (bf16[1024,1024]{1,0:T(8,128)(2,1)S(1)}, f32[1024,1024]{1,0:T(8,128)}, f32[2,4,128,256]{3,2,1,0:T(8,128)S(1)}, f32[8,256]{1,0:T(8,128)S(1)}) custom-call(s32[2,6]{1,0:T(2,128)S(1)} %add_add_fusion.1.refs_0_, f32[1024,1024]{1,0:T(8,128)} %copy-done.38, f32[1024,1024]{1,0:T(8,128)} %get-tuple-element.124.refs_2_, ...), custom_call_target="tpu_custom_call" | custom-call | tf_op jit(solution)/shard_map/gate_backward/pallas_call | solution.py:539
  625.0 10.2 %matmul.10 = (bf16[512,2048]{1,0:T(8,128)(2,1)S(1)}, bf16[128,2048]{1,0:T(8,128)(2,1)S(1)}, bf16[128,2048]{1,0:T(8,128)(2,1)S(1)}, bf16[128,2048]{1,0:T(8,128)(2,1)S(1)}, bf16[128,2048]{1,0:T(8,128)(2,1)S(1)}) custom-call(bf16[1024,1408]{1,0:T(8,128)(2,1)} %copy-done.9, bf16[2048,1408]{1,0:T(8,128)(2,1)} %get-tuple-element.112.down_ref.refs_1_, ...), custom_call_target="tpu_custom_call" | custom-call | tf_op jit(solution)/shard_map/matmul/pallas_call | solution.py:751
  659.8 10.1 %collective-permute-done.75.refs_7_.refs_4_ = bf16[128,2048]{1,0:T(8,128)(2,1)S(1)} collective-permute-done((bf16[128,2048]{1,0:T(8,128)(2,1)S(1)}, bf16[128,2048]{1,0:T(8,128)(2,1)S(1)}, u32[]{:S(2)}, u32[]{:S(2)}) %collective-permute-start.75) | collective-permute-done | bytes 524320 | tf_op jit(solution)/shard_map/ppermute | solution.py:1255
  680.9 46.2 %mix_backward.1 = (bf16[1024,2176]{1,0:T(8,128)(2,1)}, f32[2,8,2048]{2,1,0:T(8,128)S(1)}, f32[2,16,2048]{2,1,0:T(8,128)S(1)}, f32[8,2048]{1,0:T(8,128)S(1)}, f32[8,128]{1,0:T(8,128)S(1)}) custom-call(s32[2,6]{1,0:T(2,128)S(1)} %add_add_fusion.1.refs_0_, f32[1024,2176]{1,0:T(8,128)} %get-tuple-element.96.refs_1_.refs_2_, ...), custom_call_target="tpu_custom_call" | custom-call | tf_op jit(solution)/shard_map/mix_backward/pallas_call | solution.py:539
  729.1 19.7 %collective-permute-done.80.refs_6_.refs_1_ = f32[2,8,2048]{2,1,0:T(8,128)S(1)} collective-permute-done((f32[2,8,2048]{2,1,0:T(8,128)S(1)}, f32[2,8,2048]{2,1,0:T(8,128)S(1)}, u32[]{:S(2)}, u32[]{:S(2)}) %collective-permute-start.80) | collective-permute-done | bytes 131104 | tf_op jit(solution)/shard_map/ppermute | solution.py:999
  776.5 10.7 %row_blocks.28.refs_5_.refs_0_.refs_1_ = bf16[1280,2176]{1,0:T(8,128)(2,1)} custom-call(bf16[1024,2048]{1,0:T(8,128)(2,1)S(1)} %copy-done.3, bf16[1024,2176]{1,0:T(8,128)(2,1)} %bitcast.21.right_ref.refs_0_, bf16[128,2176]{1,0:T(8,128)(2,1)S(1)} %get-tuple-element.145.refs_0_, bf16[128,2176]{1,0:T(8,128)(2,1)S(1)} %get-tuple-element.146.refs_1_), custom_call_target="tpu_custom_call" | custom-call | tf_op jit(solution)/shard_map/row_blocks/pallas_call | solution.py:685
  787.2 19.7 %matmul.11 = (bf16[512,2048]{1,0:T(8,128)(2,1)S(1)}, bf16[128,2048]{1,0:T(8,128)(2,1)}, bf16[128,2048]{1,0:T(8,128)(2,1)}, bf16[128,2048]{1,0:T(8,128)(2,1)S(1)}, bf16[128,2048]{1,0:T(8,128)(2,1)}) custom-call(bf16[1024,2176]{1,0:T(8,128)(2,1)} %bitcast.21.right_ref.refs_0_, bf16[2048,2176]{1,0:T(8,128)(2,1)} %assemble.16.weights_ref.refs_1_, ...), custom_call_target="tpu_custom_call" | custom-call | tf_op jit(solution)/shard_map/matmul/pallas_call | solution.py:751
  808.2 10.7 %collective-permute-done.86.refs_12_.refs_2_ = bf16[128,2176]{1,0:T(8,128)(2,1)S(1)} collective-permute-done((bf16[128,2176]{1,0:T(8,128)(2,1)S(1)}, bf16[128,2176]{1,0:T(8,128)(2,1)S(1)}, u32[]{:S(2)}, u32[]{:S(2)}) %collective-permute-start.86) | collective-permute-done | bytes 557088 | tf_op jit(solution)/shard_map/ppermute | solution.py:1255
  830.0 16.9 %collective-permute-done.92.refs_6_.refs_4_ = bf16[256,2048]{1,0:T(8,128)(2,1)S(1)} collective-permute-done((bf16[256,2048]{1,0:T(8,128)(2,1)S(1)}, bf16[256,2048]{1,0:T(8,128)(2,1)S(1)}, u32[]{:S(2)}, u32[]{:S(2)}) %collective-permute-start.92) | collective-permute-done | bytes 1048608 | tf_op jit(solution)/shard_map/ppermute | solution.py:1255
  861.4 13.7 %collective-permute-done.94.refs_2_ = bf16[256,2176]{1,0:T(8,128)(2,1)} collective-permute-done((bf16[256,2176]{1,0:T(8,128)(2,1)S(1)}, bf16[256,2176]{1,0:T(8,128)(2,1)}, u32[]{:S(2)}, u32[]{:S(2)}) %collective-permute-start.94) | collective-permute-done | bytes 1114144 | tf_op jit(solution)/shard_map/ppermute | solution.py:1255
  889.8 11.5 %collective-permute-done.98.refs_6_.refs_0_ = bf16[256,2048]{1,0:T(8,128)(2,1)S(1)} collective-permute-done((bf16[256,2048]{1,0:T(8,128)(2,1)}, bf16[256,2048]{1,0:T(8,128)(2,1)S(1)}, u32[]{:S(2)}, u32[]{:S(2)}) %collective-permute-start.98) | collective-permute-done | bytes 1048608 | tf_op jit(solution)/shard_map/ppermute | solution.py:1255
  902.8 19.3 %collective-permute-done.96.refs_2_ = bf16[256,2176]{1,0:T(8,128)(2,1)} collective-permute-done((bf16[256,2176]{1,0:T(8,128)(2,1)S(1)}, bf16[256,2176]{1,0:T(8,128)(2,1)}, u32[]{:S(2)}, u32[]{:S(2)}) %collective-permute-start.96) | collective-permute-done | bytes 1114144 | tf_op jit(solution)/shard_map/ppermute | solution.py:1255
  (742 shorter events, 475.0 us)
Async XLA Ops:
  35.5 30.3 %collective-permute-start.5 = (bf16[256,2176]{1,0:T(8,128)(2,1)}, bf16[256,2176]{1,0:T(8,128)(2,1)}, u32[]{:S(2)}, u32[]{:S(2)}) collective-permute-start(bf16[256,2176]{1,0:T(8,128)(2,1)} %collective-permute-done.4.refs_1_), channel_id=1, source_target_pairs={{8,0},{16,8},{24,16},{28,24},{20,28},{12,20},{4,12},{0,4},{9,1},{1... | collective-permute-start | bytes 3342344 | tf_op jit(solution)/shard_map/ppermute | solution.py:1160
  36.9 30.8 %collective-permute-start = (bf16[128,2048]{1,0:T(8,128)(2,1)}, bf16[128,2048]{1,0:T(8,128)(2,1)}, u32[]{:S(2)}, u32[]{:S(2)}) collective-permute-start(bf16[128,2048]{1,0:T(8,128)(2,1)} %get-tuple-element.252), channel_id=1, source_target_pairs={{0,2},{1,3},{2,0},{3,1},{4,6},{5,7},{6,4},{7,5},{8,10},{9,11},{10,... | collective-permute-start | bytes 1572872 | tf_op jit(solution)/shard_map/ppermute | solution.py:1003
  108.7 32.8 %collective-permute-start.16 = (bf16[256,2048]{1,0:T(8,128)(2,1)}, bf16[256,2048]{1,0:T(8,128)(2,1)}, u32[]{:S(2)}, u32[]{:S(2)}) collective-permute-start(bf16[256,2048]{1,0:T(8,128)(2,1)} %tie.53.refs_9_.refs_10_.refs_0_), channel_id=1, source_target_pairs={{8,0},{16,8},{24,16},{28,24},{20,28},{12,20},{4,12},{0,4},{9,1},{1... | collective-permute-start | bytes 3145736 | tf_op jit(solution)/shard_map/ppermute | solution.py:1160
  142.4 76.5 %collective-permute-start.20 = (bf16[256,4224]{1,0:T(8,128)(2,1)}, bf16[256,4224]{1,0:T(8,128)(2,1)}, u32[]{:S(2)}, u32[]{:S(2)}) collective-permute-start(bf16[256,4224]{1,0:T(8,128)(2,1)} %tie.56.refs_5_.refs_6_.refs_0_), channel_id=1, source_target_pairs={{0,8},{8,16},{16,24},{24,28},{28,20},{20,12},{12,4},{4,0},{1,9},{9... | collective-permute-start | bytes 6488072 | tf_op jit(solution)/shard_map/ppermute | solution.py:1159
  144.5 75.1 %collective-permute-start.21 = (bf16[256,4224]{1,0:T(8,128)(2,1)}, bf16[256,4224]{1,0:T(8,128)(2,1)}, u32[]{:S(2)}, u32[]{:S(2)}) collective-permute-start(bf16[256,4224]{1,0:T(8,128)(2,1)} %tie.56.refs_5_.refs_6_.refs_0_), channel_id=1, source_target_pairs={{8,0},{16,8},{24,16},{28,24},{20,28},{12,20},{4,12},{0,4},{9,1},{1... | collective-permute-start | bytes 6488072 | tf_op jit(solution)/shard_map/ppermute | solution.py:1160
  145.7 73.1 %collective-permute-start.19 = (bf16[256,2048]{1,0:T(8,128)(2,1)}, bf16[256,2048]{1,0:T(8,128)(2,1)S(1)}, u32[]{:S(2)}, u32[]{:S(2)}) collective-permute-start(bf16[256,2048]{1,0:T(8,128)(2,1)} %tie.55.refs_2_.refs_1_), channel_id=1, source_target_pairs={{8,0},{16,8},{24,16},{28,24},{20,28},{12,20},{4,12},{0,4},{9,1},{1... | collective-permute-start | bytes 3145736 | tf_op jit(solution)/shard_map/ppermute | solution.py:1160
  146.1 72.7 %collective-permute-start.18 = (bf16[256,2048]{1,0:T(8,128)(2,1)}, bf16[256,2048]{1,0:T(8,128)(2,1)S(1)}, u32[]{:S(2)}, u32[]{:S(2)}) collective-permute-start(bf16[256,2048]{1,0:T(8,128)(2,1)} %tie.54.refs_1_.refs_8_), channel_id=1, source_target_pairs={{0,8},{8,16},{16,24},{24,28},{28,20},{20,12},{12,4},{4,0},{1,9},{9... | collective-permute-start | bytes 3145736 | tf_op jit(solution)/shard_map/ppermute | solution.py:1159
  186.7 32.2 %collective-permute-start.17 = (bf16[4,128,384]{2,1,0:T(8,128)(2,1)S(1)}, bf16[4,128,384]{2,1,0:T(8,128)(2,1)S(1)}, u32[]{:S(2)}, u32[]{:S(2)}) collective-permute-start(bf16[4,128,384]{2,1,0:T(8,128)(2,1)S(1)} %fusion.20.refs_1_), channel_id=1, source_target_pairs={{0,4},{4,0},{8,12},{12,8},{16,20},{20,16},{24,28},{28,24},{1,5},{5... | collective-permute-start | bytes 1179656 | tf_op jit(solution)/shard_map/ppermute | solution.py:1003
  226.0 35.2 %collective-permute-start.25 = (bf16[128,2048]{1,0:T(8,128)(2,1)}, bf16[128,2048]{1,0:T(8,128)(2,1)}, u32[]{:S(2)}, u32[]{:S(2)}) collective-permute-start(bf16[128,2048]{1,0:T(8,128)(2,1)} %get-tuple-element.250), channel_id=1, source_target_pairs={{0,2},{1,3},{2,0},{3,1},{4,6},{5,7},{6,4},{7,5},{8,10},{9,11},{10,... | collective-permute-start | bytes 1572872 | tf_op jit(solution)/shard_map/ppermute | solution.py:1003
  227.5 33.7 %collective-permute-start.26 = (bf16[128,2048]{1,0:T(8,128)(2,1)}, bf16[128,2048]{1,0:T(8,128)(2,1)}, u32[]{:S(2)}, u32[]{:S(2)}) collective-permute-start(bf16[128,2048]{1,0:T(8,128)(2,1)} %get-tuple-element.249), channel_id=1, source_target_pairs={{0,2},{1,3},{2,0},{3,1},{4,6},{5,7},{6,4},{7,5},{8,10},{9,11},{10,... | collective-permute-start | bytes 1572872 | tf_op jit(solution)/shard_map/ppermute | solution.py:1003
  298.0 49.2 %collective-permute-start.38 = (bf16[256,4224]{1,0:T(8,128)(2,1)}, bf16[256,4224]{1,0:T(8,128)(2,1)}, u32[]{:S(2)}, u32[]{:S(2)}) collective-permute-start(bf16[256,4224]{1,0:T(8,128)(2,1)} %tie.65.refs_10_.refs_1_), channel_id=1, source_target_pairs={{8,0},{16,8},{24,16},{28,24},{20,28},{12,20},{4,12},{0,4},{9,1},{1... | collective-permute-start | bytes 6488072 | tf_op jit(solution)/shard_map/ppermute | solution.py:1160
  298.0 49.2 %collective-permute-start.37 = (bf16[256,4224]{1,0:T(8,128)(2,1)}, bf16[256,4224]{1,0:T(8,128)(2,1)}, u32[]{:S(2)}, u32[]{:S(2)}) collective-permute-start(bf16[256,4224]{1,0:T(8,128)(2,1)} %tie.64.refs_9_.refs_8_), channel_id=1, source_target_pairs={{0,8},{8,16},{16,24},{24,28},{28,20},{20,12},{12,4},{4,0},{1,9},{9... | collective-permute-start | bytes 6488072 | tf_op jit(solution)/shard_map/ppermute | solution.py:1159
  352.2 49.2 %collective-permute-start.47 = (bf16[256,4224]{1,0:T(8,128)(2,1)}, bf16[256,4224]{1,0:T(8,128)(2,1)}, u32[]{:S(2)}, u32[]{:S(2)}) collective-permute-start(bf16[256,4224]{1,0:T(8,128)(2,1)} %tie.67.refs_2_), channel_id=1, source_target_pairs={{8,0},{16,8},{24,16},{28,24},{20,28},{12,20},{4,12},{0,4},{9,1},{1... | collective-permute-start | bytes 6488072 | tf_op jit(solution)/shard_map/ppermute | solution.py:1160
  353.0 50.9 %collective-permute-start.46 = (bf16[256,4224]{1,0:T(8,128)(2,1)}, bf16[256,4224]{1,0:T(8,128)(2,1)}, u32[]{:S(2)}, u32[]{:S(2)}) collective-permute-start(bf16[256,4224]{1,0:T(8,128)(2,1)} %tie.66.refs_1_.refs_7_), channel_id=1, source_target_pairs={{0,8},{8,16},{16,24},{24,28},{28,20},{20,12},{12,4},{4,0},{1,9},{9... | collective-permute-start | bytes 6488072 | tf_op jit(solution)/shard_map/ppermute | solution.py:1159
  532.3 48.1 %collective-permute-start.68 = (bf16[256,4224]{1,0:T(8,128)(2,1)}, bf16[256,4224]{1,0:T(8,128)(2,1)}, u32[]{:S(2)}, u32[]{:S(2)}) collective-permute-start(bf16[256,4224]{1,0:T(8,128)(2,1)} %get-tuple-element.122.refs_1_), channel_id=1, source_target_pairs={{0,8},{8,16},{16,24},{24,28},{28,20},{20,12},{12,4},{4,0},{1,9},{9... | collective-permute-start | bytes 6488072 | tf_op jit(solution)/shard_map/ppermute | solution.py:1255
  534.0 47.8 %collective-permute-start.69 = (bf16[256,4224]{1,0:T(8,128)(2,1)}, bf16[256,4224]{1,0:T(8,128)(2,1)}, u32[]{:S(2)}, u32[]{:S(2)}) collective-permute-start(bf16[256,4224]{1,0:T(8,128)(2,1)} %get-tuple-element.123.refs_2_), channel_id=1, source_target_pairs={{8,0},{16,8},{24,16},{28,24},{20,28},{12,20},{4,12},{0,4},{9,1},{1... | collective-permute-start | bytes 6488072 | tf_op jit(solution)/shard_map/ppermute | solution.py:1256
  610.3 30.9 %collective-permute-start.72 = (bf16[4,128,384]{2,1,0:T(8,128)(2,1)S(1)}, bf16[4,128,384]{2,1,0:T(8,128)(2,1)}, u32[]{:S(2)}, u32[]{:S(2)}) collective-permute-start(bf16[4,128,384]{2,1,0:T(8,128)(2,1)S(1)} %pad_maximum_fusion.6.refs_0_), channel_id=1, source_target_pairs={{8,0},{12,4},{16,8},{20,12},{24,16},{28,20},{9,1},{13,5},{17,9},{2... | collective-permute-start | bytes 1179656 | tf_op jit(solution)/shard_map/ppermute | solution.py:999
  611.6 35.9 %collective-permute-start.73 = (bf16[4,128,384]{2,1,0:T(8,128)(2,1)S(1)}, bf16[4,128,384]{2,1,0:T(8,128)(2,1)}, u32[]{:S(2)}, u32[]{:S(2)}) collective-permute-start(bf16[4,128,384]{2,1,0:T(8,128)(2,1)S(1)} %pad_maximum_fusion.6.refs_0_), channel_id=1, source_target_pairs={{16,0},{20,4},{24,8},{28,12},{17,1},{21,5},{25,9},{29,13},{18,2},{... | collective-permute-start | bytes 1179656 | tf_op jit(solution)/shard_map/ppermute | solution.py:999
  675.2 75.3 %collective-permute-start.78 = (bf16[256,4224]{1,0:T(8,128)(2,1)}, bf16[256,4224]{1,0:T(8,128)(2,1)}, u32[]{:S(2)}, u32[]{:S(2)}) collective-permute-start(bf16[256,4224]{1,0:T(8,128)(2,1)} %get-tuple-element.134.refs_6_), channel_id=1, source_target_pairs={{0,8},{8,16},{16,24},{24,28},{28,20},{20,12},{12,4},{4,0},{1,9},{9... | collective-permute-start | bytes 6488072 | tf_op jit(solution)/shard_map/ppermute | solution.py:1255
  675.3 75.2 %collective-permute-start.79 = (bf16[256,4224]{1,0:T(8,128)(2,1)}, bf16[256,4224]{1,0:T(8,128)(2,1)}, u32[]{:S(2)}, u32[]{:S(2)}) collective-permute-start(bf16[256,4224]{1,0:T(8,128)(2,1)} %get-tuple-element.135.refs_7_), channel_id=1, source_target_pairs={{8,0},{16,8},{24,16},{28,24},{20,28},{12,20},{4,12},{0,4},{9,1},{1... | collective-permute-start | bytes 6488072 | tf_op jit(solution)/shard_map/ppermute | solution.py:1256
  678.8 70.7 %collective-permute-start.81 = (bf16[256,2048]{1,0:T(8,128)(2,1)}, bf16[256,2048]{1,0:T(8,128)(2,1)S(1)}, u32[]{:S(2)}, u32[]{:S(2)}) collective-permute-start(bf16[256,2048]{1,0:T(8,128)(2,1)} %get-tuple-element.136.refs_11_), channel_id=1, source_target_pairs={{0,8},{8,16},{16,24},{24,28},{28,20},{20,12},{12,4},{4,0},{1,9},{9... | collective-permute-start | bytes 3145736 | tf_op jit(solution)/shard_map/ppermute | solution.py:1255
  678.9 70.6 %collective-permute-start.82 = (bf16[256,2048]{1,0:T(8,128)(2,1)}, bf16[256,2048]{1,0:T(8,128)(2,1)S(1)}, u32[]{:S(2)}, u32[]{:S(2)}) collective-permute-start(bf16[256,2048]{1,0:T(8,128)(2,1)} %get-tuple-element.137.refs_12_), channel_id=1, source_target_pairs={{8,0},{16,8},{24,16},{28,24},{20,28},{12,20},{4,12},{0,4},{9,1},{1... | collective-permute-start | bytes 3145736 | tf_op jit(solution)/shard_map/ppermute | solution.py:1256
  757.6 61.9 %collective-permute-start.89 = (bf16[256,4224]{1,0:T(8,128)(2,1)S(1)}, bf16[256,4224]{1,0:T(8,128)(2,1)}, u32[]{:S(2)}, u32[]{:S(2)}) collective-permute-start(bf16[256,4224]{1,0:T(8,128)(2,1)S(1)} %get-tuple-element.139.refs_1_), channel_id=1, source_target_pairs={{0,8},{8,16},{16,24},{24,28},{28,20},{20,12},{12,4},{4,0},{1,9},{9... | collective-permute-start | bytes 6488072 | tf_op jit(solution)/shard_map/ppermute | solution.py:1255
  757.6 61.8 %collective-permute-start.90 = (bf16[256,4224]{1,0:T(8,128)(2,1)}, bf16[256,4224]{1,0:T(8,128)(2,1)}, u32[]{:S(2)}, u32[]{:S(2)}) collective-permute-start(bf16[256,4224]{1,0:T(8,128)(2,1)} %get-tuple-element.140.refs_2_), channel_id=1, source_target_pairs={{8,0},{16,8},{24,16},{28,24},{20,28},{12,20},{4,12},{0,4},{9,1},{1... | collective-permute-start | bytes 6488072 | tf_op jit(solution)/shard_map/ppermute | solution.py:1256
  767.7 51.3 %collective-permute-start.86 = (bf16[128,2176]{1,0:T(8,128)(2,1)S(1)}, bf16[128,2176]{1,0:T(8,128)(2,1)S(1)}, u32[]{:S(2)}, u32[]{:S(2)}) collective-permute-start(bf16[128,2176]{1,0:T(8,128)(2,1)S(1)} %get-tuple-element.145.refs_0_), channel_id=1, source_target_pairs={{0,8},{8,16},{16,24},{24,28},{28,20},{20,12},{12,4},{4,0},{1,9},{9... | collective-permute-start | bytes 1671176 | tf_op jit(solution)/shard_map/ppermute | solution.py:1255
  767.8 51.6 %collective-permute-start.87 = (bf16[128,2176]{1,0:T(8,128)(2,1)S(1)}, bf16[128,2176]{1,0:T(8,128)(2,1)S(1)}, u32[]{:S(2)}, u32[]{:S(2)}) collective-permute-start(bf16[128,2176]{1,0:T(8,128)(2,1)S(1)} %get-tuple-element.146.refs_1_), channel_id=1, source_target_pairs={{8,0},{16,8},{24,16},{28,24},{20,28},{12,20},{4,12},{0,4},{9,1},{1... | collective-permute-start | bytes 1671176 | tf_op jit(solution)/shard_map/ppermute | solution.py:1256
  857.0 78.6 %collective-permute-start.101 = (bf16[128,2048]{1,0:T(8,128)(2,1)}, bf16[128,2048]{1,0:T(8,128)(2,1)}, u32[]{:S(2)}, u32[]{:S(2)}) collective-permute-start(bf16[128,2048]{1,0:T(8,128)(2,1)} %get-tuple-element.218.refs_1_), channel_id=1, source_target_pairs={{0,2},{1,3},{2,0},{3,1},{4,6},{5,7},{6,4},{7,5},{8,10},{9,11},{10,... | collective-permute-start | bytes 1572872 | tf_op jit(solution)/shard_map/ppermute | solution.py:1003
  880.6 41.6 %collective-permute-start.96 = (bf16[256,2176]{1,0:T(8,128)(2,1)S(1)}, bf16[256,2176]{1,0:T(8,128)(2,1)}, u32[]{:S(2)}, u32[]{:S(2)}) collective-permute-start(bf16[256,2176]{1,0:T(8,128)(2,1)S(1)} %get-tuple-element.158.refs_4_.refs_1_), channel_id=1, source_target_pairs={{0,8},{8,16},{16,24},{24,28},{28,20},{20,12},{12,4},{4,0},{1,9},{9... | collective-permute-start | bytes 3342344 | tf_op jit(solution)/shard_map/ppermute | solution.py:1255
  882.2 40.5 %collective-permute-start.97 = (bf16[256,2176]{1,0:T(8,128)(2,1)S(1)}, bf16[256,2176]{1,0:T(8,128)(2,1)}, u32[]{:S(2)}, u32[]{:S(2)}) collective-permute-start(bf16[256,2176]{1,0:T(8,128)(2,1)S(1)} %copy-done.43), channel_id=1, source_target_pairs={{8,0},{16,8},{24,16},{28,24},{20,28},{12,20},{4,12},{0,4},{9,1},{1... | collective-permute-start | bytes 3342344 | tf_op jit(solution)/shard_map/ppermute | solution.py:1256
  901.3 34.3 %collective-permute-start.84 = (bf16[128,2048]{1,0:T(8,128)(2,1)}, bf16[128,2048]{1,0:T(8,128)(2,1)}, u32[]{:S(2)}, u32[]{:S(2)}) collective-permute-start(bf16[128,2048]{1,0:T(8,128)(2,1)} %get-tuple-element.217.refs_0_), channel_id=1, source_target_pairs={{0,2},{1,3},{2,0},{3,1},{4,6},{5,7},{6,4},{7,5},{8,10},{9,11},{10,... | collective-permute-start | bytes 1572872 | tf_op jit(solution)/shard_map/ppermute | solution.py:1003
  926.2 49.5 %collective-permute-start.112 = (bf16[256,2176]{1,0:T(8,128)(2,1)}, bf16[256,2176]{1,0:T(8,128)(2,1)}, u32[]{:S(2)}, u32[]{:S(2)}) collective-permute-start(bf16[256,2176]{1,0:T(8,128)(2,1)} %get-tuple-element.160.refs_1_.refs_3_.refs_2_), channel_id=1, source_target_pairs={{0,8},{8,16},{16,24},{24,28},{28,20},{20,12},{12,4},{4,0},{1,9},{9... | collective-permute-start | bytes 3342344 | tf_op jit(solution)/shard_map/ppermute | solution.py:1255
  927.3 48.4 %collective-permute-start.113 = (bf16[256,2176]{1,0:T(8,128)(2,1)}, bf16[256,2176]{1,0:T(8,128)(2,1)}, u32[]{:S(2)}, u32[]{:S(2)}) collective-permute-start(bf16[256,2176]{1,0:T(8,128)(2,1)} %get-tuple-element.161.refs_2_.refs_4_.refs_3_), channel_id=1, source_target_pairs={{8,0},{16,8},{24,16},{28,24},{20,28},{12,20},{4,12},{0,4},{9,1},{1... | collective-permute-start | bytes 3342344 | tf_op jit(solution)/shard_map/ppermute | solution.py:1256
  (239 other events, 2992.1 us)

commit v4 on v3

--- a/solution.py
+++ b/solution.py
@@ -762,78 +762,147 @@
     return found if pieces else found[0]
 
 
-def project(rows, rim, weights, after=()):
-    tile = 256
-
-    def kernel(rows_ref, rim_ref, weights_ref, *refs):
-        out, out_rim = refs[-2:]
-        out[...] = jnp.dot(rows_ref[...], weights_ref[...], preferred_element_type=F32)
+def weighted(body, parts, cuts, operands, specs, out_specs, out_shape, steps, name, after=()):
+    count, given, kept = len(parts), len(operands), len(cuts)
+    rows, columns = sum(part.shape[0] for part in parts), parts[0].shape[1]
+
+    def kernel(*refs):
+        sources, mine = refs[:count], refs[count : count + given]
+        rest = refs[count + given + len(after) :]
+        held, into, back = rest[-3:]
+        stores = [
+            pltpu.make_async_copy(held.at[:, low:high], rest[at], back.at[at])
+            for at, (low, high) in enumerate(cuts)
+        ]
 
         @pl.when(pl.program_id(0) == 0)
         def _():
-            out_rim[...] = jnp.dot(rim_ref[...], weights_ref[...], preferred_element_type=F32)
-
-    columns = weights.shape[1]
-    return pl.pallas_call(
+            loads, row = [], 0
+            for at, source in enumerate(sources):
+                target = held.at[row : row + source.shape[0]]
+                loads.append(pltpu.make_async_copy(source, target, into.at[at]))
+                loads[-1].start()
+                row += source.shape[0]
+            for load in loads:
+                load.wait()
+            for store in stores:
+                store.start()
+
+        body(held, mine, rest[kept:-3])
+
+        @pl.when(pl.program_id(0) == steps - 1)
+        def _():
+            for store in stores:
+                store.wait()
+
+    dtype = parts[0].dtype
+    weights = [jax.ShapeDtypeStruct((rows, high - low), dtype) for low, high in cuts]
+    found = pl.pallas_call(
         kernel,
-        grid=(rows.shape[0] // tile,),
-        in_specs=[
-            pl.BlockSpec((tile, rows.shape[1]), lambda i: (i, 0)),
-            pl.BlockSpec(rim.shape, lambda i: (0, 0)),
-            pl.BlockSpec(weights.shape, lambda i: (0, 0)),
-        ]
-        + [ANYWHERE] * len(after),
-        out_specs=[
-            pl.BlockSpec((tile, columns), lambda i: (i, 0)),
-            pl.BlockSpec((rim.shape[0], columns), lambda i: (0, 0)),
-        ],
-        out_shape=[
-            jax.ShapeDtypeStruct((rows.shape[0], columns), F32),
-            jax.ShapeDtypeStruct((rim.shape[0], columns), F32),
+        grid=(steps,),
+        in_specs=[ANYWHERE] * count + specs + [ANYWHERE] * len(after),
+        out_specs=[ANYWHERE] * kept + out_specs,
+        out_shape=weights + out_shape,
+        scratch_shapes=[
+            pltpu.VMEM((rows, columns), dtype),
+            pltpu.SemaphoreType.DMA((count,)),
+            pltpu.SemaphoreType.DMA((kept,)),
         ],
         compiler_params=pltpu.CompilerParams(
             dimension_semantics=("arbitrary",), vmem_limit_bytes=VMEM_BYTES
         ),
-        name="project",
-    )(rows, rim, weights, *after)
-
-
-def feed_forward(rows, cotangent, w_ffn, w_down, after=()):
-    tile = 256
-    model, width = w_down.shape
-
-    def kernel(rows_ref, cotangent_ref, ffn_ref, down_ref, *refs):
-        hidden_ref, grad_ref = refs[-2:]
-        gate = jnp.dot(rows_ref[...], ffn_ref[:, :width], preferred_element_type=F32)
-        up = jnp.dot(rows_ref[...], ffn_ref[:, width:], preferred_element_type=F32)
-        grad = jnp.dot(cotangent_ref[...], down_ref[...], preferred_element_type=F32)
+        name=name,
+    )(*parts, *operands, *after)
+    return found[:kept], found[kept:]
+
+
+ROW_TILE = 256
+
+
+def tiles_of(columns):
+    return pl.BlockSpec((ROW_TILE, columns), lambda i: (i, 0))
+
+
+def project(rows, rim, parts, after=()):
+    columns = parts[0].shape[1]
+
+    def body(held, given, outs):
+        rows_ref, rim_ref = given
+        outs[0][...] = jnp.dot(rows_ref[...], held[...], preferred_element_type=F32)
+
+        @pl.when(pl.program_id(0) == 0)
+        def _():
+            outs[1][...] = jnp.dot(rim_ref[...], held[...], preferred_element_type=F32)
+
+    (weights,), (projected, rim_projected) = weighted(
+        body,
+        parts,
+        [(0, columns)],
+        (rows, rim),
+        [tiles_of(rows.shape[1]), pl.BlockSpec(rim.shape, lambda i: (0, 0))],
+        [tiles_of(columns), pl.BlockSpec((rim.shape[0], columns), lambda i: (0, 0))],
+        [
+            jax.ShapeDtypeStruct((rows.shape[0], columns), F32),
+            jax.ShapeDtypeStruct((rim.shape[0], columns), F32),
+        ],
+        rows.shape[0] // ROW_TILE,
+        "project",
+        after,
+    )
+    return projected, rim_projected, weights
+
+
+def gate_project(rows, parts, width, after=()):
+    def body(held, given, outs):
+        outs[0][...] = jnp.dot(given[0][...], held[:, :width], preferred_element_type=F32)
+
+    (first, second), (found,) = weighted(
+        body,
+        parts,
+        [(0, width), (width, parts[0].shape[1])],
+        (rows,),
+        [tiles_of(rows.shape[1])],
+        [tiles_of(width)],
+        [jax.ShapeDtypeStruct((rows.shape[0], width), F32)],
+        rows.shape[0] // ROW_TILE,
+        "gate_project",
+        after,
+    )
+    return found, first, second
+
+
+def feed_forward(rows, cotangent, parts, after=()):
+    width = parts[0].shape[1] // 3
+
+    def body(held, given, outs):
+        rows_ref, cotangent_ref = given
+        hidden_ref, grad_ref = outs
+        gate = jnp.dot(rows_ref[...], held[:, :width], preferred_element_type=F32)
+        up = jnp.dot(rows_ref[...], held[:, width : 2 * width], preferred_element_type=F32)
+        grad = jnp.dot(cotangent_ref[...], held[:, 2 * width :], preferred_element_type=F32)
         sig = jax.nn.sigmoid(gate)
         active = gate * sig
         hidden_ref[...] = (active * up).astype(BF16)
         grad_ref[:, :width] = (grad * up * sig * (1.0 + gate * (1.0 - sig))).astype(BF16)
         grad_ref[:, width:] = (grad * active).astype(BF16)
 
-    def by_rows(columns):
-        return pl.BlockSpec((tile, columns), lambda i: (i, 0))
-
-    def once(array):
-        return pl.BlockSpec(array.shape, lambda i: (0, 0), pipeline_mode=pl.Buffered(1))
-
-    return pl.pallas_call(
-        kernel,
-        grid=(rows.shape[0] // tile,),
-        in_specs=[by_rows(model), by_rows(model), once(w_ffn), once(w_down)]
-        + [ANYWHERE] * len(after),
-        out_specs=[by_rows(width), by_rows(2 * width)],
-        out_shape=[
+    model = rows.shape[1]
+    (w_ffn, w_down), (hidden, grad) = weighted(
+        body,
+        parts,
+        [(0, 2 * width), (2 * width, 3 * width)],
+        (rows, cotangent),
+        [tiles_of(model), tiles_of(model)],
+        [tiles_of(width), tiles_of(2 * width)],
+        [
             jax.ShapeDtypeStruct((rows.shape[0], width), BF16),
             jax.ShapeDtypeStruct((rows.shape[0], 2 * width), BF16),
         ],
-        compiler_params=pltpu.CompilerParams(
-            dimension_semantics=("arbitrary",), vmem_limit_bytes=VMEM_BYTES
-        ),
-        name="feed_forward",
-    )(rows, cotangent, w_ffn, w_down, *after)
+        rows.shape[0] // ROW_TILE,
+        "feed_forward",
+        after,
+    )
+    return hidden, grad, w_ffn, w_down
 
 
 class Mix:
@@ -1176,27 +1245,6 @@
 
     def parts(self):
         return [self.left[0]] + self.right[1:] + self.far + self.left[:0:-1]
-
-
-def gathered(wanted, after=()):
-    rings = []
-    for cuts in wanted:
-        rings += [ring for ring, _, _ in cuts if ring not in rings]
-    arrays, first = [], {}
-    for ring in rings:
-        first[ring] = len(arrays)
-        arrays += ring.parts()
-    plan = []
-    for cuts in wanted:
-        column, items = 0, []
-        for ring, low, high in cuts:
-            row = 0
-            for at, part in enumerate(ring.parts()):
-                items.append((first[ring] + at, (0, part.shape[0]), (low, high), row, column))
-                row += part.shape[0]
-            column += high - low
-        plan.append(((row, column), items))
-    return assemble(plan, arrays, after)
 
 
 class Scatter:
@@ -1468,8 +1516,7 @@
     ).astype(jnp.int32)
     mix = Mix(info, micros, ranks, heads, key_size, value_size)
     now = gate_ring.step(rim_rows, *conv_ring.far)
-    (w_conv,) = gathered([[(conv_ring, 0, conv_width + LANES)]], now)
-    projected, rim = project(normed_all, rim_rows, w_conv)
+    projected, rim, w_conv = project(normed_all, rim_rows, conv_ring.parts(), now)
     now = gate_ring.step(rim)
     now = ffn_ring.step(*now)
 
@@ -1483,10 +1530,7 @@
     cotangent_all = cotangent_rows.rows(*now)
     now = gate_ring.run(*now)
     now = ffn_ring.step(incoming, *gate_ring.far, cotangent_all)
-    w_gate, w_out = gathered(
-        [[(gate_ring, 0, v_width)], [(gate_ring, v_width, 2 * v_width)]], now
-    )
-    gate_lin = matmul([(normed_all, w_gate)], NN, F32)
+    gate_lin, w_gate, w_out = gate_project(normed_all, gate_ring.parts(), v_width, now)
     mixed, gated = mix.gate_forward(plain, carried_map, incoming, gate_lin, gain)
 
     mix_sum = HeadScatter(*matmul([(gated, w_out)], NT, BF16, pieces=PIECES))
@@ -1499,11 +1543,8 @@
     now = ffn_ring.run(ffn_rows.across[0])
     now = ffn_rows.pass_on(*now)
     ffn_all = ffn_rows.rows(*now)
-    w_ffn, w_down = gathered(
-        [[(ffn_ring, 0, 2 * ffn_width)], [(ffn_ring, 2 * ffn_width, 3 * ffn_width)]], (ffn_all,)
-    )
-
-    hidden, gate_up_grad = feed_forward(ffn_all, cotangent_all, w_ffn, w_down)
+
+    hidden, gate_up_grad, w_ffn, w_down = feed_forward(ffn_all, cotangent_all, ffn_ring.parts())
     ffn_in_sum = HeadScatter(*matmul([(gate_up_grad, w_ffn)], NT, BF16, pieces=PIECES))
     ffn_sums = Scatter(
         (ffn_all, gate_up_grad), (cotangent_all, hidden), after=ffn_in_sum.sent

time: 991 us -> 972 us (0.981)
  Pallas kernels: 373 us -> 354 us
    pallas_call x14 -> x11, Pallas kernels: 43.4 us -> 19.4 us  [assemble(): pl.pallas_call(kernel, out_shape=[jax.ShapeDtypeStruct(shape, arrays[0].d...]
    ppermute x3, waiting for transfers between devices: 7.06 us -> 20.3 us  [step(): lax.ppermute(self.left[-1][:half], 'dp', self.ahead)]
    pallas_call x2 -> x3, Pallas kernels: 46 us -> 58.7 us  [weighted(): pl.pallas_call(kernel, grid=(steps,), in_specs=[ANYWHERE] * count + specs...]
    ppermute x3, waiting for transfers between devices: 16.5 us -> 4.79 us  [step(): lax.ppermute(self.right[-1][half:], 'dp', self.back)]
    pallas_call x6 -> x5, Pallas kernels: 70.7 us -> 62.1 us  [matmul(): pl.pallas_call(kernel, grid=(grid,), in_specs=[spec for both in specs for...]
    unnamed x313 -> x309, local copies, waits for them, and re-layouts: 65.6 us -> 61.6 us
  transfers between devices with their start and end apart: 116 -> 116, of which waited for: 55 -> 54; matrix products, arithmetic and copies ran while one was open for 9% -> 9% of each run, Pallas kernels for 30% -> 30%
where the time goes in v4:
time: 972 us; the launch traced here: 964 us
  Pallas kernels  354 us (36%)
  waiting for transfers between devices  340 us (35%)
  starting transfers between devices  110 us (11%)
  local copies, waits for them, and re-layouts  97.1 us (10%)
  other arithmetic  48.1 us (5%)
  matrix products  11.1 us (1%)
    pallas_call x9, Pallas kernels, kernel_call(): pl.pallas_call(body, grid_spec=pltpu.PrefetchScalarGridSpec(num_scalar_pr...  107 us
    ppermute x60, waiting for transfers between devices, swap(): lax.ppermute(value, axis, [(at, at ^ bit) for at in range(lax.axis_size(a...  97.1 us
    ppermute x12, waiting for transfers between devices, step(): self.left = lax.ppermute(up, 'dp', self.ahead)  87.9 us
    pallas_call x15, Pallas kernels, row_blocks(): pl.pallas_call(kernel, grid=(len(blocks),), in_specs=[pl.BlockSpec((left....  77.3 us
    pallas_call x5, Pallas kernels, matmul(): pl.pallas_call(kernel, grid=(grid,), in_specs=[spec for both in specs for...  62.1 us
    unnamed x309, local copies, waits for them, and re-layouts  61.6 us
    ppermute x9, waiting for transfers between devices, step(): self.left.append(lax.ppermute(self.left[-1], 'dp', self.ahead))  60.5 us
    pallas_call x3, Pallas kernels, weighted(): pl.pallas_call(kernel, grid=(steps,), in_specs=[ANYWHERE] * count + specs...  58.7 us
  transfers between devices with their start and end apart: 116, of which 54 were waited for; matrix products, arithmetic and copies ran while one was open for 9% of the time, Pallas kernels for 30%

profile of v4, /device:TPU:0, one launch (start us, length us, event | category | flops | bytes accessed | tf_op | source)
XLA Modules:
  0.0 963.6 jit_solution(8404355283394250096)
XLA Ops:
  11.2 22.2 %collective-permute-done.3.refs_8_ = bf16[256,2176]{1,0:T(8,128)(2,1)} collective-permute-done((bf16[256,2176]{1,0:T(8,128)(2,1)}, bf16[256,2176]{1,0:T(8,128)(2,1)}, u32[]{:S(2)}, u32[]{:S(2)}) %collective-permute-start.3) | collective-permute-done | bytes 1114144 | tf_op jit(solution)/shard_map/ppermute | solution.py:1228
  40.4 19.1 %collective-permute-done.4.refs_3_.refs_7_ = bf16[256,2176]{1,0:T(8,128)(2,1)} collective-permute-done((bf16[256,2176]{1,0:T(8,128)(2,1)}, bf16[256,2176]{1,0:T(8,128)(2,1)}, u32[]{:S(2)}, u32[]{:S(2)}) %collective-permute-start.4) | collective-permute-done | bytes 1114144 | tf_op jit(solution)/shard_map/ppermute | solution.py:1228
  73.7 10.9 %collective-permute-done.5.refs_5_.refs_6_ = bf16[256,2176]{1,0:T(8,128)(2,1)} collective-permute-done((bf16[256,2176]{1,0:T(8,128)(2,1)}, bf16[256,2176]{1,0:T(8,128)(2,1)}, u32[]{:S(2)}, u32[]{:S(2)}) %collective-permute-start.5) | collective-permute-done | bytes 1114144 | tf_op jit(solution)/shard_map/ppermute | solution.py:1228
  116.1 18.1 %project.1 = (bf16[2048,2176]{1,0:T(8,128)(2,1)}, f32[1024,2176]{1,0:T(8,128)}, f32[32,2176]{1,0:T(8,128)S(1)}) custom-call(bf16[256,2176]{1,0:T(8,128)(2,1)} %concatenate.62.refs_0_, bf16[256,2176]{1,0:T(8,128)(2,1)} %collective-permute-done.refs_1_, bf16[256,2176]{1,0:T(8,128)(2,1)} %collective-permute-done.1.refs_4_.refs_2_, ...), custom_call_target="tpu_custom_call" | custom-call | tf_op jit(solution)/shard_map/project/pallas_call | solution.py:800
  143.0 36.0 %mix_forward.1 = (f32[1024,1024]{1,0:T(8,128)}, bf16[1024,512]{1,0:T(8,128)(2,1)S(1)}, bf16[8,4,128,128]{3,2,1,0:T(8,128)(2,1)S(1)}, bf16[8,4,128,384]{3,2,1,0:T(8,128)(2,1)}, f32[2,4,128,384]{3,2,1,0:T(8,128)S(1)}) custom-call(s32[2,6]{1,0:T(2,128)S(1)} %add_add_fusion.1.refs_0_, f32[1024,2176]{1,0:T(8,128)} %get-tuple-element.98.refs_1_.refs_2_, ...), custom_call_target="tpu_custom_call" | custom-call | tf_op jit(solution)/shard_map/mix_forward/pallas_call | solution.py:539
  181.9 30.3 %collective-permute-done.17.refs_0_ = bf16[4,128,384]{2,1,0:T(8,128)(2,1)S(1)} collective-permute-done((bf16[4,128,384]{2,1,0:T(8,128)(2,1)S(1)}, bf16[4,128,384]{2,1,0:T(8,128)(2,1)S(1)}, u32[]{:S(2)}, u32[]{:S(2)}) %collective-permute-start.17) | collective-permute-done | bytes 393248 | tf_op jit(solution)/shard_map/ppermute | solution.py:1072
  232.0 8.5 collective-permute-done.23.refs_3_
  296.0 11.2 %gate_project.1 = (bf16[2048,1024]{1,0:T(8,128)(2,1)}, bf16[2048,1024]{1,0:T(8,128)(2,1)}, f32[1024,1024]{1,0:T(8,128)}) custom-call(bf16[256,2048]{1,0:T(8,128)(2,1)S(1)} %copy-done.12, bf16[256,2048]{1,0:T(8,128)(2,1)} %tie.55.refs_2_.refs_1_, bf16[256,2048]{1,0:T(8,128)(2,1)S(1)} %copy-done.33, bf16[256,2048]{1,0:T(8,128)(2,1)} %tie.62.refs_3_, ...), custom_call_target="tpu_custom_call" | custom-call | tf_op jit(solution)/shard_map/gate_project/pallas_call | solution.py:800
  307.3 8.9 gate_forward.1
  317.5 7.4 matmul.5
  326.9 13.6 %collective-permute-done.38.refs_0_ = bf16[256,4224]{1,0:T(8,128)(2,1)} collective-permute-done((bf16[256,4224]{1,0:T(8,128)(2,1)}, bf16[256,4224]{1,0:T(8,128)(2,1)}, u32[]{:S(2)}, u32[]{:S(2)}) %collective-permute-start.38) | collective-permute-done | bytes 2162720 | tf_op jit(solution)/shard_map/ppermute | solution.py:1229
  347.8 9.7 %collective-permute-done.43.refs_0_ = bf16[128,2048]{1,0:T(8,128)(2,1)} collective-permute-done((bf16[128,2048]{1,0:T(8,128)(2,1)S(1)}, bf16[128,2048]{1,0:T(8,128)(2,1)}, u32[]{:S(2)}, u32[]{:S(2)}) %collective-permute-start.43) | collective-permute-done | bytes 524320 | tf_op jit(solution)/shard_map/ppermute | solution.py:1072
  357.5 10.8 %collective-permute-done.40.refs_0_ = bf16[128,2048]{1,0:T(8,128)(2,1)} collective-permute-done((bf16[128,2048]{1,0:T(8,128)(2,1)S(1)}, bf16[128,2048]{1,0:T(8,128)(2,1)}, u32[]{:S(2)}, u32[]{:S(2)}) %collective-permute-start.40) | collective-permute-done | bytes 524320 | tf_op jit(solution)/shard_map/ppermute | solution.py:1072
  374.6 12.8 %collective-permute-done.45.refs_1_ = bf16[128,2048]{1,0:T(8,128)(2,1)S(1)} collective-permute-done((bf16[128,2048]{1,0:T(8,128)(2,1)S(1)}, bf16[128,2048]{1,0:T(8,128)(2,1)S(1)}, u32[]{:S(2)}, u32[]{:S(2)}) %collective-permute-start.45) | collective-permute-done | bytes 524320 | tf_op jit(solution)/shard_map/ppermute | solution.py:1072
  407.6 14.5 %collective-permute-done.47.refs_4_ = bf16[128,4224]{1,0:T(8,128)(2,1)S(1)} collective-permute-done((bf16[128,4224]{1,0:T(8,128)(2,1)}, bf16[128,4224]{1,0:T(8,128)(2,1)S(1)}, u32[]{:S(2)}, u32[]{:S(2)}) %collective-permute-start.47) | collective-permute-done | bytes 1081376 | tf_op jit(solution)/shard_map/ppermute | solution.py:1233
  424.7 29.4 %feed_forward.1 = (bf16[2048,2816]{1,0:T(8,128)(2,1)}, bf16[2048,1408]{1,0:T(8,128)(2,1)}, bf16[1024,1408]{1,0:T(8,128)(2,1)}, bf16[1024,2816]{1,0:T(8,128)(2,1)}) custom-call(bf16[256,4224]{1,0:T(8,128)(2,1)S(1)} %copy-done.7, bf16[256,4224]{1,0:T(8,128)(2,1)} %tie.65.refs_11_.refs_1_, bf16[256,4224]{1,0:T(8,128)(2,1)} %tie.67.refs_2_, ...), custom_call_target="tpu_custom_call" | custom-call | tf_op jit(solution)/shard_map/feed_forward/pallas_call | solution.py:800
  454.2 17.1 %matmul.6 = (bf16[512,2048]{1,0:T(8,128)(2,1)S(1)}, bf16[128,2048]{1,0:T(8,128)(2,1)}, bf16[128,2048]{1,0:T(8,128)(2,1)}, bf16[128,2048]{1,0:T(8,128)(2,1)S(1)}, bf16[128,2048]{1,0:T(8,128)(2,1)S(1)}) custom-call(bf16[1024,2816]{1,0:T(8,128)(2,1)} %get-tuple-element.115.refs_0_.right_ref, bf16[2048,2816]{1,0:T(8,128)(2,1)} %get-tuple-element.116.refs_1_), custom_call_target="tpu_custom_call" | custom-call | tf_op jit(solution)/shard_map/matmul/pallas_call | solution.py:751
  524.6 7.7 row_blocks.20.refs_4_.refs_1_.refs_3_
  532.4 12.6 %row_blocks.19.refs_3_.refs_0_.refs_2_ = bf16[1280,2816]{1,0:T(8,128)(2,1)} custom-call(bf16[1024,2048]{1,0:T(8,128)(2,1)S(1)} %copy-done.3, bf16[1024,2816]{1,0:T(8,128)(2,1)} %get-tuple-element.115.refs_0_.right_ref, bf16[256,2048]{1,0:T(8,128)(2,1)S(1)} %get-tuple-element.200.refs_0_), custom_call_target="tpu_custom_call" | custom-call | tf_op jit(solution)/shard_map/row_blocks/pallas_call | solution.py:685
  553.1 7.6 matmul.7.refs_1_
  564.2 10.5 %gate_backward.1 = (bf16[1024,1024]{1,0:T(8,128)(2,1)S(1)}, f32[1024,1024]{1,0:T(8,128)}, f32[2,4,128,256]{3,2,1,0:T(8,128)S(1)}, f32[8,256]{1,0:T(8,128)S(1)}) custom-call(s32[2,6]{1,0:T(2,128)S(1)} %add_add_fusion.1.refs_0_, f32[1024,1024]{1,0:T(8,128)} %copy-done.36, f32[1024,1024]{1,0:T(8,128)} %get-tuple-element.126.refs_2_, ...), custom_call_target="tpu_custom_call" | custom-call | tf_op jit(solution)/shard_map/gate_backward/pallas_call | solution.py:539
  607.5 10.2 %matmul.8 = (bf16[512,2048]{1,0:T(8,128)(2,1)S(1)}, bf16[128,2048]{1,0:T(8,128)(2,1)S(1)}, bf16[128,2048]{1,0:T(8,128)(2,1)S(1)}, bf16[128,2048]{1,0:T(8,128)(2,1)S(1)}, bf16[128,2048]{1,0:T(8,128)(2,1)S(1)}) custom-call(bf16[1024,1408]{1,0:T(8,128)(2,1)} %get-tuple-element.113.right_ref.refs_0_, bf16[2048,1408]{1,0:T(8,128)(2,1)} %get-tuple-element.114.refs_1_, ...), custom_call_target="tpu_custom_call" | custom-call | tf_op jit(solution)/shard_map/matmul/pallas_call | solution.py:751
  642.4 9.6 collective-permute-done.75.refs_7_.refs_4_
  662.9 46.2 %mix_backward.1 = (bf16[1024,2176]{1,0:T(8,128)(2,1)}, f32[2,8,2048]{2,1,0:T(8,128)S(1)}, f32[2,16,2048]{2,1,0:T(8,128)S(1)}, f32[8,2048]{1,0:T(8,128)S(1)}, f32[8,128]{1,0:T(8,128)S(1)}) custom-call(s32[2,6]{1,0:T(2,128)S(1)} %add_add_fusion.1.refs_0_, f32[1024,2176]{1,0:T(8,128)} %get-tuple-element.98.refs_1_.refs_2_, ...), custom_call_target="tpu_custom_call" | custom-call | tf_op jit(solution)/shard_map/mix_backward/pallas_call | solution.py:539
  711.2 19.7 %collective-permute-done.80.refs_6_.refs_1_ = f32[2,8,2048]{2,1,0:T(8,128)S(1)} collective-permute-done((f32[2,8,2048]{2,1,0:T(8,128)S(1)}, f32[2,8,2048]{2,1,0:T(8,128)S(1)}, u32[]{:S(2)}, u32[]{:S(2)}) %collective-permute-start.80) | collective-permute-done | bytes 131104 | tf_op jit(solution)/shard_map/ppermute | solution.py:1068
  757.2 11.4 %row_blocks.28.refs_5_.refs_0_.refs_1_ = bf16[1280,2176]{1,0:T(8,128)(2,1)} custom-call(bf16[1024,2048]{1,0:T(8,128)(2,1)S(1)} %copy-done.2, bf16[1024,2176]{1,0:T(8,128)(2,1)} %bitcast.21.right_ref.refs_0_, bf16[128,2176]{1,0:T(8,128)(2,1)S(1)} %get-tuple-element.147.refs_0_, bf16[128,2176]{1,0:T(8,128)(2,1)S(1)} %get-tuple-element.148.refs_1_), custom_call_target="tpu_custom_call" | custom-call | tf_op jit(solution)/shard_map/row_blocks/pallas_call | solution.py:685
  768.7 19.7 %matmul.9 = (bf16[512,2048]{1,0:T(8,128)(2,1)S(1)}, bf16[128,2048]{1,0:T(8,128)(2,1)}, bf16[128,2048]{1,0:T(8,128)(2,1)}, bf16[128,2048]{1,0:T(8,128)(2,1)S(1)}, bf16[128,2048]{1,0:T(8,128)(2,1)}) custom-call(bf16[1024,2176]{1,0:T(8,128)(2,1)} %bitcast.21.right_ref.refs_0_, bf16[2048,2176]{1,0:T(8,128)(2,1)} %get-tuple-element.149.refs_1_, ...), custom_call_target="tpu_custom_call" | custom-call | tf_op jit(solution)/shard_map/matmul/pallas_call | solution.py:751
  789.7 11.3 %collective-permute-done.86.refs_12_.refs_2_ = bf16[128,2176]{1,0:T(8,128)(2,1)S(1)} collective-permute-done((bf16[128,2176]{1,0:T(8,128)(2,1)S(1)}, bf16[128,2176]{1,0:T(8,128)(2,1)S(1)}, u32[]{:S(2)}, u32[]{:S(2)}) %collective-permute-start.86) | collective-permute-done | bytes 557088 | tf_op jit(solution)/shard_map/ppermute | solution.py:1303
  812.1 16.9 %collective-permute-done.92.refs_6_.refs_4_ = bf16[256,2048]{1,0:T(8,128)(2,1)S(1)} collective-permute-done((bf16[256,2048]{1,0:T(8,128)(2,1)S(1)}, bf16[256,2048]{1,0:T(8,128)(2,1)S(1)}, u32[]{:S(2)}, u32[]{:S(2)}) %collective-permute-start.92) | collective-permute-done | bytes 1048608 | tf_op jit(solution)/shard_map/ppermute | solution.py:1303
  843.4 13.7 %collective-permute-done.94.refs_2_ = bf16[256,2176]{1,0:T(8,128)(2,1)} collective-permute-done((bf16[256,2176]{1,0:T(8,128)(2,1)S(1)}, bf16[256,2176]{1,0:T(8,128)(2,1)}, u32[]{:S(2)}, u32[]{:S(2)}) %collective-permute-start.94) | collective-permute-done | bytes 1114144 | tf_op jit(solution)/shard_map/ppermute | solution.py:1303
  871.8 11.5 %collective-permute-done.98.refs_6_.refs_0_ = bf16[256,2048]{1,0:T(8,128)(2,1)S(1)} collective-permute-done((bf16[256,2048]{1,0:T(8,128)(2,1)}, bf16[256,2048]{1,0:T(8,128)(2,1)S(1)}, u32[]{:S(2)}, u32[]{:S(2)}) %collective-permute-start.98) | collective-permute-done | bytes 1048608 | tf_op jit(solution)/shard_map/ppermute | solution.py:1303
  884.8 19.3 %collective-permute-done.96.refs_2_ = bf16[256,2176]{1,0:T(8,128)(2,1)} collective-permute-done((bf16[256,2176]{1,0:T(8,128)(2,1)S(1)}, bf16[256,2176]{1,0:T(8,128)(2,1)}, u32[]{:S(2)}, u32[]{:S(2)}) %collective-permute-start.96) | collective-permute-done | bytes 1114144 | tf_op jit(solution)/shard_map/ppermute | solution.py:1303
  (735 shorter events, 451.7 us)
Async XLA Ops:
  35.5 30.3 %collective-permute-start.1 = (bf16[256,2176]{1,0:T(8,128)(2,1)}, bf16[256,2176]{1,0:T(8,128)(2,1)}, u32[]{:S(2)}, u32[]{:S(2)}) collective-permute-start(bf16[256,2176]{1,0:T(8,128)(2,1)} %collective-permute-done.refs_1_), channel_id=1, source_target_pairs={{8,0},{16,8},{24,16},{28,24},{20,28},{12,20},{4,12},{0,4},{9,1},{1... | collective-permute-start | bytes 3342344 | tf_op jit(solution)/shard_map/ppermute | solution.py:1229
  36.9 30.8 %collective-permute-start.8 = (bf16[128,2048]{1,0:T(8,128)(2,1)}, bf16[128,2048]{1,0:T(8,128)(2,1)}, u32[]{:S(2)}, u32[]{:S(2)}) collective-permute-start(bf16[128,2048]{1,0:T(8,128)(2,1)} %get-tuple-element.256), channel_id=1, source_target_pairs={{0,2},{1,3},{2,0},{3,1},{4,6},{5,7},{6,4},{7,5},{8,10},{9,11},{10,... | collective-permute-start | bytes 1572872 | tf_op jit(solution)/shard_map/ppermute | solution.py:1072
  38.6 29.0 %collective-permute-start.9 = (bf16[128,2048]{1,0:T(8,128)(2,1)}, bf16[128,2048]{1,0:T(8,128)(2,1)}, u32[]{:S(2)}, u32[]{:S(2)}) collective-permute-start(bf16[128,2048]{1,0:T(8,128)(2,1)} %get-tuple-element.255), channel_id=1, source_target_pairs={{0,2},{1,3},{2,0},{3,1},{4,6},{5,7},{6,4},{7,5},{8,10},{9,11},{10,... | collective-permute-start | bytes 1572872 | tf_op jit(solution)/shard_map/ppermute | solution.py:1072
  135.9 76.5 %collective-permute-start.20 = (bf16[256,4224]{1,0:T(8,128)(2,1)}, bf16[256,4224]{1,0:T(8,128)(2,1)}, u32[]{:S(2)}, u32[]{:S(2)}) collective-permute-start(bf16[256,4224]{1,0:T(8,128)(2,1)} %tie.56.refs_5_.refs_6_.refs_0_), channel_id=1, source_target_pairs={{0,8},{8,16},{16,24},{24,28},{28,20},{20,12},{12,4},{4,0},{1,9},{9... | collective-permute-start | bytes 6488072 | tf_op jit(solution)/shard_map/ppermute | solution.py:1228
  137.9 75.1 %collective-permute-start.21 = (bf16[256,4224]{1,0:T(8,128)(2,1)}, bf16[256,4224]{1,0:T(8,128)(2,1)}, u32[]{:S(2)}, u32[]{:S(2)}) collective-permute-start(bf16[256,4224]{1,0:T(8,128)(2,1)} %tie.56.refs_5_.refs_6_.refs_0_), channel_id=1, source_target_pairs={{8,0},{16,8},{24,16},{28,24},{20,28},{12,20},{4,12},{0,4},{9,1},{1... | collective-permute-start | bytes 6488072 | tf_op jit(solution)/shard_map/ppermute | solution.py:1229
  139.1 73.1 %collective-permute-start.19 = (bf16[256,2048]{1,0:T(8,128)(2,1)}, bf16[256,2048]{1,0:T(8,128)(2,1)S(1)}, u32[]{:S(2)}, u32[]{:S(2)}) collective-permute-start(bf16[256,2048]{1,0:T(8,128)(2,1)} %tie.55.refs_2_.refs_1_), channel_id=1, source_target_pairs={{8,0},{16,8},{24,16},{28,24},{20,28},{12,20},{4,12},{0,4},{9,1},{1... | collective-permute-start | bytes 3145736 | tf_op jit(solution)/shard_map/ppermute | solution.py:1229
  139.6 72.7 %collective-permute-start.18 = (bf16[256,2048]{1,0:T(8,128)(2,1)}, bf16[256,2048]{1,0:T(8,128)(2,1)S(1)}, u32[]{:S(2)}, u32[]{:S(2)}) collective-permute-start(bf16[256,2048]{1,0:T(8,128)(2,1)} %tie.54.refs_1_.refs_8_), channel_id=1, source_target_pairs={{0,8},{8,16},{16,24},{24,28},{28,20},{20,12},{12,4},{4,0},{1,9},{9... | collective-permute-start | bytes 3145736 | tf_op jit(solution)/shard_map/ppermute | solution.py:1228
  180.1 32.2 %collective-permute-start.17 = (bf16[4,128,384]{2,1,0:T(8,128)(2,1)S(1)}, bf16[4,128,384]{2,1,0:T(8,128)(2,1)S(1)}, u32[]{:S(2)}, u32[]{:S(2)}) collective-permute-start(bf16[4,128,384]{2,1,0:T(8,128)(2,1)S(1)} %fusion.20.refs_1_), channel_id=1, source_target_pairs={{0,4},{4,0},{8,12},{12,8},{16,20},{20,16},{24,28},{28,24},{1,5},{5... | collective-permute-start | bytes 1179656 | tf_op jit(solution)/shard_map/ppermute | solution.py:1072
  219.3 35.2 %collective-permute-start.25 = (bf16[128,2048]{1,0:T(8,128)(2,1)}, bf16[128,2048]{1,0:T(8,128)(2,1)}, u32[]{:S(2)}, u32[]{:S(2)}) collective-permute-start(bf16[128,2048]{1,0:T(8,128)(2,1)} %get-tuple-element.254), channel_id=1, source_target_pairs={{0,2},{1,3},{2,0},{3,1},{4,6},{5,7},{6,4},{7,5},{8,10},{9,11},{10,... | collective-permute-start | bytes 1572872 | tf_op jit(solution)/shard_map/ppermute | solution.py:1072
  220.8 33.7 %collective-permute-start.26 = (bf16[128,2048]{1,0:T(8,128)(2,1)}, bf16[128,2048]{1,0:T(8,128)(2,1)}, u32[]{:S(2)}, u32[]{:S(2)}) collective-permute-start(bf16[128,2048]{1,0:T(8,128)(2,1)} %get-tuple-element.253), channel_id=1, source_target_pairs={{0,2},{1,3},{2,0},{3,1},{4,6},{5,7},{6,4},{7,5},{8,10},{9,11},{10,... | collective-permute-start | bytes 1572872 | tf_op jit(solution)/shard_map/ppermute | solution.py:1072
  291.4 49.2 %collective-permute-start.38 = (bf16[256,4224]{1,0:T(8,128)(2,1)}, bf16[256,4224]{1,0:T(8,128)(2,1)}, u32[]{:S(2)}, u32[]{:S(2)}) collective-permute-start(bf16[256,4224]{1,0:T(8,128)(2,1)} %tie.65.refs_11_.refs_1_), channel_id=1, source_target_pairs={{8,0},{16,8},{24,16},{28,24},{20,28},{12,20},{4,12},{0,4},{9,1},{1... | collective-permute-start | bytes 6488072 | tf_op jit(solution)/shard_map/ppermute | solution.py:1229
  291.4 49.2 %collective-permute-start.37 = (bf16[256,4224]{1,0:T(8,128)(2,1)}, bf16[256,4224]{1,0:T(8,128)(2,1)}, u32[]{:S(2)}, u32[]{:S(2)}) collective-permute-start(bf16[256,4224]{1,0:T(8,128)(2,1)} %tie.64.refs_10_.refs_8_), channel_id=1, source_target_pairs={{0,8},{8,16},{16,24},{24,28},{28,20},{20,12},{12,4},{4,0},{1,9},{9... | collective-permute-start | bytes 6488072 | tf_op jit(solution)/shard_map/ppermute | solution.py:1228
  345.5 49.2 %collective-permute-start.46 = (bf16[256,4224]{1,0:T(8,128)(2,1)}, bf16[256,4224]{1,0:T(8,128)(2,1)}, u32[]{:S(2)}, u32[]{:S(2)}) collective-permute-start(bf16[256,4224]{1,0:T(8,128)(2,1)} %tie.66.refs_1_.refs_7_), channel_id=1, source_target_pairs={{0,8},{8,16},{16,24},{24,28},{28,20},{20,12},{12,4},{4,0},{1,9},{9... | collective-permute-start | bytes 6488072 | tf_op jit(solution)/shard_map/ppermute | solution.py:1228
  347.3 51.5 %collective-permute-start.44 = (bf16[256,4224]{1,0:T(8,128)(2,1)}, bf16[256,4224]{1,0:T(8,128)(2,1)}, u32[]{:S(2)}, u32[]{:S(2)}) collective-permute-start(bf16[256,4224]{1,0:T(8,128)(2,1)} %tie.67.refs_2_), channel_id=1, source_target_pairs={{8,0},{16,8},{24,16},{28,24},{20,28},{12,20},{4,12},{0,4},{9,1},{1... | collective-permute-start | bytes 6488072 | tf_op jit(solution)/shard_map/ppermute | solution.py:1229
  514.7 48.1 %collective-permute-start.68 = (bf16[256,4224]{1,0:T(8,128)(2,1)}, bf16[256,4224]{1,0:T(8,128)(2,1)}, u32[]{:S(2)}, u32[]{:S(2)}) collective-permute-start(bf16[256,4224]{1,0:T(8,128)(2,1)} %get-tuple-element.124.refs_1_), channel_id=1, source_target_pairs={{0,8},{8,16},{16,24},{24,28},{28,20},{20,12},{12,4},{4,0},{1,9},{9... | collective-permute-start | bytes 6488072 | tf_op jit(solution)/shard_map/ppermute | solution.py:1303
  516.4 47.8 %collective-permute-start.69 = (bf16[256,4224]{1,0:T(8,128)(2,1)}, bf16[256,4224]{1,0:T(8,128)(2,1)}, u32[]{:S(2)}, u32[]{:S(2)}) collective-permute-start(bf16[256,4224]{1,0:T(8,128)(2,1)} %get-tuple-element.125.refs_2_), channel_id=1, source_target_pairs={{8,0},{16,8},{24,16},{28,24},{20,28},{12,20},{4,12},{0,4},{9,1},{1... | collective-permute-start | bytes 6488072 | tf_op jit(solution)/shard_map/ppermute | solution.py:1304
  592.8 30.9 %collective-permute-start.72 = (bf16[4,128,384]{2,1,0:T(8,128)(2,1)S(1)}, bf16[4,128,384]{2,1,0:T(8,128)(2,1)}, u32[]{:S(2)}, u32[]{:S(2)}) collective-permute-start(bf16[4,128,384]{2,1,0:T(8,128)(2,1)S(1)} %pad_maximum_fusion.6.refs_0_), channel_id=1, source_target_pairs={{8,0},{12,4},{16,8},{20,12},{24,16},{28,20},{9,1},{13,5},{17,9},{2... | collective-permute-start | bytes 1179656 | tf_op jit(solution)/shard_map/ppermute | solution.py:1068
  594.1 35.9 %collective-permute-start.73 = (bf16[4,128,384]{2,1,0:T(8,128)(2,1)S(1)}, bf16[4,128,384]{2,1,0:T(8,128)(2,1)}, u32[]{:S(2)}, u32[]{:S(2)}) collective-permute-start(bf16[4,128,384]{2,1,0:T(8,128)(2,1)S(1)} %pad_maximum_fusion.6.refs_0_), channel_id=1, source_target_pairs={{16,0},{20,4},{24,8},{28,12},{17,1},{21,5},{25,9},{29,13},{18,2},{... | collective-permute-start | bytes 1179656 | tf_op jit(solution)/shard_map/ppermute | solution.py:1068
  657.3 75.2 %collective-permute-start.78 = (bf16[256,4224]{1,0:T(8,128)(2,1)}, bf16[256,4224]{1,0:T(8,128)(2,1)}, u32[]{:S(2)}, u32[]{:S(2)}) collective-permute-start(bf16[256,4224]{1,0:T(8,128)(2,1)} %get-tuple-element.136.refs_6_), channel_id=1, source_target_pairs={{0,8},{8,16},{16,24},{24,28},{28,20},{20,12},{12,4},{4,0},{1,9},{9... | collective-permute-start | bytes 6488072 | tf_op jit(solution)/shard_map/ppermute | solution.py:1303
  657.4 75.2 %collective-permute-start.79 = (bf16[256,4224]{1,0:T(8,128)(2,1)}, bf16[256,4224]{1,0:T(8,128)(2,1)}, u32[]{:S(2)}, u32[]{:S(2)}) collective-permute-start(bf16[256,4224]{1,0:T(8,128)(2,1)} %get-tuple-element.137.refs_7_), channel_id=1, source_target_pairs={{8,0},{16,8},{24,16},{28,24},{20,28},{12,20},{4,12},{0,4},{9,1},{1... | collective-permute-start | bytes 6488072 | tf_op jit(solution)/shard_map/ppermute | solution.py:1304
  660.9 70.6 %collective-permute-start.81 = (bf16[256,2048]{1,0:T(8,128)(2,1)}, bf16[256,2048]{1,0:T(8,128)(2,1)S(1)}, u32[]{:S(2)}, u32[]{:S(2)}) collective-permute-start(bf16[256,2048]{1,0:T(8,128)(2,1)} %get-tuple-element.138.refs_11_), channel_id=1, source_target_pairs={{0,8},{8,16},{16,24},{24,28},{28,20},{20,12},{12,4},{4,0},{1,9},{9... | collective-permute-start | bytes 3145736 | tf_op jit(solution)/shard_map/ppermute | solution.py:1303
  660.9 70.6 %collective-permute-start.82 = (bf16[256,2048]{1,0:T(8,128)(2,1)}, bf16[256,2048]{1,0:T(8,128)(2,1)S(1)}, u32[]{:S(2)}, u32[]{:S(2)}) collective-permute-start(bf16[256,2048]{1,0:T(8,128)(2,1)} %get-tuple-element.139.refs_12_), channel_id=1, source_target_pairs={{8,0},{16,8},{24,16},{28,24},{20,28},{12,20},{4,12},{0,4},{9,1},{1... | collective-permute-start | bytes 3145736 | tf_op jit(solution)/shard_map/ppermute | solution.py:1304
  739.6 61.9 %collective-permute-start.89 = (bf16[256,4224]{1,0:T(8,128)(2,1)S(1)}, bf16[256,4224]{1,0:T(8,128)(2,1)}, u32[]{:S(2)}, u32[]{:S(2)}) collective-permute-start(bf16[256,4224]{1,0:T(8,128)(2,1)S(1)} %get-tuple-element.141.refs_1_), channel_id=1, source_target_pairs={{0,8},{8,16},{16,24},{24,28},{28,20},{20,12},{12,4},{4,0},{1,9},{9... | collective-permute-start | bytes 6488072 | tf_op jit(solution)/shard_map/ppermute | solution.py:1303
  739.7 61.8 %collective-permute-start.90 = (bf16[256,4224]{1,0:T(8,128)(2,1)}, bf16[256,4224]{1,0:T(8,128)(2,1)}, u32[]{:S(2)}, u32[]{:S(2)}) collective-permute-start(bf16[256,4224]{1,0:T(8,128)(2,1)} %get-tuple-element.142.refs_2_), channel_id=1, source_target_pairs={{8,0},{16,8},{24,16},{28,24},{20,28},{12,20},{4,12},{0,4},{9,1},{1... | collective-permute-start | bytes 6488072 | tf_op jit(solution)/shard_map/ppermute | solution.py:1304
  749.7 51.3 %collective-permute-start.86 = (bf16[128,2176]{1,0:T(8,128)(2,1)S(1)}, bf16[128,2176]{1,0:T(8,128)(2,1)S(1)}, u32[]{:S(2)}, u32[]{:S(2)}) collective-permute-start(bf16[128,2176]{1,0:T(8,128)(2,1)S(1)} %get-tuple-element.147.refs_0_), channel_id=1, source_target_pairs={{0,8},{8,16},{16,24},{24,28},{28,20},{20,12},{12,4},{4,0},{1,9},{9... | collective-permute-start | bytes 1671176 | tf_op jit(solution)/shard_map/ppermute | solution.py:1303
  749.8 51.6 %collective-permute-start.87 = (bf16[128,2176]{1,0:T(8,128)(2,1)S(1)}, bf16[128,2176]{1,0:T(8,128)(2,1)S(1)}, u32[]{:S(2)}, u32[]{:S(2)}) collective-permute-start(bf16[128,2176]{1,0:T(8,128)(2,1)S(1)} %get-tuple-element.148.refs_1_), channel_id=1, source_target_pairs={{8,0},{16,8},{24,16},{28,24},{20,28},{12,20},{4,12},{0,4},{9,1},{1... | collective-permute-start | bytes 1671176 | tf_op jit(solution)/shard_map/ppermute | solution.py:1304
  839.0 78.5 %collective-permute-start.101 = (bf16[128,2048]{1,0:T(8,128)(2,1)}, bf16[128,2048]{1,0:T(8,128)(2,1)}, u32[]{:S(2)}, u32[]{:S(2)}) collective-permute-start(bf16[128,2048]{1,0:T(8,128)(2,1)} %get-tuple-element.222.refs_1_), channel_id=1, source_target_pairs={{0,2},{1,3},{2,0},{3,1},{4,6},{5,7},{6,4},{7,5},{8,10},{9,11},{10,... | collective-permute-start | bytes 1572872 | tf_op jit(solution)/shard_map/ppermute | solution.py:1072
  862.6 41.6 %collective-permute-start.96 = (bf16[256,2176]{1,0:T(8,128)(2,1)S(1)}, bf16[256,2176]{1,0:T(8,128)(2,1)}, u32[]{:S(2)}, u32[]{:S(2)}) collective-permute-start(bf16[256,2176]{1,0:T(8,128)(2,1)S(1)} %get-tuple-element.162.refs_4_.refs_1_), channel_id=1, source_target_pairs={{0,8},{8,16},{16,24},{24,28},{28,20},{20,12},{12,4},{4,0},{1,9},{9... | collective-permute-start | bytes 3342344 | tf_op jit(solution)/shard_map/ppermute | solution.py:1303
  864.2 40.5 %collective-permute-start.97 = (bf16[256,2176]{1,0:T(8,128)(2,1)S(1)}, bf16[256,2176]{1,0:T(8,128)(2,1)}, u32[]{:S(2)}, u32[]{:S(2)}) collective-permute-start(bf16[256,2176]{1,0:T(8,128)(2,1)S(1)} %copy-done.41), channel_id=1, source_target_pairs={{8,0},{16,8},{24,16},{28,24},{20,28},{12,20},{4,12},{0,4},{9,1},{1... | collective-permute-start | bytes 3342344 | tf_op jit(solution)/shard_map/ppermute | solution.py:1304
  883.4 34.2 %collective-permute-start.84 = (bf16[128,2048]{1,0:T(8,128)(2,1)}, bf16[128,2048]{1,0:T(8,128)(2,1)}, u32[]{:S(2)}, u32[]{:S(2)}) collective-permute-start(bf16[128,2048]{1,0:T(8,128)(2,1)} %get-tuple-element.221.refs_0_), channel_id=1, source_target_pairs={{0,2},{1,3},{2,0},{3,1},{4,6},{5,7},{6,4},{7,5},{8,10},{9,11},{10,... | collective-permute-start | bytes 1572872 | tf_op jit(solution)/shard_map/ppermute | solution.py:1072
  908.2 48.9 %collective-permute-start.112 = (bf16[256,2176]{1,0:T(8,128)(2,1)}, bf16[256,2176]{1,0:T(8,128)(2,1)}, u32[]{:S(2)}, u32[]{:S(2)}) collective-permute-start(bf16[256,2176]{1,0:T(8,128)(2,1)} %get-tuple-element.164.refs_1_.refs_3_.refs_2_), channel_id=1, source_target_pairs={{0,8},{8,16},{16,24},{24,28},{28,20},{20,12},{12,4},{4,0},{1,9},{9... | collective-permute-start | bytes 3342344 | tf_op jit(solution)/shard_map/ppermute | solution.py:1303
  908.9 48.3 %collective-permute-start.113 = (bf16[256,2176]{1,0:T(8,128)(2,1)}, bf16[256,2176]{1,0:T(8,128)(2,1)}, u32[]{:S(2)}, u32[]{:S(2)}) collective-permute-start(bf16[256,2176]{1,0:T(8,128)(2,1)} %get-tuple-element.165.refs_2_.refs_4_.refs_3_), channel_id=1, source_target_pairs={{8,0},{16,8},{24,16},{28,24},{20,28},{12,20},{4,12},{0,4},{9,1},{1... | collective-permute-start | bytes 3342344 | tf_op jit(solution)/shard_map/ppermute | solution.py:1304
  (237 other events, 2928.4 us)

commit v5 on v4

--- a/solution.py
+++ b/solution.py
@@ -1493,8 +1493,8 @@
     scale_one = lax.rsqrt(jnp.mean(residual * residual, axis=-1, keepdims=True) + EPSILON)
     normed_one = residual * scale_one
     normed_rows = HeadGather((normed_one * attn_gain).astype(BF16))
-    conv_ring.step()
-    (pair,) = normed_rows.pass_on(*conv_ring.came(), gate_ring.left[0], ffn_ring.left[0])
+    conv_ring.step(gate_ring.left[0], ffn_ring.left[0])
+    normed_rows.pass_on(*conv_ring.came())
     conv_ring.step()
     normed_all = normed_rows.rows(*conv_ring.came())
     last_chunk = rank_block(ranks - 1, head_rank)
@@ -1515,14 +1515,14 @@
         axis=1,
     ).astype(jnp.int32)
     mix = Mix(info, micros, ranks, heads, key_size, value_size)
-    now = gate_ring.step(rim_rows, *conv_ring.far)
+    now = ffn_ring.step(rim_rows, *conv_ring.far)
+    now = gate_ring.step(*now)
     projected, rim, w_conv = project(normed_all, rim_rows, conv_ring.parts(), now)
-    now = gate_ring.step(rim)
-    now = ffn_ring.step(*now)
 
     plain, carried_map, inverses, starts, final = mix.forward(projected, rim, taps, par, now)
     scan = Scan(final, value_size)
-    now = scan.send(scan.sent, *gate_ring.came(), *ffn_ring.came())
+    now = gate_ring.step(scan.sent)
+    now = scan.send(*now, *ffn_ring.came())
     cotangent_rows = HeadGather(tie(cotangent, *now))
     now = gate_ring.step(*now, *scan.before)
     now = cotangent_rows.pass_on(*now)

time: 972 us -> 965 us (level)
  waiting for transfers between devices: 340 us -> 326 us
    ppermute x60, waiting for transfers between devices: 97.1 us -> 68.9 us  [swap(): lax.ppermute(value, axis, [(at, at ^ bit) for at in range(lax.axis_size(a...]
    ppermute x9, waiting for transfers between devices: 60.5 us -> 79 us  [step(): self.left.append(lax.ppermute(self.left[-1], 'dp', self.ahead))]
    unnamed x309 -> x307, local copies, waits for them, and re-layouts: 61.6 us -> 62.4 us
  transfers between devices with their start and end apart: 116 -> 116, of which waited for: 54 -> 56; matrix products, arithmetic and copies ran while one was open for 9% -> 9% of each run, Pallas kernels for 30% -> 30%
where the time goes in v5:
time: 965 us; the launch traced here: 955 us
  Pallas kernels  352 us (36%)
  waiting for transfers between devices  326 us (34%)
  starting transfers between devices  119 us (12%)
  local copies, waits for them, and re-layouts  94.6 us (10%)
  other arithmetic  49.5 us (5%)
  matrix products  11 us (1%)
    pallas_call x9, Pallas kernels, kernel_call(): pl.pallas_call(body, grid_spec=pltpu.PrefetchScalarGridSpec(num_scalar_pr...  107 us
    ppermute x12, waiting for transfers between devices, step(): self.left = lax.ppermute(up, 'dp', self.ahead)  89.1 us
    ppermute x9, waiting for transfers between devices, step(): self.left.append(lax.ppermute(self.left[-1], 'dp', self.ahead))  79 us
    pallas_call x15, Pallas kernels, row_blocks(): pl.pallas_call(kernel, grid=(len(blocks),), in_specs=[pl.BlockSpec((left....  76.4 us
    ppermute x60, waiting for transfers between devices, swap(): lax.ppermute(value, axis, [(at, at ^ bit) for at in range(lax.axis_size(a...  68.9 us
    unnamed x307, local copies, waits for them, and re-layouts  62.4 us
    pallas_call x5, Pallas kernels, matmul(): pl.pallas_call(kernel, grid=(grid,), in_specs=[spec for both in specs for...  61.7 us
    pallas_call x3, Pallas kernels, weighted(): pl.pallas_call(kernel, grid=(steps,), in_specs=[ANYWHERE] * count + specs...  58.5 us
  transfers between devices with their start and end apart: 116, of which 56 were waited for; matrix products, arithmetic and copies ran while one was open for 9% of the time, Pallas kernels for 30%

profile of v5, /device:TPU:0, one launch (start us, length us, event | category | flops | bytes accessed | tf_op | source)
XLA Modules:
  0.0 954.7 jit_solution(1995704260760383209)
XLA Ops:
  18.9 13.7 %collective-permute-done.3.refs_0_ = bf16[256,2176]{1,0:T(8,128)(2,1)} collective-permute-done((bf16[256,2176]{1,0:T(8,128)(2,1)S(1)}, bf16[256,2176]{1,0:T(8,128)(2,1)}, u32[]{:S(2)}, u32[]{:S(2)}) %collective-permute-start.3) | collective-permute-done | bytes 1114144 | tf_op jit(solution)/shard_map/ppermute | solution.py:1228
  37.5 21.1 %collective-permute-done.4.refs_3_.refs_7_ = bf16[256,2176]{1,0:T(8,128)(2,1)} collective-permute-done((bf16[256,2176]{1,0:T(8,128)(2,1)}, bf16[256,2176]{1,0:T(8,128)(2,1)}, u32[]{:S(2)}, u32[]{:S(2)}) %collective-permute-start.4) | collective-permute-done | bytes 1114144 | tf_op jit(solution)/shard_map/ppermute | solution.py:1228
  65.5 18.2 %collective-permute-done.5.refs_5_.refs_6_ = bf16[256,2176]{1,0:T(8,128)(2,1)S(1)} collective-permute-done((bf16[256,2176]{1,0:T(8,128)(2,1)}, bf16[256,2176]{1,0:T(8,128)(2,1)S(1)}, u32[]{:S(2)}, u32[]{:S(2)}) %collective-permute-start.5) | collective-permute-done | bytes 1114144 | tf_op jit(solution)/shard_map/ppermute | solution.py:1228
  117.8 17.9 %project.1 = (bf16[2048,2176]{1,0:T(8,128)(2,1)}, f32[1024,2176]{1,0:T(8,128)}, f32[32,2176]{1,0:T(8,128)S(1)}) custom-call(bf16[256,2176]{1,0:T(8,128)(2,1)S(1)} %copy-done.56, bf16[256,2176]{1,0:T(8,128)(2,1)} %tie.55.refs_1_, bf16[256,2176]{1,0:T(8,128)(2,1)S(1)} %copy-done.54, bf16[256,2176]{1,0:T(8,128)(2,1)} %copy-done.45, ...), custom_call_target="tpu_custom_call" | custom-call | tf_op jit(solution)/shard_map/project/pallas_call | solution.py:800
  135.8 35.9 %mix_forward.1 = (f32[1024,1024]{1,0:T(8,128)}, bf16[1024,512]{1,0:T(8,128)(2,1)S(1)}, bf16[8,4,128,128]{3,2,1,0:T(8,128)(2,1)S(1)}, bf16[8,4,128,384]{3,2,1,0:T(8,128)(2,1)}, f32[2,4,128,384]{3,2,1,0:T(8,128)S(1)}) custom-call(s32[2,6]{1,0:T(2,128)S(1)} %add_add_fusion.1.refs_0_, f32[1024,2176]{1,0:T(8,128)} %get-tuple-element.98.refs_1_.refs_2_, ...), custom_call_target="tpu_custom_call" | custom-call | tf_op jit(solution)/shard_map/mix_forward/pallas_call | solution.py:539
  198.2 10.9 %collective-permute-done.25.refs_0_ = bf16[256,2048]{1,0:T(8,128)(2,1)S(1)} collective-permute-done((bf16[256,2048]{1,0:T(8,128)(2,1)}, bf16[256,2048]{1,0:T(8,128)(2,1)S(1)}, u32[]{:S(2)}, u32[]{:S(2)}) %collective-permute-start.25) | collective-permute-done | bytes 1048608 | tf_op jit(solution)/shard_map/ppermute | solution.py:1228
  229.4 10.9 %collective-permute-start.29 = (bf16[256,2048]{1,0:T(8,128)(2,1)}, bf16[256,2048]{1,0:T(8,128)(2,1)}, u32[]{:S(2)}, u32[]{:S(2)}) collective-permute-start(bf16[256,2048]{1,0:T(8,128)(2,1)} %tie.63.refs_3_.refs_7_), channel_id=1, source_target_pairs={{0,8},{8,16},{16,24},{24,28},{28,20},{20,12},{12,4},{4,0},{1,9},{9... | collective-permute-start | bytes 3145736 | tf_op jit(solution)/shard_map/ppermute | solution.py:1228
  252.4 8.2 collective-permute-done.29.refs_0_
  287.7 11.2 %gate_project.1 = (bf16[2048,1024]{1,0:T(8,128)(2,1)}, bf16[2048,1024]{1,0:T(8,128)(2,1)}, f32[1024,1024]{1,0:T(8,128)}) custom-call(bf16[256,2048]{1,0:T(8,128)(2,1)S(1)} %copy-done.8, bf16[256,2048]{1,0:T(8,128)(2,1)S(1)} %copy-done.36, bf16[256,2048]{1,0:T(8,128)(2,1)} %tie.64.refs_4_.refs_2_, bf16[256,2048]{1,0:T(8,128)(2,1)} %tie.66.refs_3_, ...), custom_call_target="tpu_custom_call" | custom-call | tf_op jit(solution)/shard_map/gate_project/pallas_call | solution.py:800
  299.0 8.9 gate_forward.1
  318.6 12.1 %collective-permute-done.38.refs_0_ = bf16[256,4224]{1,0:T(8,128)(2,1)} collective-permute-done((bf16[256,4224]{1,0:T(8,128)(2,1)}, bf16[256,4224]{1,0:T(8,128)(2,1)}, u32[]{:S(2)}, u32[]{:S(2)}) %collective-permute-start.38) | collective-permute-done | bytes 2162720 | tf_op jit(solution)/shard_map/ppermute | solution.py:1229
  339.0 8.6 collective-permute-done.43.refs_0_
  347.7 10.8 %collective-permute-done.40.refs_0_ = bf16[128,2048]{1,0:T(8,128)(2,1)} collective-permute-done((bf16[128,2048]{1,0:T(8,128)(2,1)S(1)}, bf16[128,2048]{1,0:T(8,128)(2,1)}, u32[]{:S(2)}, u32[]{:S(2)}) %collective-permute-start.40) | collective-permute-done | bytes 524320 | tf_op jit(solution)/shard_map/ppermute | solution.py:1072
  364.8 12.8 %collective-permute-done.45.refs_1_ = bf16[128,2048]{1,0:T(8,128)(2,1)S(1)} collective-permute-done((bf16[128,2048]{1,0:T(8,128)(2,1)S(1)}, bf16[128,2048]{1,0:T(8,128)(2,1)S(1)}, u32[]{:S(2)}, u32[]{:S(2)}) %collective-permute-start.45) | collective-permute-done | bytes 524320 | tf_op jit(solution)/shard_map/ppermute | solution.py:1072
  397.4 13.9 %collective-permute-done.47.refs_4_ = bf16[128,4224]{1,0:T(8,128)(2,1)S(1)} collective-permute-done((bf16[128,4224]{1,0:T(8,128)(2,1)}, bf16[128,4224]{1,0:T(8,128)(2,1)S(1)}, u32[]{:S(2)}, u32[]{:S(2)}) %collective-permute-start.47) | collective-permute-done | bytes 1081376 | tf_op jit(solution)/shard_map/ppermute | solution.py:1233
  415.3 29.4 %feed_forward.1 = (bf16[2048,2816]{1,0:T(8,128)(2,1)}, bf16[2048,1408]{1,0:T(8,128)(2,1)}, bf16[1024,1408]{1,0:T(8,128)(2,1)}, bf16[1024,2816]{1,0:T(8,128)(2,1)}) custom-call(bf16[256,4224]{1,0:T(8,128)(2,1)S(1)} %copy-done.3, bf16[256,4224]{1,0:T(8,128)(2,1)} %tie.69.refs_11_.refs_1_, bf16[256,4224]{1,0:T(8,128)(2,1)} %tie.71.refs_2_, ...), custom_call_target="tpu_custom_call" | custom-call | tf_op jit(solution)/shard_map/feed_forward/pallas_call | solution.py:800
  444.7 17.1 %matmul.6 = (bf16[512,2048]{1,0:T(8,128)(2,1)S(1)}, bf16[128,2048]{1,0:T(8,128)(2,1)}, bf16[128,2048]{1,0:T(8,128)(2,1)}, bf16[128,2048]{1,0:T(8,128)(2,1)S(1)}, bf16[128,2048]{1,0:T(8,128)(2,1)S(1)}) custom-call(bf16[1024,2816]{1,0:T(8,128)(2,1)} %get-tuple-element.115.refs_0_.right_ref, bf16[2048,2816]{1,0:T(8,128)(2,1)} %get-tuple-element.116.refs_1_), custom_call_target="tpu_custom_call" | custom-call | tf_op jit(solution)/shard_map/matmul/pallas_call | solution.py:751
  515.4 7.7 row_blocks.20.refs_4_.refs_1_.refs_3_
  523.2 12.7 %row_blocks.19.refs_3_.refs_0_.refs_2_ = bf16[1280,2816]{1,0:T(8,128)(2,1)} custom-call(bf16[1024,2048]{1,0:T(8,128)(2,1)S(1)} %copy-done.4, bf16[1024,2816]{1,0:T(8,128)(2,1)} %get-tuple-element.115.refs_0_.right_ref, bf16[256,2048]{1,0:T(8,128)(2,1)S(1)} %get-tuple-element.200.refs_0_), custom_call_target="tpu_custom_call" | custom-call | tf_op jit(solution)/shard_map/row_blocks/pallas_call | solution.py:685
  543.9 7.6 matmul.7.refs_1_
  554.6 10.5 %gate_backward.1 = (bf16[1024,1024]{1,0:T(8,128)(2,1)S(1)}, f32[1024,1024]{1,0:T(8,128)}, f32[2,4,128,256]{3,2,1,0:T(8,128)S(1)}, f32[8,256]{1,0:T(8,128)S(1)}) custom-call(s32[2,6]{1,0:T(2,128)S(1)} %add_add_fusion.1.refs_0_, f32[1024,1024]{1,0:T(8,128)} %copy-done.29, f32[1024,1024]{1,0:T(8,128)} %get-tuple-element.126.refs_2_, ...), custom_call_target="tpu_custom_call" | custom-call | tf_op jit(solution)/shard_map/gate_backward/pallas_call | solution.py:539
  599.5 9.8 %matmul.8 = (bf16[512,2048]{1,0:T(8,128)(2,1)S(1)}, bf16[128,2048]{1,0:T(8,128)(2,1)S(1)}, bf16[128,2048]{1,0:T(8,128)(2,1)S(1)}, bf16[128,2048]{1,0:T(8,128)(2,1)S(1)}, bf16[128,2048]{1,0:T(8,128)(2,1)S(1)}) custom-call(bf16[1024,1408]{1,0:T(8,128)(2,1)} %get-tuple-element.113.right_ref.refs_0_, bf16[2048,1408]{1,0:T(8,128)(2,1)} %get-tuple-element.114.refs_1_, ...), custom_call_target="tpu_custom_call" | custom-call | tf_op jit(solution)/shard_map/matmul/pallas_call | solution.py:751
  633.6 9.6 %collective-permute-done.75.refs_7_.refs_4_ = bf16[128,2048]{1,0:T(8,128)(2,1)S(1)} collective-permute-done((bf16[128,2048]{1,0:T(8,128)(2,1)S(1)}, bf16[128,2048]{1,0:T(8,128)(2,1)S(1)}, u32[]{:S(2)}, u32[]{:S(2)}) %collective-permute-start.75) | collective-permute-done | bytes 524320 | tf_op jit(solution)/shard_map/ppermute | solution.py:1303
  653.9 46.2 %mix_backward.1 = (bf16[1024,2176]{1,0:T(8,128)(2,1)}, f32[2,8,2048]{2,1,0:T(8,128)S(1)}, f32[2,16,2048]{2,1,0:T(8,128)S(1)}, f32[8,2048]{1,0:T(8,128)S(1)}, f32[8,128]{1,0:T(8,128)S(1)}) custom-call(s32[2,6]{1,0:T(2,128)S(1)} %add_add_fusion.1.refs_0_, f32[1024,2176]{1,0:T(8,128)} %get-tuple-element.98.refs_1_.refs_2_, ...), custom_call_target="tpu_custom_call" | custom-call | tf_op jit(solution)/shard_map/mix_backward/pallas_call | solution.py:539
  702.1 19.6 %collective-permute-done.80.refs_6_.refs_1_ = f32[2,8,2048]{2,1,0:T(8,128)S(1)} collective-permute-done((f32[2,8,2048]{2,1,0:T(8,128)S(1)}, f32[2,8,2048]{2,1,0:T(8,128)S(1)}, u32[]{:S(2)}, u32[]{:S(2)}) %collective-permute-start.80) | collective-permute-done | bytes 131104 | tf_op jit(solution)/shard_map/ppermute | solution.py:1068
  749.6 10.7 %row_blocks.28.refs_5_.refs_0_.refs_1_ = bf16[1280,2176]{1,0:T(8,128)(2,1)} custom-call(bf16[1024,2048]{1,0:T(8,128)(2,1)S(1)} %copy-done.2, bf16[1024,2176]{1,0:T(8,128)(2,1)} %bitcast.21.right_ref.refs_0_, bf16[128,2176]{1,0:T(8,128)(2,1)S(1)} %get-tuple-element.147.refs_0_, bf16[128,2176]{1,0:T(8,128)(2,1)S(1)} %get-tuple-element.148.refs_1_), custom_call_target="tpu_custom_call" | custom-call | tf_op jit(solution)/shard_map/row_blocks/pallas_call | solution.py:685
  760.4 19.7 %matmul.9 = (bf16[512,2048]{1,0:T(8,128)(2,1)S(1)}, bf16[128,2048]{1,0:T(8,128)(2,1)}, bf16[128,2048]{1,0:T(8,128)(2,1)}, bf16[128,2048]{1,0:T(8,128)(2,1)S(1)}, bf16[128,2048]{1,0:T(8,128)(2,1)}) custom-call(bf16[1024,2176]{1,0:T(8,128)(2,1)} %bitcast.21.right_ref.refs_0_, bf16[2048,2176]{1,0:T(8,128)(2,1)} %get-tuple-element.149.refs_1_, ...), custom_call_target="tpu_custom_call" | custom-call | tf_op jit(solution)/shard_map/matmul/pallas_call | solution.py:751
  780.1 11.7 %collective-permute-done.86.refs_12_.refs_2_ = bf16[128,2176]{1,0:T(8,128)(2,1)S(1)} collective-permute-done((bf16[128,2176]{1,0:T(8,128)(2,1)S(1)}, bf16[128,2176]{1,0:T(8,128)(2,1)S(1)}, u32[]{:S(2)}, u32[]{:S(2)}) %collective-permute-start.86) | collective-permute-done | bytes 557088 | tf_op jit(solution)/shard_map/ppermute | solution.py:1303
  803.1 16.9 %collective-permute-done.92.refs_6_.refs_4_ = bf16[256,2048]{1,0:T(8,128)(2,1)S(1)} collective-permute-done((bf16[256,2048]{1,0:T(8,128)(2,1)S(1)}, bf16[256,2048]{1,0:T(8,128)(2,1)S(1)}, u32[]{:S(2)}, u32[]{:S(2)}) %collective-permute-start.92) | collective-permute-done | bytes 1048608 | tf_op jit(solution)/shard_map/ppermute | solution.py:1303
  834.2 13.9 %collective-permute-done.94.refs_2_ = bf16[256,2176]{1,0:T(8,128)(2,1)} collective-permute-done((bf16[256,2176]{1,0:T(8,128)(2,1)S(1)}, bf16[256,2176]{1,0:T(8,128)(2,1)}, u32[]{:S(2)}, u32[]{:S(2)}) %collective-permute-start.94) | collective-permute-done | bytes 1114144 | tf_op jit(solution)/shard_map/ppermute | solution.py:1303
  862.8 11.6 %collective-permute-done.98.refs_6_.refs_0_ = bf16[256,2048]{1,0:T(8,128)(2,1)S(1)} collective-permute-done((bf16[256,2048]{1,0:T(8,128)(2,1)}, bf16[256,2048]{1,0:T(8,128)(2,1)S(1)}, u32[]{:S(2)}, u32[]{:S(2)}) %collective-permute-start.98) | collective-permute-done | bytes 1048608 | tf_op jit(solution)/shard_map/ppermute | solution.py:1303
  875.6 19.5 %collective-permute-done.96.refs_2_ = bf16[256,2176]{1,0:T(8,128)(2,1)} collective-permute-done((bf16[256,2176]{1,0:T(8,128)(2,1)S(1)}, bf16[256,2176]{1,0:T(8,128)(2,1)}, u32[]{:S(2)}, u32[]{:S(2)}) %collective-permute-start.96) | collective-permute-done | bytes 1114144 | tf_op jit(solution)/shard_map/ppermute | solution.py:1303
  (735 shorter events, 462.3 us)
Async XLA Ops:
  106.5 81.8 %collective-permute-start.18 = (bf16[256,4224]{1,0:T(8,128)(2,1)}, bf16[256,4224]{1,0:T(8,128)(2,1)}, u32[]{:S(2)}, u32[]{:S(2)}) collective-permute-start(bf16[256,4224]{1,0:T(8,128)(2,1)} %tie.57.refs_1_.refs_2_.refs_0_), channel_id=1, source_target_pairs={{0,8},{8,16},{16,24},{24,28},{28,20},{20,12},{12,4},{4,0},{1,9},{9... | collective-permute-start | bytes 6488072 | tf_op jit(solution)/shard_map/ppermute | solution.py:1228
  109.6 78.7 %collective-permute-start.19 = (bf16[256,4224]{1,0:T(8,128)(2,1)}, bf16[256,4224]{1,0:T(8,128)(2,1)}, u32[]{:S(2)}, u32[]{:S(2)}) collective-permute-start(bf16[256,4224]{1,0:T(8,128)(2,1)} %tie.57.refs_1_.refs_2_.refs_0_), channel_id=1, source_target_pairs={{8,0},{16,8},{24,16},{28,24},{20,28},{12,20},{4,12},{0,4},{9,1},{1... | collective-permute-start | bytes 6488072 | tf_op jit(solution)/shard_map/ppermute | solution.py:1229
  110.8 69.5 %collective-permute-start.17 = (bf16[256,2048]{1,0:T(8,128)(2,1)}, bf16[256,2048]{1,0:T(8,128)(2,1)S(1)}, u32[]{:S(2)}, u32[]{:S(2)}) collective-permute-start(bf16[256,2048]{1,0:T(8,128)(2,1)} %tie.58.refs_11_.refs_12_.refs_5_.refs_6_.refs_0_), channel_id=1, source_target_pairs={{8,0},{16,8},{24,16},{28,24},{20,28},{12,20},{4,12},{0,4},{9,1},{1... | collective-permute-start | bytes 3145736 | tf_op jit(solution)/shard_map/ppermute | solution.py:1229
  112.2 71.0 %collective-permute-start.16 = (bf16[256,2048]{1,0:T(8,128)(2,1)}, bf16[256,2048]{1,0:T(8,128)(2,1)}, u32[]{:S(2)}, u32[]{:S(2)}) collective-permute-start(bf16[256,2048]{1,0:T(8,128)(2,1)} %tie.58.refs_11_.refs_12_.refs_5_.refs_6_.refs_0_), channel_id=1, source_target_pairs={{0,8},{8,16},{16,24},{24,28},{28,20},{20,12},{12,4},{4,0},{1,9},{9... | collective-permute-start | bytes 3145736 | tf_op jit(solution)/shard_map/ppermute | solution.py:1228
  181.2 59.1 %collective-permute-start.26 = (bf16[256,2048]{1,0:T(8,128)(2,1)}, bf16[256,2048]{1,0:T(8,128)(2,1)}, u32[]{:S(2)}, u32[]{:S(2)}) collective-permute-start(bf16[256,2048]{1,0:T(8,128)(2,1)} %tie.60.refs_2_.refs_1_), channel_id=1, source_target_pairs={{8,0},{16,8},{24,16},{28,24},{20,28},{12,20},{4,12},{0,4},{9,1},{1... | collective-permute-start | bytes 3145736 | tf_op jit(solution)/shard_map/ppermute | solution.py:1229
  196.2 44.1 %collective-permute-start.23 = (bf16[128,2048]{1,0:T(8,128)(2,1)}, bf16[128,2048]{1,0:T(8,128)(2,1)}, u32[]{:S(2)}, u32[]{:S(2)}) collective-permute-start(bf16[128,2048]{1,0:T(8,128)(2,1)} %get-tuple-element.254), channel_id=1, source_target_pairs={{0,2},{1,3},{2,0},{3,1},{4,6},{5,7},{6,4},{7,5},{8,10},{9,11},{10,... | collective-permute-start | bytes 1572872 | tf_op jit(solution)/shard_map/ppermute | solution.py:1072
  197.7 42.7 %collective-permute-start.24 = (bf16[128,2048]{1,0:T(8,128)(2,1)}, bf16[128,2048]{1,0:T(8,128)(2,1)}, u32[]{:S(2)}, u32[]{:S(2)}) collective-permute-start(bf16[128,2048]{1,0:T(8,128)(2,1)} %get-tuple-element.253), channel_id=1, source_target_pairs={{0,2},{1,3},{2,0},{3,1},{4,6},{5,7},{6,4},{7,5},{8,10},{9,11},{10,... | collective-permute-start | bytes 1572872 | tf_op jit(solution)/shard_map/ppermute | solution.py:1072
  229.4 31.2 %collective-permute-start.29 = (bf16[256,2048]{1,0:T(8,128)(2,1)}, bf16[256,2048]{1,0:T(8,128)(2,1)}, u32[]{:S(2)}, u32[]{:S(2)}) collective-permute-start(bf16[256,2048]{1,0:T(8,128)(2,1)} %tie.63.refs_3_.refs_7_), channel_id=1, source_target_pairs={{0,8},{8,16},{16,24},{24,28},{28,20},{20,12},{12,4},{4,0},{1,9},{9... | collective-permute-start | bytes 3145736 | tf_op jit(solution)/shard_map/ppermute | solution.py:1228
  282.0 48.8 %collective-permute-start.38 = (bf16[256,4224]{1,0:T(8,128)(2,1)}, bf16[256,4224]{1,0:T(8,128)(2,1)}, u32[]{:S(2)}, u32[]{:S(2)}) collective-permute-start(bf16[256,4224]{1,0:T(8,128)(2,1)} %tie.69.refs_11_.refs_1_), channel_id=1, source_target_pairs={{8,0},{16,8},{24,16},{28,24},{20,28},{12,20},{4,12},{0,4},{9,1},{1... | collective-permute-start | bytes 6488072 | tf_op jit(solution)/shard_map/ppermute | solution.py:1229
  283.3 47.5 %collective-permute-start.37 = (bf16[256,4224]{1,0:T(8,128)(2,1)}, bf16[256,4224]{1,0:T(8,128)(2,1)}, u32[]{:S(2)}, u32[]{:S(2)}) collective-permute-start(bf16[256,4224]{1,0:T(8,128)(2,1)} %tie.68.refs_10_.refs_8_), channel_id=1, source_target_pairs={{0,8},{8,16},{16,24},{24,28},{28,20},{20,12},{12,4},{4,0},{1,9},{9... | collective-permute-start | bytes 6488072 | tf_op jit(solution)/shard_map/ppermute | solution.py:1228
  334.9 49.6 %collective-permute-start.46 = (bf16[256,4224]{1,0:T(8,128)(2,1)}, bf16[256,4224]{1,0:T(8,128)(2,1)}, u32[]{:S(2)}, u32[]{:S(2)}) collective-permute-start(bf16[256,4224]{1,0:T(8,128)(2,1)} %tie.70.refs_1_.refs_7_), channel_id=1, source_target_pairs={{0,8},{8,16},{16,24},{24,28},{28,20},{20,12},{12,4},{4,0},{1,9},{9... | collective-permute-start | bytes 6488072 | tf_op jit(solution)/shard_map/ppermute | solution.py:1228
  337.1 51.5 %collective-permute-start.44 = (bf16[256,4224]{1,0:T(8,128)(2,1)}, bf16[256,4224]{1,0:T(8,128)(2,1)}, u32[]{:S(2)}, u32[]{:S(2)}) collective-permute-start(bf16[256,4224]{1,0:T(8,128)(2,1)} %tie.71.refs_2_), channel_id=1, source_target_pairs={{8,0},{16,8},{24,16},{28,24},{20,28},{12,20},{4,12},{0,4},{9,1},{1... | collective-permute-start | bytes 6488072 | tf_op jit(solution)/shard_map/ppermute | solution.py:1229
  478.2 29.3 %collective-permute-start.61 = (bf16[128,2048]{1,0:T(8,128)(2,1)}, bf16[128,2048]{1,0:T(8,128)(2,1)}, u32[]{:S(2)}, u32[]{:S(2)}) collective-permute-start(bf16[128,2048]{1,0:T(8,128)(2,1)} %get-tuple-element.230.refs_1_), channel_id=1, source_target_pairs={{0,2},{1,3},{2,0},{3,1},{4,6},{5,7},{6,4},{7,5},{8,10},{9,11},{10,... | collective-permute-start | bytes 1572872 | tf_op jit(solution)/shard_map/ppermute | solution.py:1072
  479.5 28.1 %collective-permute-start.56 = (bf16[128,2048]{1,0:T(8,128)(2,1)S(1)}, bf16[128,2048]{1,0:T(8,128)(2,1)}, u32[]{:S(2)}, u32[]{:S(2)}) collective-permute-start(bf16[128,2048]{1,0:T(8,128)(2,1)S(1)} %get-tuple-element.229.refs_0_), channel_id=1, source_target_pairs={{0,2},{1,3},{2,0},{3,1},{4,6},{5,7},{6,4},{7,5},{8,10},{9,11},{10,... | collective-permute-start | bytes 1572872 | tf_op jit(solution)/shard_map/ppermute | solution.py:1072
  505.5 48.1 %collective-permute-start.68 = (bf16[256,4224]{1,0:T(8,128)(2,1)}, bf16[256,4224]{1,0:T(8,128)(2,1)}, u32[]{:S(2)}, u32[]{:S(2)}) collective-permute-start(bf16[256,4224]{1,0:T(8,128)(2,1)} %get-tuple-element.124.refs_1_), channel_id=1, source_target_pairs={{0,8},{8,16},{16,24},{24,28},{28,20},{20,12},{12,4},{4,0},{1,9},{9... | collective-permute-start | bytes 6488072 | tf_op jit(solution)/shard_map/ppermute | solution.py:1303
  506.8 47.8 %collective-permute-start.69 = (bf16[256,4224]{1,0:T(8,128)(2,1)}, bf16[256,4224]{1,0:T(8,128)(2,1)}, u32[]{:S(2)}, u32[]{:S(2)}) collective-permute-start(bf16[256,4224]{1,0:T(8,128)(2,1)} %get-tuple-element.125.refs_2_), channel_id=1, source_target_pairs={{8,0},{16,8},{24,16},{28,24},{20,28},{12,20},{4,12},{0,4},{9,1},{1... | collective-permute-start | bytes 6488072 | tf_op jit(solution)/shard_map/ppermute | solution.py:1304
  584.1 31.3 %collective-permute-start.72 = (bf16[4,128,384]{2,1,0:T(8,128)(2,1)}, bf16[4,128,384]{2,1,0:T(8,128)(2,1)}, u32[]{:S(2)}, u32[]{:S(2)}) collective-permute-start(bf16[4,128,384]{2,1,0:T(8,128)(2,1)} %pad_maximum_fusion.6.refs_0_), channel_id=1, source_target_pairs={{8,0},{12,4},{16,8},{20,12},{24,16},{28,20},{9,1},{13,5},{17,9},{2... | collective-permute-start | bytes 1179656 | tf_op jit(solution)/shard_map/ppermute | solution.py:1068
  585.4 35.9 %collective-permute-start.73 = (bf16[4,128,384]{2,1,0:T(8,128)(2,1)}, bf16[4,128,384]{2,1,0:T(8,128)(2,1)}, u32[]{:S(2)}, u32[]{:S(2)}) collective-permute-start(bf16[4,128,384]{2,1,0:T(8,128)(2,1)} %pad_maximum_fusion.6.refs_0_), channel_id=1, source_target_pairs={{16,0},{20,4},{24,8},{28,12},{17,1},{21,5},{25,9},{29,13},{18,2},{... | collective-permute-start | bytes 1179656 | tf_op jit(solution)/shard_map/ppermute | solution.py:1068
  648.6 74.8 %collective-permute-start.78 = (bf16[256,4224]{1,0:T(8,128)(2,1)}, bf16[256,4224]{1,0:T(8,128)(2,1)}, u32[]{:S(2)}, u32[]{:S(2)}) collective-permute-start(bf16[256,4224]{1,0:T(8,128)(2,1)} %get-tuple-element.136.refs_6_), channel_id=1, source_target_pairs={{0,8},{8,16},{16,24},{24,28},{28,20},{20,12},{12,4},{4,0},{1,9},{9... | collective-permute-start | bytes 6488072 | tf_op jit(solution)/shard_map/ppermute | solution.py:1303
  648.6 74.7 %collective-permute-start.79 = (bf16[256,4224]{1,0:T(8,128)(2,1)}, bf16[256,4224]{1,0:T(8,128)(2,1)}, u32[]{:S(2)}, u32[]{:S(2)}) collective-permute-start(bf16[256,4224]{1,0:T(8,128)(2,1)} %get-tuple-element.137.refs_7_), channel_id=1, source_target_pairs={{8,0},{16,8},{24,16},{28,24},{20,28},{12,20},{4,12},{0,4},{9,1},{1... | collective-permute-start | bytes 6488072 | tf_op jit(solution)/shard_map/ppermute | solution.py:1304
  651.8 70.5 %collective-permute-start.81 = (bf16[256,2048]{1,0:T(8,128)(2,1)}, bf16[256,2048]{1,0:T(8,128)(2,1)S(1)}, u32[]{:S(2)}, u32[]{:S(2)}) collective-permute-start(bf16[256,2048]{1,0:T(8,128)(2,1)} %get-tuple-element.138.refs_11_), channel_id=1, source_target_pairs={{0,8},{8,16},{16,24},{24,28},{28,20},{20,12},{12,4},{4,0},{1,9},{9... | collective-permute-start | bytes 3145736 | tf_op jit(solution)/shard_map/ppermute | solution.py:1303
  651.9 70.5 %collective-permute-start.82 = (bf16[256,2048]{1,0:T(8,128)(2,1)S(1)}, bf16[256,2048]{1,0:T(8,128)(2,1)S(1)}, u32[]{:S(2)}, u32[]{:S(2)}) collective-permute-start(bf16[256,2048]{1,0:T(8,128)(2,1)S(1)} %get-tuple-element.139.refs_12_), channel_id=1, source_target_pairs={{8,0},{16,8},{24,16},{28,24},{20,28},{12,20},{4,12},{0,4},{9,1},{1... | collective-permute-start | bytes 3145736 | tf_op jit(solution)/shard_map/ppermute | solution.py:1304
  730.4 62.1 %collective-permute-start.89 = (bf16[256,4224]{1,0:T(8,128)(2,1)S(1)}, bf16[256,4224]{1,0:T(8,128)(2,1)}, u32[]{:S(2)}, u32[]{:S(2)}) collective-permute-start(bf16[256,4224]{1,0:T(8,128)(2,1)S(1)} %get-tuple-element.141.refs_1_), channel_id=1, source_target_pairs={{0,8},{8,16},{16,24},{24,28},{28,20},{20,12},{12,4},{4,0},{1,9},{9... | collective-permute-start | bytes 6488072 | tf_op jit(solution)/shard_map/ppermute | solution.py:1303
  730.5 62.0 %collective-permute-start.90 = (bf16[256,4224]{1,0:T(8,128)(2,1)}, bf16[256,4224]{1,0:T(8,128)(2,1)}, u32[]{:S(2)}, u32[]{:S(2)}) collective-permute-start(bf16[256,4224]{1,0:T(8,128)(2,1)} %get-tuple-element.142.refs_2_), channel_id=1, source_target_pairs={{8,0},{16,8},{24,16},{28,24},{20,28},{12,20},{4,12},{0,4},{9,1},{1... | collective-permute-start | bytes 6488072 | tf_op jit(solution)/shard_map/ppermute | solution.py:1304
  740.7 51.1 %collective-permute-start.86 = (bf16[128,2176]{1,0:T(8,128)(2,1)S(1)}, bf16[128,2176]{1,0:T(8,128)(2,1)S(1)}, u32[]{:S(2)}, u32[]{:S(2)}) collective-permute-start(bf16[128,2176]{1,0:T(8,128)(2,1)S(1)} %get-tuple-element.147.refs_0_), channel_id=1, source_target_pairs={{0,8},{8,16},{16,24},{24,28},{28,20},{20,12},{12,4},{4,0},{1,9},{9... | collective-permute-start | bytes 1671176 | tf_op jit(solution)/shard_map/ppermute | solution.py:1303
  740.9 51.6 %collective-permute-start.87 = (bf16[128,2176]{1,0:T(8,128)(2,1)S(1)}, bf16[128,2176]{1,0:T(8,128)(2,1)S(1)}, u32[]{:S(2)}, u32[]{:S(2)}) collective-permute-start(bf16[128,2176]{1,0:T(8,128)(2,1)S(1)} %get-tuple-element.148.refs_1_), channel_id=1, source_target_pairs={{8,0},{16,8},{24,16},{28,24},{20,28},{12,20},{4,12},{0,4},{9,1},{1... | collective-permute-start | bytes 1671176 | tf_op jit(solution)/shard_map/ppermute | solution.py:1304
  829.9 78.8 %collective-permute-start.101 = (bf16[128,2048]{1,0:T(8,128)(2,1)}, bf16[128,2048]{1,0:T(8,128)(2,1)}, u32[]{:S(2)}, u32[]{:S(2)}) collective-permute-start(bf16[128,2048]{1,0:T(8,128)(2,1)} %get-tuple-element.222.refs_1_), channel_id=1, source_target_pairs={{0,2},{1,3},{2,0},{3,1},{4,6},{5,7},{6,4},{7,5},{8,10},{9,11},{10,... | collective-permute-start | bytes 1572872 | tf_op jit(solution)/shard_map/ppermute | solution.py:1072
  853.6 41.5 %collective-permute-start.96 = (bf16[256,2176]{1,0:T(8,128)(2,1)S(1)}, bf16[256,2176]{1,0:T(8,128)(2,1)}, u32[]{:S(2)}, u32[]{:S(2)}) collective-permute-start(bf16[256,2176]{1,0:T(8,128)(2,1)S(1)} %get-tuple-element.162.refs_4_.refs_1_), channel_id=1, source_target_pairs={{0,8},{8,16},{16,24},{24,28},{28,20},{20,12},{12,4},{4,0},{1,9},{9... | collective-permute-start | bytes 3342344 | tf_op jit(solution)/shard_map/ppermute | solution.py:1303
  855.2 40.6 %collective-permute-start.97 = (bf16[256,2176]{1,0:T(8,128)(2,1)S(1)}, bf16[256,2176]{1,0:T(8,128)(2,1)}, u32[]{:S(2)}, u32[]{:S(2)}) collective-permute-start(bf16[256,2176]{1,0:T(8,128)(2,1)S(1)} %copy-done.34), channel_id=1, source_target_pairs={{8,0},{16,8},{24,16},{28,24},{20,28},{12,20},{4,12},{0,4},{9,1},{1... | collective-permute-start | bytes 3342344 | tf_op jit(solution)/shard_map/ppermute | solution.py:1304
  874.3 34.3 %collective-permute-start.84 = (bf16[128,2048]{1,0:T(8,128)(2,1)}, bf16[128,2048]{1,0:T(8,128)(2,1)}, u32[]{:S(2)}, u32[]{:S(2)}) collective-permute-start(bf16[128,2048]{1,0:T(8,128)(2,1)} %get-tuple-element.221.refs_0_), channel_id=1, source_target_pairs={{0,2},{1,3},{2,0},{3,1},{4,6},{5,7},{6,4},{7,5},{8,10},{9,11},{10,... | collective-permute-start | bytes 1572872 | tf_op jit(solution)/shard_map/ppermute | solution.py:1072
  899.3 49.2 %collective-permute-start.112 = (bf16[256,2176]{1,0:T(8,128)(2,1)}, bf16[256,2176]{1,0:T(8,128)(2,1)}, u32[]{:S(2)}, u32[]{:S(2)}) collective-permute-start(bf16[256,2176]{1,0:T(8,128)(2,1)} %get-tuple-element.164.refs_1_.refs_3_.refs_2_), channel_id=1, source_target_pairs={{0,8},{8,16},{16,24},{24,28},{28,20},{20,12},{12,4},{4,0},{1,9},{9... | collective-permute-start | bytes 3342344 | tf_op jit(solution)/shard_map/ppermute | solution.py:1303
  900.3 48.1 %collective-permute-start.113 = (bf16[256,2176]{1,0:T(8,128)(2,1)}, bf16[256,2176]{1,0:T(8,128)(2,1)}, u32[]{:S(2)}, u32[]{:S(2)}) collective-permute-start(bf16[256,2176]{1,0:T(8,128)(2,1)} %get-tuple-element.165.refs_2_.refs_4_.refs_3_), channel_id=1, source_target_pairs={{8,0},{16,8},{24,16},{28,24},{20,28},{12,20},{4,12},{0,4},{9,1},{1... | collective-permute-start | bytes 3342344 | tf_op jit(solution)/shard_map/ppermute | solution.py:1304
  (236 other events, 2811.2 us)
